TPU v7x, 256 devices: a whole 4x4x8 slice. The times are simulated.
256 devices in a mesh: dp: 32 (over y, z_hi, x), tensor: 8 (over z_lo, core).
Axes of the slice: x: 4, y: 4, z: 8 (z_hi: 2, z_lo: 4; z = z_hi * 4 + z_lo), core: 2. Of those that a mesh axis runs over, the one named last changes fastest.
Arguments:
- inputs: bfloat16 [32768, 1536], P(('dp', 'tensor')), may hold values from -360 to 360
- norm_gain: float32 [1536], replicated, may hold values from 0.1 to 1.9
- norm_bias: float32 [1536], replicated, may hold values from -3 to 3
- w_in: bfloat16 [1536, 6144], P('dp', 'tensor'), may hold values from -0.15625 to 0.15625
- bias_in: float32 [6144], P('tensor'), may hold values from -3 to 3
- w_out: bfloat16 [6144, 1536], P('tensor', 'dp'), may hold values from -0.078125 to 0.078125
- grad_out: bfloat16 [32768, 1536], P(('dp', 'tensor')), may hold values from -24 to 24
Outputs:
- grad_in: bfloat16 [32768, 1536], P(('dp', 'tensor'))
- grad_w_in: float32 [1536, 6144], P('dp', 'tensor')
- grad_w_out: float32 [6144, 1536], P('tensor', 'dp')
All inputs are finite; a program needn't handle non-finite values.
Results may differ from a plain program's by a relative error of at most 0.0054.
Values may be sent and summed in bfloat16 or wider, within the bound.
No kernel may reach another device: no remote copies, remote signals or barrier semaphores. Data moves between devices by JAX's collectives and lax.ppermute only.
A program may use at most 128 MiB of HBM per device.

v0:
```python
import jax
import jax.numpy as jnp
from jax import lax
from jax.sharding import PartitionSpec as P


def layer_rows(rows_in, norm_gain, norm_bias):
    centred = rows_in.astype(jnp.float32)
    centred = centred - jnp.mean(centred, axis=-1, keepdims=True)
    variance = jnp.mean(centred * centred, axis=-1, keepdims=True)
    inv_scale = lax.rsqrt(variance + 1e-05)
    normed = centred * inv_scale
    return (normed, inv_scale, (normed * norm_gain + norm_bias).astype(jnp.bfloat16))


def on_device(inputs, norm_gain, norm_bias, w_in, bias_in, w_out, grad_out):
    normed, inv_scale, normed_local = layer_rows(inputs, norm_gain, norm_bias)
    normed_full, grad_full = (
        lax.all_gather(normed_local, "tensor", axis=0, tiled=True),
        lax.all_gather(grad_out, "tensor", axis=0, tiled=True),
    )
    w_in_full = lax.all_gather(w_in, "dp", axis=0, tiled=True)
    pre_act = jnp.dot(normed_full, w_in_full, preferred_element_type=jnp.float32) + bias_in
    logistic = jax.nn.sigmoid(pre_act)
    activated = (pre_act * logistic).astype(jnp.bfloat16)
    columns = grad_full
    grad_act = 0.5 * lax.dot_general(
        columns,
        lax.all_gather(w_out, "dp", axis=1, tiled=True),
        (((1,), (1,)), ((), ())),
        preferred_element_type=jnp.float32,
    )
    grad_pre = (grad_act * logistic * (1.0 + pre_act * (1.0 - logistic))).astype(jnp.bfloat16)
    columns = grad_full
    joined = lax.psum_scatter(
        jnp.concatenate(
            [
                lax.dot_general(
                    normed_full,
                    grad_pre,
                    (((0,), (0,)), ((), ())),
                    preferred_element_type=jnp.float32,
                ),
                0.5
                * lax.dot_general(
                    columns, activated, (((0,), (0,)), ((), ())), preferred_element_type=jnp.float32
                ),
            ],
            axis=1,
        ),
        "dp",
        scatter_dimension=0,
        tiled=True,
    )
    grad_w_in = joined[:, : w_in.shape[1]]
    out_sum_t = joined[:, w_in.shape[1] :]
    grad_normed = lax.psum_scatter(
        lax.dot_general(
            grad_pre, w_in_full, (((1,), (1,)), ((), ())), preferred_element_type=jnp.float32
        ).astype(jnp.bfloat16),
        "tensor",
        scatter_dimension=0,
        tiled=True,
    ).astype(jnp.float32)
    scaled = grad_normed * norm_gain
    first = jnp.mean(scaled, axis=-1, keepdims=True)
    second = jnp.mean(scaled * normed, axis=-1, keepdims=True)
    grad_in = grad_out.astype(jnp.float32) + inv_scale * (scaled - first - normed * second)
    return (grad_in.astype(jnp.bfloat16), grad_w_in, out_sum_t.T)


def solution(mesh):
    in_specs = (
        P(("dp", "tensor"), None),
        P(),
        P(),
        P("dp", "tensor"),
        P("tensor"),
        P("tensor", "dp"),
        P(("dp", "tensor"), None),
    )
    out_specs = (P(("dp", "tensor"), None), P("dp", "tensor"), P("tensor", "dp"))
    return jax.shard_map(
        on_device, mesh=mesh, in_specs=in_specs, out_specs=out_specs, check_vma=False
    )
```

profile of v0, /device:TPU:16, one launch (start us, length us, event | category | flops | bytes accessed | tf_op | source)
XLA Modules:
  0.0 647.6 jit_solution(8374045257849454259)
XLA Ops:
  7.2 0.0 all-gather.11.cloned.1.call-start
  7.2 0.7 all-gather.11.cloned.1.call-update
  7.9 0.0 all-gather.9.cloned.1.call-start
  7.9 1.1 convert_reduce_fusion
  9.1 1.2 fusion.14
  10.3 2.1 fusion.8
  12.4 0.0 all-gather.9.cloned.1.call-update
  12.4 0.0 all-gather.7.cloned.1.call-start
  12.5 0.7 all-gather.7.cloned.1.call-update
  13.2 0.0 all-gather.5.cloned.1.call-start
  13.2 0.5 all-gather.5.cloned.1.call-update
  13.8 0.0 copy-start.6
  13.8 0.0 reduce-scatter.5.cloned.1.call-start
  13.8 92.7 %all-gather.11.cloned.1.call-done = bf16[1536,768]{1,0:T(8,128)(2,1)} async-done(((bf16[48,768]{1,0:T(8,128)(2,1)}), bf16[1536,768]{1,0:T(8,128)(2,1)}) %all-gather.11.cloned.1.call-update) | async-done | bytes 2359312 | tf_op jit(solution)/shard_map/all_gather | solution.py:22
  106.6 43.0 %all-gather.9.cloned.1.call-done = bf16[1024,1536]{1,0:T(8,128)(2,1)} async-done(((bf16[128,1536]{1,0:T(8,128)(2,1)}), bf16[1024,1536]{1,0:T(8,128)(2,1)}) %all-gather.9.cloned.1.call-update) | async-done | bytes 3145744 | tf_op jit(solution)/shard_map/all_gather | solution.py:19
  149.5 6.9 %fusion.17 = f32[1024,768]{1,0:T(8,128)} fusion(bf16[1024,1536]{1,0:T(8,128)(2,1)} %all-gather.9.cloned.1.call-done, bf16[1536,768]{1,0:T(8,128)(2,1)} %all-gather.11.cloned.1.call-done), kind=kOutput, calls=%fused_computation.31 | convolution fusion | flops 2415919104 | bytes 8650752 | tf_op jit(solution)/shard_map/dot_general | solution.py:23
  156.4 0.0 copy-start.5
  156.4 87.7 %all-gather.7.cloned.1.call-done = bf16[768,1536]{0,1:T(8,128)(2,1)} async-done(((bf16[768,48]{0,1:T(8,128)(2,1)}), bf16[768,1536]{0,1:T(8,128)(2,1)}) %all-gather.7.cloned.1.call-update) | async-done | bytes 2359312 | tf_op jit(solution)/shard_map/all_gather | solution.py:29
  244.1 42.2 %all-gather.5.cloned.1.call-done = bf16[1024,1536]{1,0:T(8,128)(2,1)} async-done(((bf16[128,1536]{1,0:T(8,128)(2,1)}), bf16[1024,1536]{1,0:T(8,128)(2,1)}) %all-gather.5.cloned.1.call-update) | async-done | bytes 3145744 | tf_op jit(solution)/shard_map/all_gather | solution.py:20
  286.4 0.0 copy-done.6
  286.4 6.7 %multiply_convert_fusion.1 = bf16[1024,768]{1,0:T(8,128)(2,1)S(1)} fusion(f32[1024,768]{1,0:T(8,128)} %fusion.17, bf16[1024,1536]{1,0:T(8,128)(2,1)} %all-gather.5.cloned.1.call-done, bf16[768,1536]{0,1:T(8,128)(2,1)} %all-gather.7.cloned.1.call-done, f32[768]{0:T(1024)S(1)} %copy-done.6), kind=kOutput, calls=%fused_computation.4 | convolution fusion | flops 2424569856 | bytes 10226688 | tf_op jit(solution)/shard_map/dot_general | solution.py:27
  293.0 0.0 copy-start.8
  293.1 1.2 copy-done.8
  294.3 0.0 copy-done.5
  294.3 4.1 convolution_convert_fusion
  298.3 0.0 copy-start.3
  298.3 0.0 reduce-scatter.5.cloned.1.call-update
  298.4 0.2 reduce-scatter.7.cloned.1.call-start
  298.6 1.6 copy-done.3
  300.2 0.0 copy-start.4
  300.2 0.0 copy-start.7
  300.2 4.4 fusion.18
  304.6 0.0 copy-done.4
  304.6 0.0 copy-done.7
  304.6 2.7 multiply_bitcast_fusion
  307.4 4.5 pad_maximum_fusion
  311.9 9.7 %copy.14 = f32[1536,1536]{1,0:T(8,128)} copy(f32[1536,1536]{0,1:T(8,128)} %pad_maximum_fusion) | data formatting | bytes 18874368
  321.6 0.0 copy-start
  321.6 0.0 copy-start.2
  321.6 0.0 reduce-scatter.7.cloned.1.call-update
  321.6 21.4 %reduce-scatter.5.cloned.1.call-done = bf16[128,1536]{1,0:T(8,128)(2,1)} async-done(((bf16[1024,1536]{1,0:T(8,128)(2,1)}), bf16[128,1536]{1,0:T(8,128)(2,1)}) %reduce-scatter.5.cloned.1.call-update) | async-done | bytes 393232 | tf_op jit(solution)/shard_map/reduce_scatter | solution.py:57
  343.0 0.0 copy-done
  343.0 0.0 copy-done.2
  343.0 1.3 fusion.15
  344.3 0.0 copy-done.1
  344.3 2.2 fusion.13
  346.5 292.6 %reduce-scatter.7.cloned.1.call-done = f32[48,1536]{1,0:T(8,128)} async-done(((f32[1536,1536]{1,0:T(8,128)}), f32[48,1536]{1,0:T(8,128)}) %reduce-scatter.7.cloned.1.call-update) | async-done | bytes 294928
  639.1 1.7 slice_bitcast_fusion
  (4 shorter events, 0.0 us)
Async XLA Ops:
  7.2 99.4 %all-gather.11.cloned.1.call-start = ((), (), s32[]{:S(2)}) async-start(), calls=%async_computation.5 | async-start | bytes 2433024 | tf_op jit(solution)/shard_map/all_gather | solution.py:22
  7.9 141.6 %all-gather.9.cloned.1.call-start = ((), (), s32[]{:S(2)}) async-start(), calls=%async_computation.4 | async-start | bytes 3538944 | tf_op jit(solution)/shard_map/all_gather | solution.py:19
  12.4 231.7 %all-gather.7.cloned.1.call-start = ((), (), s32[]{:S(2)}) async-start(), calls=%async_computation.3 | async-start | bytes 2433024 | tf_op jit(solution)/shard_map/all_gather | solution.py:29
  13.2 273.2 %all-gather.5.cloned.1.call-start = ((), (), s32[]{:S(2)}) async-start(), calls=%async_computation.2 | async-start | bytes 3538944 | tf_op jit(solution)/shard_map/all_gather | solution.py:20
  13.8 272.6 %copy-start.6 = (f32[768]{0:T(1024)S(1)}, f32[768]{0:T(1024)}, u32[]{:S(2)}) copy-start(f32[768]{0:T(1024)} %param.11) | copy-start | bytes 9220
  13.8 329.2 %reduce-scatter.5.cloned.1.call-start = ((), (), s32[]{:S(2)}) async-start(), calls=%async_computation.6 | async-start | bytes 3538944 | tf_op jit(solution)/shard_map/reduce_scatter | solution.py:57
  156.4 137.8 %copy-start.5 = (bf16[1536,768]{1,0:T(8,128)(2,1)S(1)}, bf16[1536,768]{1,0:T(8,128)(2,1)}, u32[]{:S(2)}) copy-start(bf16[1536,768]{1,0:T(8,128)(2,1)} %all-gather.11.cloned.1.call-done) | copy-start | bytes 7077892
  293.0 1.2 copy-start.8
  298.3 1.9 copy-start.3
  298.4 340.7 %reduce-scatter.7.cloned.1.call-start = ((), (), s32[]{:S(2)}) async-start(), calls=%async_computation.7 | async-start | bytes 9732096
  300.2 4.4 copy-start.4
  300.2 4.4 copy-start.7
  321.6 21.4 %copy-start = (bf16[128,1536]{1,0:T(8,128)(2,1)S(1)}, bf16[128,1536]{1,0:T(8,128)(2,1)}, u32[]{:S(2)}) copy-start(bf16[128,1536]{1,0:T(8,128)(2,1)} %param.7) | copy-start | bytes 1179652
  321.6 21.4 %copy-start.2 = (f32[1536]{0:T(1024)S(1)}, f32[1536]{0:T(1024)}, u32[]{:S(2)}) copy-start(f32[1536]{0:T(1024)} %param.8) | copy-start | bytes 18436
  321.6 22.7 %copy-start.1 = (bf16[128,1536]{1,0:T(8,128)(2,1)S(1)}, bf16[128,1536]{1,0:T(8,128)(2,1)}, u32[]{:S(2)}) copy-start(bf16[128,1536]{1,0:T(8,128)(2,1)} %param.13) | copy-start | bytes 1179652
Sparse Core Ops, SparseCore 0:
  11.4 95.1 all-gather.10
  108.9 40.5 all-gather.8
  152.9 91.1 all-gather.6
  245.8 40.5 all-gather.4
  298.5 44.4 reduce-scatter.4
  348.6 290.4 reduce-scatter.6
where the time goes:
time: 649 us; the launch traced here: 648 us
  waiting for transfers between devices  582 us (90%)
  matrix products  24.8 us (4%)
  local copies, waits for them, and re-layouts  14.3 us (2%)
  between operations  14.2 us (2%)
  other arithmetic  12.4 us (2%)
    unnamed x7, waiting for transfers between devices  295 us
    all_gather x1, waiting for transfers between devices, on_device(): w_in_full = lax.all_gather(w_in, 'dp', axis=0, tiled=True)  92.7 us
    all_gather x1, waiting for transfers between devices, on_device(): lax.all_gather(w_out, 'dp', axis=1, tiled=True)  87.7 us
    all_gather x1, waiting for transfers between devices, on_device(): lax.all_gather(normed_local, 'tensor', axis=0, tiled=True)  43 us
    all_gather x1, waiting for transfers between devices, on_device(): lax.all_gather(grad_out, 'tensor', axis=0, tiled=True)  42.2 us
    reduce_scatter x1, waiting for transfers between devices, on_device(): lax.psum_scatter(lax.dot_general(grad_pre, w_in_full, (((1,), (1,)), ((),...  21.4 us
  transfers between devices with their start and end apart: 6, of which 6 were waited for; matrix products, arithmetic and copies ran while one was open for 6% of the time, Pallas kernels for 0%

commit v1 on v0

v1 whole, which is shorter than its diff:
```python
import functools

import jax
import jax.numpy as jnp
from jax import lax
from jax.experimental import pallas as pl
from jax.experimental.pallas import tpu as pltpu
from jax.sharding import Mesh, PartitionSpec as P

D = 1536
FD = 768
TD = 128
RB = 48
BF = jnp.bfloat16
F32 = jnp.float32
Z = ("zh", "zl")
X_STEPS = (0, 1, -1, 2)
Y_STEPS = (0, 1, -1, 2)
Z_STEPS = (0, 1, -1, 2, -2, 3, -3, 4)
SIZES = {"y": 4, "x": 4, "c": 2, Z: 8}
ANY = pl.BlockSpec(memory_space=pl.ANY)
VM = pl.BlockSpec(memory_space=pltpu.VMEM)
SM = pl.BlockSpec(memory_space=pltpu.SMEM)
PARAMS = pltpu.CompilerParams(vmem_limit_bytes=44 * 1024 * 1024)


def shift(value, axis, by):
    n = SIZES[axis]
    return lax.ppermute(value, axis, [(i, (i + by) % n) for i in range(n)])


def turn(value):
    pairs = [(y * 4 + z, z * 4 + y) for y in range(4) for z in range(4)]
    return lax.ppermute(value, ("y", "zl"), pairs)


def row_block(z, x):
    return ((z % 4) * 8 + (z // 4) * 4 + x) * RB


def rows_at(ref, z, x):
    return ref.at[pl.ds(pl.multiple_of(row_block(z, x), 16), RB)]


def norm_kernel(x_ref, gain_ref, bias_ref, grad_ref, out_ref):
    centred = x_ref[...].astype(F32)
    centred = centred - jnp.mean(centred, axis=-1, keepdims=True)
    variance = jnp.mean(centred * centred, axis=-1, keepdims=True)
    normed = centred * lax.rsqrt(variance + 1e-05)
    out_ref[0] = (normed * gain_ref[...] + bias_ref[...]).astype(BF)
    out_ref[1] = grad_ref[...]


def token_copies(pieces, kind, dst, sems):
    return [
        pltpu.make_async_copy(piece.at[kind], dst.at[pl.ds(i * TD, TD)], sems.at[i])
        for i, piece in enumerate(pieces)
    ]


def win_copies(pieces, me, dst, sems):
    copies = []
    for i, xs in enumerate(X_STEPS):
        for j, zs in enumerate(Z_STEPS):
            at = rows_at(dst, (me[1] - zs + 8) % 8, (me[0] - xs + 4) % 4)
            copies.append(pltpu.make_async_copy(pieces[i].at[j], at, sems.at[i * 8 + j]))
    return copies


def act_kernel(me, *refs):
    toks, wins = refs[:8], refs[8:12]
    wo_in, bias_ref, gp_ref, dwo_ref = refs[12:16]
    n_s, g_s, win_s, wo_s, dwo_s, sem_n, sem_g, sem_i, sem_o = refs[16:]
    n_copies = token_copies(toks, 0, n_s, sem_n)
    g_copies = token_copies(toks, 1, g_s, sem_g)
    i_copies = win_copies(wins, me, win_s, sem_i)
    o_copies = []
    for z in range(8):
        for i, xs in enumerate(X_STEPS):
            at = rows_at(wo_s, z, (me[0] - xs + 4) % 4)
            o_copies.append(pltpu.make_async_copy(wo_in.at[z, i], at, sem_o.at[z * 4 + i]))
    for group in (n_copies, i_copies, g_copies, o_copies):
        for copy in group:
            copy.start()
    for group in (n_copies, i_copies, g_copies, o_copies):
        for copy in group:
            copy.wait()

    def step(j, carry):
        cols = pl.ds(pl.multiple_of(j * 256, 256), 256)
        pre = jnp.dot(n_s[...], win_s[:, cols], preferred_element_type=F32) + bias_ref[:, cols]
        ga = 0.5 * jnp.dot(g_s[...], wo_s[:, cols], preferred_element_type=F32)
        s = jax.nn.sigmoid(pre)
        act = (pre * s).astype(BF)
        gp_ref[:, cols] = (ga * s * (1.0 + pre * (1.0 - s))).astype(BF)
        dwo = lax.dot_general(g_s[...], act, (((0,), (0,)), ((), ())), preferred_element_type=F32)
        dwo_s[:, cols] = (0.5 * dwo).astype(BF)
        return carry

    lax.fori_loop(0, 3, step, 0)
    outs = []
    for z in range(8):
        for i, xs in enumerate(X_STEPS):
            src = rows_at(dwo_s, z, (me[0] + xs + 4) % 4)
            outs.append(pltpu.make_async_copy(src, dwo_ref.at[z, i], sem_o.at[z * 4 + i]))
    for copy in outs:
        copy.start()
    for copy in outs:
        copy.wait()


def dwin_kernel(me, *refs):
    toks, gp_ref, outs = refs[:8], refs[8], refs[9:13]
    n_s, dw_s, sem_n, sem_o = refs[13:]
    copies = token_copies(toks, 0, n_s, sem_n)
    for copy in copies:
        copy.start()
    for copy in copies:
        copy.wait()

    def step(j, carry):
        cols = pl.ds(pl.multiple_of(j * 256, 256), 256)
        dw = lax.dot_general(
            n_s[...], gp_ref[:, cols], (((0,), (0,)), ((), ())), preferred_element_type=F32
        )
        dw_s[:, cols] = dw.astype(BF)
        return carry

    lax.fori_loop(0, 3, step, 0)
    copies = []
    for i, xs in enumerate(X_STEPS):
        for j, zs in enumerate(Z_STEPS):
            src = rows_at(dw_s, (me[1] + zs + 8) % 8, (me[0] + xs + 4) % 4)
            copies.append(pltpu.make_async_copy(src, outs[i].at[j], sem_o.at[i * 8 + j]))
    for copy in copies:
        copy.start()
    for copy in copies:
        copy.wait()


def dx_kernel(me, *refs):
    gp_ref, wins, own_ref, other_ref = refs[0], refs[1:5], refs[5], refs[6]
    win_s, sem_i = refs[7:]
    copies = win_copies(wins, me, win_s, sem_i)
    for copy in copies:
        copy.start()
    for copy in copies:
        copy.wait()

    def step(j, carry):
        cols = pl.ds(pl.multiple_of(j * 256, 256), 256)
        dx = lax.dot_general(
            gp_ref[...], win_s[cols, :], (((1,), (1,)), ((), ())), preferred_element_type=F32
        ).astype(BF)
        own_ref[:, cols] = dx[:512]
        other_ref[:, cols] = dx[512:]
        return carry

    lax.fori_loop(0, 6, step, 0)


def final_kernel(x_ref, gain_ref, grad_ref, a_ref, b_ref, c_ref, d_ref, out_ref):
    centred = x_ref[...].astype(F32)
    centred = centred - jnp.mean(centred, axis=-1, keepdims=True)
    variance = jnp.mean(centred * centred, axis=-1, keepdims=True)
    inv_scale = lax.rsqrt(variance + 1e-05)
    normed = centred * inv_scale
    total = (a_ref[...].astype(F32) + b_ref[...].astype(F32)) + (
        c_ref[...].astype(F32) + d_ref[...].astype(F32)
    )
    scaled = total * gain_ref[...]
    first = jnp.mean(scaled, axis=-1, keepdims=True)
    second = jnp.mean(scaled * normed, axis=-1, keepdims=True)
    result = grad_ref[...].astype(F32) + inv_scale * (scaled - first - normed * second)
    out_ref[...] = result.astype(BF)


def cost(flops, moved):
    return pl.CostEstimate(flops=flops, bytes_accessed=moved, transcendentals=0)


def add_up(parts):
    total = parts[0].astype(F32)
    for part in parts[1:]:
        total = total + part.astype(F32)
    return total


def on_device(inputs, norm_gain, norm_bias, w_in, bias_in, w_out, grad_out):
    me = jnp.stack([lax.axis_index("x"), lax.axis_index(Z)]).astype(jnp.int32)
    gain, nbias = norm_gain.reshape(1, D), norm_bias.reshape(1, D)

    wo_own = turn(w_out.T)
    win_own = turn(w_in)
    bias = turn(bias_in).reshape(1, FD)

    tok = pl.pallas_call(
        norm_kernel,
        out_shape=jax.ShapeDtypeStruct((2, TD, D), BF),
        in_specs=[VM] * 4,
        out_specs=VM,
        compiler_params=PARAMS,
        cost_estimate=cost(10 * TD * D, 8 * TD * D),
    )(inputs, gain, nbias, grad_out)

    wo_x = jnp.stack([wo_own] + [shift(wo_own, "x", s) for s in X_STEPS[1:]])
    wo_all = lax.all_gather(wo_x, Z, axis=0, tiled=False)

    own = [tok] + [shift(tok, "y", s) for s in Y_STEPS[1:]]
    toks = own + [shift(piece, "c", 1) for piece in own]

    win_z = jnp.stack([win_own] + [shift(win_own, Z, s) for s in Z_STEPS[1:]])
    wins = [win_z] + [shift(win_z, "x", s) for s in X_STEPS[1:]]

    mm = 2 * 1024 * FD * D
    gp, dwo = pl.pallas_call(
        act_kernel,
        out_shape=(
            jax.ShapeDtypeStruct((1024, FD), BF),
            jax.ShapeDtypeStruct((8, 4, RB, FD), BF),
        ),
        in_specs=[SM] + [ANY] * 13 + [VM],
        out_specs=(VM, ANY),
        scratch_shapes=[
            pltpu.VMEM((1024, D), BF),
            pltpu.VMEM((1024, D), BF),
            pltpu.VMEM((D, FD), BF),
            pltpu.VMEM((D, FD), BF),
            pltpu.VMEM((D, FD), BF),
            pltpu.SemaphoreType.DMA((8,)),
            pltpu.SemaphoreType.DMA((8,)),
            pltpu.SemaphoreType.DMA((32,)),
            pltpu.SemaphoreType.DMA((32,)),
        ],
        compiler_params=PARAMS,
        cost_estimate=cost(3 * mm, 16 << 20),
    )(me, *toks, *wins, wo_all, bias)

    dwo_z = lax.psum_scatter(dwo, Z, scatter_dimension=0, tiled=False)

    dws = pl.pallas_call(
        dwin_kernel,
        out_shape=[jax.ShapeDtypeStruct((8, RB, FD), BF)] * 4,
        in_specs=[SM] + [ANY] * 8 + [VM],
        out_specs=[ANY] * 4,
        scratch_shapes=[
            pltpu.VMEM((1024, D), BF),
            pltpu.VMEM((D, FD), BF),
            pltpu.SemaphoreType.DMA((8,)),
            pltpu.SemaphoreType.DMA((32,)),
        ],
        compiler_params=PARAMS,
        cost_estimate=cost(mm, 7 << 20),
    )(me, *toks, gp)

    dx_own, dx_other = pl.pallas_call(
        dx_kernel,
        out_shape=[jax.ShapeDtypeStruct((512, D), BF)] * 2,
        in_specs=[SM, VM] + [ANY] * 4,
        out_specs=[VM, VM],
        scratch_shapes=[pltpu.VMEM((D, FD), BF), pltpu.SemaphoreType.DMA((32,))],
        compiler_params=PARAMS,
        cost_estimate=cost(mm, 7 << 20),
    )(me, gp, *wins)

    dwin_x = add_up([dws[0]] + [shift(dws[i], "x", X_STEPS[i]) for i in range(1, 4)]).astype(BF)

    dx_swapped = shift(dx_other, "c", 1)
    parts = []
    for i, s in enumerate(Y_STEPS):
        rows = slice(i * TD, (i + 1) * TD)
        part = add_up([dx_own[rows], dx_swapped[rows]]).astype(BF)
        parts.append(part if i == 0 else shift(part, "y", -s))

    dwin = add_up([dwin_x[0]] + [shift(dwin_x[j], Z, Z_STEPS[j]) for j in range(1, 8)]).astype(BF)
    grad_w_in = turn(dwin).astype(F32)

    dwo_sum = add_up([dwo_z[0]] + [shift(dwo_z[i], "x", X_STEPS[i]) for i in range(1, 4)]).astype(BF)
    grad_w_out = turn(dwo_sum).astype(F32).T

    grad_in = pl.pallas_call(
        final_kernel,
        out_shape=jax.ShapeDtypeStruct((TD, D), BF),
        in_specs=[VM] * 7,
        out_specs=VM,
        compiler_params=PARAMS,
        cost_estimate=cost(20 * TD * D, 14 * TD * D),
    )(inputs, gain, grad_out, *parts)
    return grad_in, grad_w_in, grad_w_out


def solution(mesh):
    fine = Mesh(mesh.devices.reshape(4, 2, 4, 4, 2), ("y", "zh", "x", "zl", "c"))
    dp, tensor = ("y", "zh", "x"), ("zl", "c")
    rows = P(dp + tensor, None)
    return jax.shard_map(
        on_device,
        mesh=fine,
        in_specs=(rows, P(), P(), P(dp, tensor), P(tensor), P(tensor, dp), rows),
        out_specs=(rows, P(dp, tensor), P(tensor, dp)),
        check_vma=False,
    )
```

time: 649 us -> 248 us (0.38)
  waiting for transfers between devices: 582 us -> 94.4 us
  starting transfers between devices: 0.42 us -> 86.2 us
  Pallas kernels: 0 us -> 36.8 us
  matrix products: 24.8 us -> 0 us
  other arithmetic: 12.4 us -> 5.29 us
    unnamed x7 -> x2, waiting for transfers between devices: 295 us -> 0.03 us
    all_gather x4 -> x1, waiting for transfers between devices: 266 us -> 0.02 us  [on_device(): wo_all = lax.all_gather(wo_x, Z, axis=0, tiled=False)]
    ppermute x0 -> x42, waiting for transfers between devices: none -> 94.3 us  [the longest x37 83.4 us: shift(): return lax.ppermute(value, axis, [(i, (i + by) % n) for i in range(n)])]
    ppermute x0 -> x42, starting transfers between devices: none -> 86.1 us  [the longest x37 62.3 us: shift(): return lax.ppermute(value, axis, [(i, (i + by) % n) for i in range(n)])]
    pallas_call x0 -> x5, Pallas kernels: none -> 36.8 us  [the longest x1 17 us: on_device(): pl.pallas_call(act_kernel, out_shape=(jax.ShapeDtypeStruct((1024, FD), BF...]
    dot_general x5 -> x0, matrix products: 24.8 us -> none  [the longest x1 6.92 us: on_device(): jnp.dot(normed_full, w_in_full, preferred_element_type=jnp.float32)]
    reduce_scatter x1, waiting for transfers between devices: 21.4 us -> 0.01 us  [on_device(): dwo_z = lax.psum_scatter(dwo, Z, scatter_dimension=0, tiled=False)]
    unnamed x19 -> x31, local copies, waits for them, and re-layouts: 12.6 us -> 5.66 us
  transfers between devices with their start and end apart: 6 -> 44, of which waited for: 6 -> 19; matrix products, arithmetic and copies ran while one was open for 6% -> 3% of each run, Pallas kernels for 0% -> 8%
where the time goes in v1:
time: 248 us; the launch traced here: 245 us
  waiting for transfers between devices  94.4 us (38%)
  starting transfers between devices  86.2 us (35%)
  Pallas kernels  36.8 us (15%)
  between operations  14.3 us (6%)
  local copies, waits for them, and re-layouts  8.09 us (3%)
  other arithmetic  5.29 us (2%)
    ppermute x37, waiting for transfers between devices, shift(): return lax.ppermute(value, axis, [(i, (i + by) % n) for i in range(n)])  83.4 us
    ppermute x37, starting transfers between devices, shift(): return lax.ppermute(value, axis, [(i, (i + by) % n) for i in range(n)])  62.3 us
    ppermute x5, starting transfers between devices, turn(): return lax.ppermute(value, ('y', 'zl'), pairs)  23.9 us
    pallas_call x1, Pallas kernels, on_device(): pl.pallas_call(act_kernel, out_shape=(jax.ShapeDtypeStruct((1024, FD), BF...  17 us
    ppermute x5, waiting for transfers between devices, turn(): return lax.ppermute(value, ('y', 'zl'), pairs)  10.9 us
    pallas_call x1, Pallas kernels, on_device(): pl.pallas_call(dwin_kernel, out_shape=[jax.ShapeDtypeStruct((8, RB, FD),...  9.55 us
    pallas_call x1, Pallas kernels, on_device(): pl.pallas_call(dx_kernel, out_shape=[jax.ShapeDtypeStruct((512, D), BF)]...  8.49 us
    unnamed x31, local copies, waits for them, and re-layouts  5.66 us
  transfers between devices with their start and end apart: 44, of which 19 were waited for; matrix products, arithmetic and copies ran while one was open for 3% of the time, Pallas kernels for 8%

profile of v1, /device:TPU:16, one launch (start us, length us, event | category | flops | bytes accessed | tf_op | source)
XLA Modules:
  0.0 245.1 jit_solution(1965807486871421490)
XLA Ops:
  7.2 5.0 %collective-permute-start.18 = (bf16[48,768]{1,0:T(8,128)(2,1)}, bf16[48,768]{1,0:T(8,128)(2,1)S(1)}, u32[]{:S(2)}, u32[]{:S(2)}) collective-permute-start(bf16[48,768]{1,0:T(8,128)(2,1)} %bitcast.61), channel_id=1, source_target_pairs={{0,0},{2,64},{4,128},{6,192},{64,2},{66,66},{68,130},{70,194},{128... | collective-permute-start | bytes 221192 | tf_op jit(solution)/shard_map/ppermute | solution.py:34
  12.2 6.0 %collective-permute-done.18 = bf16[48,768]{1,0:T(8,128)(2,1)S(1)} collective-permute-done((bf16[48,768]{1,0:T(8,128)(2,1)}, bf16[48,768]{1,0:T(8,128)(2,1)S(1)}, u32[]{:S(2)}, u32[]{:S(2)}) %collective-permute-start.18) | collective-permute-done | bytes 73760 | tf_op jit(solution)/shard_map/ppermute | solution.py:34
  18.2 3.0 %collective-permute-start.21 = (bf16[48,768]{1,0:T(8,128)(2,1)S(1)}, bf16[48,768]{1,0:T(8,128)(2,1)S(1)}, u32[]{:S(2)}, u32[]{:S(2)}) collective-permute-start(bf16[48,768]{1,0:T(8,128)(2,1)S(1)} %collective-permute-done.18), channel_id=1, source_target_pairs={{0,16},{8,24},{16,0},{24,8},{1,17},{9,25},{17,1},{25,9},{2,18},{10... | collective-permute-start | bytes 221192 | tf_op jit(solution)/shard_map/ppermute | solution.py:29
  21.2 1.1 collective-permute-start.20
  24.2 1.4 collective-permute-done.20
  25.6 2.4 collective-permute-done.19
  28.8 4.9 %collective-permute-start.7 = (bf16[48,768]{1,0:T(8,128)(2,1)}, bf16[48,768]{1,0:T(8,128)(2,1)S(1)}, u32[]{:S(2)}, u32[]{:S(2)}) collective-permute-start(bf16[48,768]{1,0:T(8,128)(2,1)} %param.10), channel_id=1, source_target_pairs={{0,0},{2,64},{4,128},{6,192},{64,2},{66,66},{68,130},{70,194},{128... | collective-permute-start | bytes 221192 | tf_op jit(solution)/shard_map/ppermute | solution.py:34
  37.5 3.5 %collective-permute-start.1 = (bf16[2,128,1536]{2,1,0:T(8,128)(2,1)S(1)}, bf16[2,128,1536]{2,1,0:T(8,128)(2,1)}, u32[]{:S(2)}, u32[]{:S(2)}) collective-permute-start(bf16[2,128,1536]{2,1,0:T(8,128)(2,1)S(1)} %shard_map.94.refs_0_), channel_id=1, source_target_pairs={{0,192},{64,0},{128,64},{192,128},{1,193},{65,1},{129,65},{193,129... | collective-permute-start | bytes 2359304 | tf_op jit(solution)/shard_map/ppermute | solution.py:29
  41.0 5.7 %collective-permute-start.14 = (bf16[48,768]{1,0:T(8,128)(2,1)S(1)}, bf16[48,768]{1,0:T(8,128)(2,1)S(1)}, u32[]{:S(2)}, u32[]{:S(2)}) collective-permute-start(bf16[48,768]{1,0:T(8,128)(2,1)S(1)} %collective-permute-done.7), channel_id=1, source_target_pairs={{0,32},{2,34},{4,36},{6,38},{32,0},{34,2},{36,4},{38,6},{1,33},{3,... | collective-permute-start | bytes 221192 | tf_op jit(solution)/shard_map/ppermute | solution.py:29
  47.6 6.4 %collective-permute-done.8 = bf16[48,768]{1,0:T(8,128)(2,1)S(1)} collective-permute-done((bf16[48,768]{1,0:T(8,128)(2,1)S(1)}, bf16[48,768]{1,0:T(8,128)(2,1)S(1)}, u32[]{:S(2)}, u32[]{:S(2)}) %collective-permute-start.8) | collective-permute-done | bytes 73760 | tf_op jit(solution)/shard_map/ppermute | solution.py:29
  54.8 4.8 %collective-permute-done.9 = bf16[48,768]{1,0:T(8,128)(2,1)S(1)} collective-permute-done((bf16[48,768]{1,0:T(8,128)(2,1)S(1)}, bf16[48,768]{1,0:T(8,128)(2,1)S(1)}, u32[]{:S(2)}, u32[]{:S(2)}) %collective-permute-start.9) | collective-permute-done | bytes 73760 | tf_op jit(solution)/shard_map/ppermute | solution.py:29
  59.6 2.4 collective-permute-start.10
  62.0 6.0 %collective-permute-done.10 = bf16[48,768]{1,0:T(8,128)(2,1)S(1)} collective-permute-done((bf16[48,768]{1,0:T(8,128)(2,1)S(1)}, bf16[48,768]{1,0:T(8,128)(2,1)S(1)}, u32[]{:S(2)}, u32[]{:S(2)}) %collective-permute-start.10) | collective-permute-done | bytes 73760 | tf_op jit(solution)/shard_map/ppermute | solution.py:29
  68.1 6.7 %collective-permute-done.11 = bf16[48,768]{1,0:T(8,128)(2,1)S(1)} collective-permute-done((bf16[48,768]{1,0:T(8,128)(2,1)S(1)}, bf16[48,768]{1,0:T(8,128)(2,1)S(1)}, u32[]{:S(2)}, u32[]{:S(2)}) %collective-permute-start.11) | collective-permute-done | bytes 73760 | tf_op jit(solution)/shard_map/ppermute | solution.py:29
  74.7 3.9 %collective-permute-start.12 = (bf16[48,768]{1,0:T(8,128)(2,1)S(1)}, bf16[48,768]{1,0:T(8,128)(2,1)S(1)}, u32[]{:S(2)}, u32[]{:S(2)}) collective-permute-start(bf16[48,768]{1,0:T(8,128)(2,1)S(1)} %collective-permute-done.7), channel_id=1, source_target_pairs={{0,6},{2,32},{4,34},{6,36},{32,38},{34,0},{36,2},{38,4},{1,7},{3,3... | collective-permute-start | bytes 221192 | tf_op jit(solution)/shard_map/ppermute | solution.py:29
  78.6 3.6 %collective-permute-done.12 = bf16[48,768]{1,0:T(8,128)(2,1)S(1)} collective-permute-done((bf16[48,768]{1,0:T(8,128)(2,1)S(1)}, bf16[48,768]{1,0:T(8,128)(2,1)S(1)}, u32[]{:S(2)}, u32[]{:S(2)}) %collective-permute-start.12) | collective-permute-done | bytes 73760 | tf_op jit(solution)/shard_map/ppermute | solution.py:29
  82.2 3.5 %collective-permute-start.13 = (bf16[48,768]{1,0:T(8,128)(2,1)S(1)}, bf16[48,768]{1,0:T(8,128)(2,1)S(1)}, u32[]{:S(2)}, u32[]{:S(2)}) collective-permute-start(bf16[48,768]{1,0:T(8,128)(2,1)S(1)} %collective-permute-done.7), channel_id=1, source_target_pairs={{0,34},{2,36},{4,38},{6,0},{32,2},{34,4},{36,6},{38,32},{1,35},{3,... | collective-permute-start | bytes 221192 | tf_op jit(solution)/shard_map/ppermute | solution.py:29
  85.7 2.7 %collective-permute-done.13 = bf16[48,768]{1,0:T(8,128)(2,1)S(1)} collective-permute-done((bf16[48,768]{1,0:T(8,128)(2,1)S(1)}, bf16[48,768]{1,0:T(8,128)(2,1)S(1)}, u32[]{:S(2)}, u32[]{:S(2)}) %collective-permute-start.13) | collective-permute-done | bytes 73760 | tf_op jit(solution)/shard_map/ppermute | solution.py:29
  88.4 2.2 collective-permute-start.17
  90.7 4.9 %collective-permute-start.22 = (f32[768]{0:T(1024)S(1)}, f32[768]{0:T(1024)S(1)}, u32[]{:S(2)}, u32[]{:S(2)}) collective-permute-start(f32[768]{0:T(1024)S(1)} %copy-done.11), channel_id=1, source_target_pairs={{0,0},{2,64},{4,128},{6,192},{64,2},{66,66},{68,130},{70,194},{128... | collective-permute-start | bytes 9224 | tf_op jit(solution)/shard_map/ppermute | solution.py:34
  95.6 3.9 %collective-permute-done.22 = f32[768]{0:T(1024)S(1)} collective-permute-done((f32[768]{0:T(1024)S(1)}, f32[768]{0:T(1024)S(1)}, u32[]{:S(2)}, u32[]{:S(2)}) %collective-permute-start.22) | collective-permute-done | bytes 3104 | tf_op jit(solution)/shard_map/ppermute | solution.py:34
  99.5 2.7 %collective-permute-start.16 = (bf16[8,48,768]{2,1,0:T(8,128)(2,1)S(1)}, bf16[8,48,768]{2,1,0:T(8,128)(2,1)S(1)}, u32[]{:S(2)}, u32[]{:S(2)}) collective-permute-start(bf16[8,48,768]{2,1,0:T(8,128)(2,1)S(1)} %bitcast_dynamic-update-slice_fusion.refs_8_.refs_1_), channel_id=1, source_target_pairs={{0,24},{8,0},{16,8},{24,16},{1,25},{9,1},{17,9},{25,17},{2,26},{10... | collective-permute-start | bytes 1769480 | tf_op jit(solution)/shard_map/ppermute | solution.py:29
  103.2 7.7 %collective-permute-done.16.refs_10_.refs_3_ = bf16[8,48,768]{2,1,0:T(8,128)(2,1)S(1)} collective-permute-done((bf16[8,48,768]{2,1,0:T(8,128)(2,1)S(1)}, bf16[8,48,768]{2,1,0:T(8,128)(2,1)S(1)}, u32[]{:S(2)}, u32[]{:S(2)}) %collective-permute-start.16) | collective-permute-done | bytes 589856 | tf_op jit(solution)/shard_map/ppermute | solution.py:29
  110.9 1.8 collective-permute-start.15
  112.8 10.2 %collective-permute-done.15.refs_9_.refs_2_ = bf16[8,48,768]{2,1,0:T(8,128)(2,1)} collective-permute-done((bf16[8,48,768]{2,1,0:T(8,128)(2,1)S(1)}, bf16[8,48,768]{2,1,0:T(8,128)(2,1)}, u32[]{:S(2)}, u32[]{:S(2)}) %collective-permute-start.15) | collective-permute-done | bytes 589856 | tf_op jit(solution)/shard_map/ppermute | solution.py:29
  123.1 17.0 %shard_map.95 = (bf16[1024,768]{1,0:T(8,128)(2,1)S(1)}, bf16[8,4,48,768]{3,2,1,0:T(8,128)(2,1)}) custom-call(s32[2]{0:T(128)S(1)} %pad_add_fusion.me, bf16[2,128,1536]{2,1,0:T(8,128)(2,1)S(1)} %shard_map.94.refs_0_, bf16[2,128,1536]{2,1,0:T(8,128)(2,1)} %collective-permute-done.refs_1_, bf16[2,128,1536]{2,1,0:T(8,128)(2,1)} %collective-permute-done.1.refs_2_, ...), custom_call_target="tpu_custom_call" | custom-call | flops 7247757312 | bytes 16777216 | tf_op jit(solution)/shard_map/pallas_call | solution.py:216
  140.1 1.1 copy-done.8
  142.3 1.4 copy-done.9
  143.7 8.5 %shard_map.96 = (bf16[512,1536]{1,0:T(8,128)(2,1)S(1)}, bf16[512,1536]{1,0:T(8,128)(2,1)}) custom-call(s32[2]{0:T(128)S(1)} %pad_add_fusion.me, bf16[1024,768]{1,0:T(8,128)(2,1)S(1)} %copy-done.9, bf16[8,48,768]{2,1,0:T(8,128)(2,1)S(1)} %bitcast_dynamic-update-slice_fusion.refs_8_.refs_1_, bf16[8,48,768]{2,1,0:T(8,128)(2,1)} %collective-permute-done.15.refs_9_.refs_2_, ...), custom_call_target="tpu_custom_call" | custom-call | flops 2415919104 | bytes 7340032 | tf_op jit(solution)/shard_map/pallas_call | solution.py:256
  152.3 9.5 %shard_map.98 = (bf16[8,48,768]{2,1,0:T(8,128)(2,1)S(1)}, bf16[8,48,768]{2,1,0:T(8,128)(2,1)S(1)}, bf16[8,48,768]{2,1,0:T(8,128)(2,1)S(1)}, bf16[8,48,768]{2,1,0:T(8,128)(2,1)S(1)}) custom-call(s32[2]{0:T(128)S(1)} %pad_add_fusion.me, bf16[2,128,1536]{2,1,0:T(8,128)(2,1)S(1)} %shard_map.94.refs_0_, bf16[2,128,1536]{2,1,0:T(8,128)(2,1)} %collective-permute-done.refs_1_, ...), custom_call_target="tpu_custom_call" | custom-call | flops 2415919104 | bytes 7340032 | tf_op jit(solution)/shard_map/pallas_call | solution.py:241
  162.2 3.0 %collective-permute-start.28 = (bf16[8,48,768]{2,1,0:T(8,128)(2,1)S(1)}, bf16[8,48,768]{2,1,0:T(8,128)(2,1)S(1)}, u32[]{:S(2)}, u32[]{:S(2)}) collective-permute-start(bf16[8,48,768]{2,1,0:T(8,128)(2,1)S(1)} %get-tuple-element.16), channel_id=1, source_target_pairs={{0,24},{8,0},{16,8},{24,16},{1,25},{9,1},{17,9},{25,17},{2,26},{10... | collective-permute-start | bytes 1769480 | tf_op jit(solution)/shard_map/ppermute | solution.py:29
  165.2 14.1 %collective-permute-done.27 = bf16[8,48,768]{2,1,0:T(8,128)(2,1)S(1)} collective-permute-done((bf16[8,48,768]{2,1,0:T(8,128)(2,1)S(1)}, bf16[8,48,768]{2,1,0:T(8,128)(2,1)S(1)}, u32[]{:S(2)}, u32[]{:S(2)}) %collective-permute-start.27) | collective-permute-done | bytes 589856 | tf_op jit(solution)/shard_map/ppermute | solution.py:29
  179.3 11.5 %collective-permute-done.28 = bf16[8,48,768]{2,1,0:T(8,128)(2,1)S(1)} collective-permute-done((bf16[8,48,768]{2,1,0:T(8,128)(2,1)S(1)}, bf16[8,48,768]{2,1,0:T(8,128)(2,1)S(1)}, u32[]{:S(2)}, u32[]{:S(2)}) %collective-permute-start.28) | collective-permute-done | bytes 589856 | tf_op jit(solution)/shard_map/ppermute | solution.py:29
  191.9 1.4 collective-permute-start.30
  193.3 3.3 %collective-permute-start.36 = (bf16[48,768]{1,0:T(8,128)(2,1)S(1)}, bf16[48,768]{1,0:T(8,128)(2,1)S(1)}, u32[]{:S(2)}, u32[]{:S(2)}) collective-permute-start(bf16[48,768]{1,0:T(8,128)(2,1)S(1)} %get-tuple-element.24), channel_id=1, source_target_pairs={{0,32},{2,34},{4,36},{6,38},{32,0},{34,2},{36,4},{38,6},{1,33},{3,... | collective-permute-start | bytes 221192 | tf_op jit(solution)/shard_map/ppermute | solution.py:29
  196.5 1.3 collective-permute-start.35
  197.8 2.5 %collective-permute-start.34 = (bf16[48,768]{1,0:T(8,128)(2,1)S(1)}, bf16[48,768]{1,0:T(8,128)(2,1)S(1)}, u32[]{:S(2)}, u32[]{:S(2)}) collective-permute-start(bf16[48,768]{1,0:T(8,128)(2,1)S(1)} %get-tuple-element.26), channel_id=1, source_target_pairs={{0,6},{2,32},{4,34},{6,36},{32,38},{34,0},{36,2},{38,4},{1,7},{3,3... | collective-permute-start | bytes 221192 | tf_op jit(solution)/shard_map/ppermute | solution.py:29
  201.4 2.1 collective-permute-start.33
  204.4 2.0 collective-permute-done.35
  206.4 4.9 %collective-permute-start.31 = (bf16[48,768]{1,0:T(8,128)(2,1)S(1)}, bf16[48,768]{1,0:T(8,128)(2,1)S(1)}, u32[]{:S(2)}, u32[]{:S(2)}) collective-permute-start(bf16[48,768]{1,0:T(8,128)(2,1)S(1)} %get-tuple-element.29), channel_id=1, source_target_pairs={{0,38},{2,0},{4,2},{6,4},{32,6},{34,32},{36,34},{38,36},{1,39},{3,... | collective-permute-start | bytes 221192 | tf_op jit(solution)/shard_map/ppermute | solution.py:29
  212.3 1.8 add_convert_fusion.1
  214.1 2.0 collective-permute-start.26
  216.2 1.2 collective-permute-start.25
  218.2 3.8 %collective-permute-start.40 = (bf16[48,768]{1,0:T(8,128)(2,1)S(1)}, bf16[48,768]{1,0:T(8,128)(2,1)S(1)}, u32[]{:S(2)}, u32[]{:S(2)}) collective-permute-start(bf16[48,768]{1,0:T(8,128)(2,1)S(1)} %get-tuple-element.31), channel_id=1, source_target_pairs={{0,16},{8,24},{16,0},{24,8},{1,17},{9,25},{17,1},{25,9},{2,18},{10... | collective-permute-start | bytes 221192 | tf_op jit(solution)/shard_map/ppermute | solution.py:29
  222.1 2.2 collective-permute-done.40
  224.3 2.8 %collective-permute-start.37 = (bf16[48,768]{1,0:T(8,128)(2,1)S(1)}, bf16[48,768]{1,0:T(8,128)(2,1)S(1)}, u32[]{:S(2)}, u32[]{:S(2)}) collective-permute-start(bf16[48,768]{1,0:T(8,128)(2,1)S(1)} %fusion.9), channel_id=1, source_target_pairs={{0,0},{2,64},{4,128},{6,192},{64,2},{66,66},{68,130},{70,194},{128... | collective-permute-start | bytes 221192 | tf_op jit(solution)/shard_map/ppermute | solution.py:34
  228.1 6.3 %collective-permute-start.41 = (bf16[48,768]{1,0:T(8,128)(2,1)S(1)}, bf16[48,768]{1,0:T(8,128)(2,1)S(1)}, u32[]{:S(2)}, u32[]{:S(2)}) collective-permute-start(bf16[48,768]{1,0:T(8,128)(2,1)S(1)} %fusion.2), channel_id=1, source_target_pairs={{0,0},{2,64},{4,128},{6,192},{64,2},{66,66},{68,130},{70,194},{128... | collective-permute-start | bytes 221192 | tf_op jit(solution)/shard_map/ppermute | solution.py:34
  236.1 1.5 shard_map.97
  (92 shorter events, 19.0 us)
Async XLA Ops:
  7.2 115.9 %all-gather.3.cloned.1.call-start = ((), (), s32[]{:S(2)}) async-start(), calls=%async_computation.2 | async-start | bytes 2654208 | tf_op jit(solution)/shard_map/all_gather | solution.py:207
  7.2 11.0 %collective-permute-start.18 = (bf16[48,768]{1,0:T(8,128)(2,1)}, bf16[48,768]{1,0:T(8,128)(2,1)S(1)}, u32[]{:S(2)}, u32[]{:S(2)}) collective-permute-start(bf16[48,768]{1,0:T(8,128)(2,1)} %bitcast.61), channel_id=1, source_target_pairs={{0,0},{2,64},{4,128},{6,192},{64,2},{66,66},{68,130},{70,194},{128... | collective-permute-start | bytes 221192 | tf_op jit(solution)/shard_map/ppermute | solution.py:34
  18.2 6.0 %collective-permute-start.21 = (bf16[48,768]{1,0:T(8,128)(2,1)S(1)}, bf16[48,768]{1,0:T(8,128)(2,1)S(1)}, u32[]{:S(2)}, u32[]{:S(2)}) collective-permute-start(bf16[48,768]{1,0:T(8,128)(2,1)S(1)} %collective-permute-done.18), channel_id=1, source_target_pairs={{0,16},{8,24},{16,0},{24,8},{1,17},{9,25},{17,1},{25,9},{2,18},{10... | collective-permute-start | bytes 221192 | tf_op jit(solution)/shard_map/ppermute | solution.py:29
  21.2 4.4 %collective-permute-start.20 = (bf16[48,768]{1,0:T(8,128)(2,1)S(1)}, bf16[48,768]{1,0:T(8,128)(2,1)S(1)}, u32[]{:S(2)}, u32[]{:S(2)}) collective-permute-start(bf16[48,768]{1,0:T(8,128)(2,1)S(1)} %collective-permute-done.18), channel_id=1, source_target_pairs={{0,24},{8,0},{16,8},{24,16},{1,25},{9,1},{17,9},{25,17},{2,26},{10... | collective-permute-start | bytes 221192 | tf_op jit(solution)/shard_map/ppermute | solution.py:29
  22.4 5.6 %collective-permute-start.19 = (bf16[48,768]{1,0:T(8,128)(2,1)S(1)}, bf16[48,768]{1,0:T(8,128)(2,1)S(1)}, u32[]{:S(2)}, u32[]{:S(2)}) collective-permute-start(bf16[48,768]{1,0:T(8,128)(2,1)S(1)} %collective-permute-done.18), channel_id=1, source_target_pairs={{0,8},{8,16},{16,24},{24,0},{1,9},{9,17},{17,25},{25,1},{2,10},{10... | collective-permute-start | bytes 221192 | tf_op jit(solution)/shard_map/ppermute | solution.py:29
  28.7 62.0 %copy-start.11 = (f32[768]{0:T(1024)S(1)}, f32[768]{0:T(1024)}, u32[]{:S(2)}) copy-start(f32[768]{0:T(1024)} %param.11) | copy-start | bytes 9220
  28.7 171.7 %reduce-scatter.2.cloned.1.call-start = ((), (), s32[]{:S(2)}) async-start(), calls=%async_computation.1 | async-start | bytes 2654208 | tf_op jit(solution)/shard_map/reduce_scatter | solution.py:239
  28.8 12.2 %collective-permute-start.7 = (bf16[48,768]{1,0:T(8,128)(2,1)}, bf16[48,768]{1,0:T(8,128)(2,1)S(1)}, u32[]{:S(2)}, u32[]{:S(2)}) collective-permute-start(bf16[48,768]{1,0:T(8,128)(2,1)} %param.10), channel_id=1, source_target_pairs={{0,0},{2,64},{4,128},{6,192},{64,2},{66,66},{68,130},{70,194},{128... | collective-permute-start | bytes 221192 | tf_op jit(solution)/shard_map/ppermute | solution.py:34
  37.4 64.8 %collective-permute-start.2 = (bf16[2,128,1536]{2,1,0:T(8,128)(2,1)S(1)}, bf16[2,128,1536]{2,1,0:T(8,128)(2,1)S(1)}, u32[]{:S(2)}, u32[]{:S(2)}) collective-permute-start(bf16[2,128,1536]{2,1,0:T(8,128)(2,1)S(1)} %shard_map.94.refs_0_), channel_id=1, source_target_pairs={{0,128},{64,192},{128,0},{192,64},{1,129},{65,193},{129,1},{193,65... | collective-permute-start | bytes 2359304 | tf_op jit(solution)/shard_map/ppermute | solution.py:29
  37.5 65.2 %collective-permute-start.1 = (bf16[2,128,1536]{2,1,0:T(8,128)(2,1)S(1)}, bf16[2,128,1536]{2,1,0:T(8,128)(2,1)}, u32[]{:S(2)}, u32[]{:S(2)}) collective-permute-start(bf16[2,128,1536]{2,1,0:T(8,128)(2,1)S(1)} %shard_map.94.refs_0_), channel_id=1, source_target_pairs={{0,192},{64,0},{128,64},{192,128},{1,193},{65,1},{129,65},{193,129... | collective-permute-start | bytes 2359304 | tf_op jit(solution)/shard_map/ppermute | solution.py:29
  41.0 62.0 %collective-permute-start = (bf16[2,128,1536]{2,1,0:T(8,128)(2,1)S(1)}, bf16[2,128,1536]{2,1,0:T(8,128)(2,1)}, u32[]{:S(2)}, u32[]{:S(2)}) collective-permute-start(bf16[2,128,1536]{2,1,0:T(8,128)(2,1)S(1)} %shard_map.94.refs_0_), channel_id=1, source_target_pairs={{0,64},{64,128},{128,192},{192,0},{1,65},{65,129},{129,193},{193,1... | collective-permute-start | bytes 2359304 | tf_op jit(solution)/shard_map/ppermute | solution.py:29
  41.0 47.5 %collective-permute-start.14 = (bf16[48,768]{1,0:T(8,128)(2,1)S(1)}, bf16[48,768]{1,0:T(8,128)(2,1)S(1)}, u32[]{:S(2)}, u32[]{:S(2)}) collective-permute-start(bf16[48,768]{1,0:T(8,128)(2,1)S(1)} %collective-permute-done.7), channel_id=1, source_target_pairs={{0,32},{2,34},{4,36},{6,38},{32,0},{34,2},{36,4},{38,6},{1,33},{3,... | collective-permute-start | bytes 221192 | tf_op jit(solution)/shard_map/ppermute | solution.py:29
  46.7 7.3 %collective-permute-start.8 = (bf16[48,768]{1,0:T(8,128)(2,1)S(1)}, bf16[48,768]{1,0:T(8,128)(2,1)S(1)}, u32[]{:S(2)}, u32[]{:S(2)}) collective-permute-start(bf16[48,768]{1,0:T(8,128)(2,1)S(1)} %collective-permute-done.7), channel_id=1, source_target_pairs={{0,2},{2,4},{4,6},{6,32},{32,34},{34,36},{36,38},{38,0},{1,3},{3,5... | collective-permute-start | bytes 221192 | tf_op jit(solution)/shard_map/ppermute | solution.py:29
  54.0 5.6 %collective-permute-start.9 = (bf16[48,768]{1,0:T(8,128)(2,1)S(1)}, bf16[48,768]{1,0:T(8,128)(2,1)S(1)}, u32[]{:S(2)}, u32[]{:S(2)}) collective-permute-start(bf16[48,768]{1,0:T(8,128)(2,1)S(1)} %collective-permute-done.7), channel_id=1, source_target_pairs={{0,38},{2,0},{4,2},{6,4},{32,6},{34,32},{36,34},{38,36},{1,39},{3,... | collective-permute-start | bytes 221192 | tf_op jit(solution)/shard_map/ppermute | solution.py:29
  59.6 8.4 %collective-permute-start.10 = (bf16[48,768]{1,0:T(8,128)(2,1)S(1)}, bf16[48,768]{1,0:T(8,128)(2,1)S(1)}, u32[]{:S(2)}, u32[]{:S(2)}) collective-permute-start(bf16[48,768]{1,0:T(8,128)(2,1)S(1)} %collective-permute-done.7), channel_id=1, source_target_pairs={{0,4},{2,6},{4,32},{6,34},{32,36},{34,38},{36,0},{38,2},{1,5},{3,7... | collective-permute-start | bytes 221192 | tf_op jit(solution)/shard_map/ppermute | solution.py:29
  68.0 6.7 %collective-permute-start.11 = (bf16[48,768]{1,0:T(8,128)(2,1)S(1)}, bf16[48,768]{1,0:T(8,128)(2,1)S(1)}, u32[]{:S(2)}, u32[]{:S(2)}) collective-permute-start(bf16[48,768]{1,0:T(8,128)(2,1)S(1)} %collective-permute-done.7), channel_id=1, source_target_pairs={{0,36},{2,38},{4,0},{6,2},{32,4},{34,6},{36,32},{38,34},{1,37},{3,... | collective-permute-start | bytes 221192 | tf_op jit(solution)/shard_map/ppermute | solution.py:29
  74.7 7.5 %collective-permute-start.12 = (bf16[48,768]{1,0:T(8,128)(2,1)S(1)}, bf16[48,768]{1,0:T(8,128)(2,1)S(1)}, u32[]{:S(2)}, u32[]{:S(2)}) collective-permute-start(bf16[48,768]{1,0:T(8,128)(2,1)S(1)} %collective-permute-done.7), channel_id=1, source_target_pairs={{0,6},{2,32},{4,34},{6,36},{32,38},{34,0},{36,2},{38,4},{1,7},{3,3... | collective-permute-start | bytes 221192 | tf_op jit(solution)/shard_map/ppermute | solution.py:29
  82.2 6.2 %collective-permute-start.13 = (bf16[48,768]{1,0:T(8,128)(2,1)S(1)}, bf16[48,768]{1,0:T(8,128)(2,1)S(1)}, u32[]{:S(2)}, u32[]{:S(2)}) collective-permute-start(bf16[48,768]{1,0:T(8,128)(2,1)S(1)} %collective-permute-done.7), channel_id=1, source_target_pairs={{0,34},{2,36},{4,38},{6,0},{32,2},{34,4},{36,6},{38,32},{1,35},{3,... | collective-permute-start | bytes 221192 | tf_op jit(solution)/shard_map/ppermute | solution.py:29
  88.4 13.7 %collective-permute-start.17 = (bf16[8,48,768]{2,1,0:T(8,128)(2,1)S(1)}, bf16[8,48,768]{2,1,0:T(8,128)(2,1)S(1)}, u32[]{:S(2)}, u32[]{:S(2)}) collective-permute-start(bf16[8,48,768]{2,1,0:T(8,128)(2,1)S(1)} %bitcast_dynamic-update-slice_fusion.refs_8_.refs_1_), channel_id=1, source_target_pairs={{0,16},{8,24},{16,0},{24,8},{1,17},{9,25},{17,1},{25,9},{2,18},{10... | collective-permute-start | bytes 1769480 | tf_op jit(solution)/shard_map/ppermute | solution.py:29
  90.7 8.8 %collective-permute-start.22 = (f32[768]{0:T(1024)S(1)}, f32[768]{0:T(1024)S(1)}, u32[]{:S(2)}, u32[]{:S(2)}) collective-permute-start(f32[768]{0:T(1024)S(1)} %copy-done.11), channel_id=1, source_target_pairs={{0,0},{2,64},{4,128},{6,192},{64,2},{66,66},{68,130},{70,194},{128... | collective-permute-start | bytes 9224 | tf_op jit(solution)/shard_map/ppermute | solution.py:34
  99.5 11.4 %collective-permute-start.16 = (bf16[8,48,768]{2,1,0:T(8,128)(2,1)S(1)}, bf16[8,48,768]{2,1,0:T(8,128)(2,1)S(1)}, u32[]{:S(2)}, u32[]{:S(2)}) collective-permute-start(bf16[8,48,768]{2,1,0:T(8,128)(2,1)S(1)} %bitcast_dynamic-update-slice_fusion.refs_8_.refs_1_), channel_id=1, source_target_pairs={{0,24},{8,0},{16,8},{24,16},{1,25},{9,1},{17,9},{25,17},{2,26},{10... | collective-permute-start | bytes 1769480 | tf_op jit(solution)/shard_map/ppermute | solution.py:29
  102.2 20.8 %collective-permute-start.3 = (bf16[2,128,1536]{2,1,0:T(8,128)(2,1)S(1)}, bf16[2,128,1536]{2,1,0:T(8,128)(2,1)}, u32[]{:S(2)}, u32[]{:S(2)}) collective-permute-start(bf16[2,128,1536]{2,1,0:T(8,128)(2,1)S(1)} %shard_map.94.refs_0_), channel_id=1, source_target_pairs={{0,1},{1,0},{2,3},{3,2},{4,5},{5,4},{6,7},{7,6},{8,9},{9,8},{10,11... | collective-permute-start | bytes 2359304 | tf_op jit(solution)/shard_map/ppermute | solution.py:29
  102.2 37.8 %copy-start.4 = (bf16[2,128,1536]{2,1,0:T(8,128)(2,1)}, bf16[2,128,1536]{2,1,0:T(8,128)(2,1)S(1)}, u32[]{:S(2)}) copy-start(bf16[2,128,1536]{2,1,0:T(8,128)(2,1)S(1)} %collective-permute-done.2.refs_3_) | copy-start | bytes 2359300
  102.2 20.8 %collective-permute-start.6 = (bf16[2,128,1536]{2,1,0:T(8,128)(2,1)S(1)}, bf16[2,128,1536]{2,1,0:T(8,128)(2,1)}, u32[]{:S(2)}, u32[]{:S(2)}) collective-permute-start(bf16[2,128,1536]{2,1,0:T(8,128)(2,1)S(1)} %collective-permute-done.2.refs_3_), channel_id=1, source_target_pairs={{0,1},{1,0},{2,3},{3,2},{4,5},{5,4},{6,7},{7,6},{8,9},{9,8},{10,11... | collective-permute-start | bytes 2359304 | tf_op jit(solution)/shard_map/ppermute | solution.py:29
  102.7 20.3 %collective-permute-start.5 = (bf16[2,128,1536]{2,1,0:T(8,128)(2,1)}, bf16[2,128,1536]{2,1,0:T(8,128)(2,1)}, u32[]{:S(2)}, u32[]{:S(2)}) collective-permute-start(bf16[2,128,1536]{2,1,0:T(8,128)(2,1)} %collective-permute-done.1.refs_2_), channel_id=1, source_target_pairs={{0,1},{1,0},{2,3},{3,2},{4,5},{5,4},{6,7},{7,6},{8,9},{9,8},{10,11... | collective-permute-start | bytes 2359304 | tf_op jit(solution)/shard_map/ppermute | solution.py:29
  103.0 20.0 %collective-permute-start.4 = (bf16[2,128,1536]{2,1,0:T(8,128)(2,1)}, bf16[2,128,1536]{2,1,0:T(8,128)(2,1)}, u32[]{:S(2)}, u32[]{:S(2)}) collective-permute-start(bf16[2,128,1536]{2,1,0:T(8,128)(2,1)} %collective-permute-done.refs_1_), channel_id=1, source_target_pairs={{0,1},{1,0},{2,3},{3,2},{4,5},{5,4},{6,7},{7,6},{8,9},{9,8},{10,11... | collective-permute-start | bytes 2359304 | tf_op jit(solution)/shard_map/ppermute | solution.py:29
  110.9 29.1 %copy-start.6 = (bf16[8,48,768]{2,1,0:T(8,128)(2,1)}, bf16[8,48,768]{2,1,0:T(8,128)(2,1)S(1)}, u32[]{:S(2)}) copy-start(bf16[8,48,768]{2,1,0:T(8,128)(2,1)S(1)} %collective-permute-done.16.refs_10_.refs_3_) | copy-start | bytes 1769476
  110.9 12.1 %collective-permute-start.15 = (bf16[8,48,768]{2,1,0:T(8,128)(2,1)S(1)}, bf16[8,48,768]{2,1,0:T(8,128)(2,1)}, u32[]{:S(2)}, u32[]{:S(2)}) collective-permute-start(bf16[8,48,768]{2,1,0:T(8,128)(2,1)S(1)} %bitcast_dynamic-update-slice_fusion.refs_8_.refs_1_), channel_id=1, source_target_pairs={{0,8},{8,16},{16,24},{24,0},{1,9},{9,17},{17,25},{25,1},{2,10},{10... | collective-permute-start | bytes 1769480 | tf_op jit(solution)/shard_map/ppermute | solution.py:29
  152.2 59.1 %collective-permute-start.23 = (bf16[512,1536]{1,0:T(8,128)(2,1)}, bf16[512,1536]{1,0:T(8,128)(2,1)}, u32[]{:S(2)}, u32[]{:S(2)}) collective-permute-start(bf16[512,1536]{1,0:T(8,128)(2,1)} %get-tuple-element.13), channel_id=1, source_target_pairs={{0,1},{1,0},{2,3},{3,2},{4,5},{5,4},{6,7},{7,6},{8,9},{9,8},{10,11... | collective-permute-start | bytes 4718600 | tf_op jit(solution)/shard_map/ppermute | solution.py:29
  161.9 17.4 %collective-permute-start.27 = (bf16[8,48,768]{2,1,0:T(8,128)(2,1)S(1)}, bf16[8,48,768]{2,1,0:T(8,128)(2,1)S(1)}, u32[]{:S(2)}, u32[]{:S(2)}) collective-permute-start(bf16[8,48,768]{2,1,0:T(8,128)(2,1)S(1)} %get-tuple-element.15), channel_id=1, source_target_pairs={{0,8},{8,16},{16,24},{24,0},{1,9},{9,17},{17,25},{25,1},{2,10},{10... | collective-permute-start | bytes 1769480 | tf_op jit(solution)/shard_map/ppermute | solution.py:29
  162.2 28.6 %collective-permute-start.28 = (bf16[8,48,768]{2,1,0:T(8,128)(2,1)S(1)}, bf16[8,48,768]{2,1,0:T(8,128)(2,1)S(1)}, u32[]{:S(2)}, u32[]{:S(2)}) collective-permute-start(bf16[8,48,768]{2,1,0:T(8,128)(2,1)S(1)} %get-tuple-element.16), channel_id=1, source_target_pairs={{0,24},{8,0},{16,8},{24,16},{1,25},{9,1},{17,9},{25,17},{2,26},{10... | collective-permute-start | bytes 1769480 | tf_op jit(solution)/shard_map/ppermute | solution.py:29
  165.2 26.3 %collective-permute-start.29 = (bf16[8,48,768]{2,1,0:T(8,128)(2,1)S(1)}, bf16[8,48,768]{2,1,0:T(8,128)(2,1)S(1)}, u32[]{:S(2)}, u32[]{:S(2)}) collective-permute-start(bf16[8,48,768]{2,1,0:T(8,128)(2,1)S(1)} %get-tuple-element.17), channel_id=1, source_target_pairs={{0,16},{8,24},{16,0},{24,8},{1,17},{9,25},{17,1},{25,9},{2,18},{10... | collective-permute-start | bytes 1769480 | tf_op jit(solution)/shard_map/ppermute | solution.py:29
  191.9 9.5 %collective-permute-start.30 = (bf16[48,768]{1,0:T(8,128)(2,1)S(1)}, bf16[48,768]{1,0:T(8,128)(2,1)S(1)}, u32[]{:S(2)}, u32[]{:S(2)}) collective-permute-start(bf16[48,768]{1,0:T(8,128)(2,1)S(1)} %get-tuple-element.23), channel_id=1, source_target_pairs={{0,2},{2,4},{4,6},{6,32},{32,34},{34,36},{36,38},{38,0},{1,3},{3,5... | collective-permute-start | bytes 221192 | tf_op jit(solution)/shard_map/ppermute | solution.py:29
  193.3 10.2 %collective-permute-start.36 = (bf16[48,768]{1,0:T(8,128)(2,1)S(1)}, bf16[48,768]{1,0:T(8,128)(2,1)S(1)}, u32[]{:S(2)}, u32[]{:S(2)}) collective-permute-start(bf16[48,768]{1,0:T(8,128)(2,1)S(1)} %get-tuple-element.24), channel_id=1, source_target_pairs={{0,32},{2,34},{4,36},{6,38},{32,0},{34,2},{36,4},{38,6},{1,33},{3,... | collective-permute-start | bytes 221192 | tf_op jit(solution)/shard_map/ppermute | solution.py:29
  196.5 9.8 %collective-permute-start.35 = (bf16[48,768]{1,0:T(8,128)(2,1)S(1)}, bf16[48,768]{1,0:T(8,128)(2,1)S(1)}, u32[]{:S(2)}, u32[]{:S(2)}) collective-permute-start(bf16[48,768]{1,0:T(8,128)(2,1)S(1)} %get-tuple-element.25), channel_id=1, source_target_pairs={{0,34},{2,36},{4,38},{6,0},{32,2},{34,4},{36,6},{38,32},{1,35},{3,... | collective-permute-start | bytes 221192 | tf_op jit(solution)/shard_map/ppermute | solution.py:29
  197.8 16.3 %collective-permute-start.34 = (bf16[48,768]{1,0:T(8,128)(2,1)S(1)}, bf16[48,768]{1,0:T(8,128)(2,1)S(1)}, u32[]{:S(2)}, u32[]{:S(2)}) collective-permute-start(bf16[48,768]{1,0:T(8,128)(2,1)S(1)} %get-tuple-element.26), channel_id=1, source_target_pairs={{0,6},{2,32},{4,34},{6,36},{32,38},{34,0},{36,2},{38,4},{1,7},{3,3... | collective-permute-start | bytes 221192 | tf_op jit(solution)/shard_map/ppermute | solution.py:29
  201.4 14.8 %collective-permute-start.33 = (bf16[48,768]{1,0:T(8,128)(2,1)S(1)}, bf16[48,768]{1,0:T(8,128)(2,1)S(1)}, u32[]{:S(2)}, u32[]{:S(2)}) collective-permute-start(bf16[48,768]{1,0:T(8,128)(2,1)S(1)} %get-tuple-element.27), channel_id=1, source_target_pairs={{0,36},{2,38},{4,0},{6,2},{32,4},{34,6},{36,32},{38,34},{1,37},{3,... | collective-permute-start | bytes 221192 | tf_op jit(solution)/shard_map/ppermute | solution.py:29
  203.4 14.0 %collective-permute-start.32 = (bf16[48,768]{1,0:T(8,128)(2,1)S(1)}, bf16[48,768]{1,0:T(8,128)(2,1)S(1)}, u32[]{:S(2)}, u32[]{:S(2)}) collective-permute-start(bf16[48,768]{1,0:T(8,128)(2,1)S(1)} %get-tuple-element.28), channel_id=1, source_target_pairs={{0,4},{2,6},{4,32},{6,34},{32,36},{34,38},{36,0},{38,2},{1,5},{3,7... | collective-permute-start | bytes 221192 | tf_op jit(solution)/shard_map/ppermute | solution.py:29
  206.4 11.8 %collective-permute-start.31 = (bf16[48,768]{1,0:T(8,128)(2,1)S(1)}, bf16[48,768]{1,0:T(8,128)(2,1)S(1)}, u32[]{:S(2)}, u32[]{:S(2)}) collective-permute-start(bf16[48,768]{1,0:T(8,128)(2,1)S(1)} %get-tuple-element.29), channel_id=1, source_target_pairs={{0,38},{2,0},{4,2},{6,4},{32,6},{34,32},{36,34},{38,36},{1,39},{3,... | collective-permute-start | bytes 221192 | tf_op jit(solution)/shard_map/ppermute | solution.py:29
  211.3 10.7 %collective-permute-start.38 = (bf16[48,768]{1,0:T(8,128)(2,1)S(1)}, bf16[48,768]{1,0:T(8,128)(2,1)S(1)}, u32[]{:S(2)}, u32[]{:S(2)}) collective-permute-start(bf16[48,768]{1,0:T(8,128)(2,1)S(1)} %get-tuple-element.30), channel_id=1, source_target_pairs={{0,8},{8,16},{16,24},{24,0},{1,9},{9,17},{17,25},{25,1},{2,10},{10... | collective-permute-start | bytes 221192 | tf_op jit(solution)/shard_map/ppermute | solution.py:29
  212.3 23.8 %copy-start.3 = (bf16[128,1536]{1,0:T(8,128)(2,1)S(1)}, bf16[128,1536]{1,0:T(8,128)(2,1)}, u32[]{:S(2)}) copy-start(bf16[128,1536]{1,0:T(8,128)(2,1)} %grad_ref.3) | copy-start | bytes 1179652
  214.1 22.0 %collective-permute-start.26 = (bf16[128,1536]{1,0:T(8,128)(2,1)S(1)}, bf16[128,1536]{1,0:T(8,128)(2,1)S(1)}, u32[]{:S(2)}, u32[]{:S(2)}) collective-permute-start(bf16[128,1536]{1,0:T(8,128)(2,1)S(1)} %get-tuple-element.19), channel_id=1, source_target_pairs={{0,128},{64,192},{128,0},{192,64},{1,129},{65,193},{129,1},{193,65... | collective-permute-start | bytes 1179656 | tf_op jit(solution)/shard_map/ppermute | solution.py:29
  216.2 19.9 %collective-permute-start.25 = (bf16[128,1536]{1,0:T(8,128)(2,1)S(1)}, bf16[128,1536]{1,0:T(8,128)(2,1)S(1)}, u32[]{:S(2)}, u32[]{:S(2)}) collective-permute-start(bf16[128,1536]{1,0:T(8,128)(2,1)S(1)} %get-tuple-element.20), channel_id=1, source_target_pairs={{0,64},{64,128},{128,192},{192,0},{1,65},{65,129},{129,193},{193,1... | collective-permute-start | bytes 1179656 | tf_op jit(solution)/shard_map/ppermute | solution.py:29
  217.4 18.7 %collective-permute-start.24 = (bf16[128,1536]{1,0:T(8,128)(2,1)S(1)}, bf16[128,1536]{1,0:T(8,128)(2,1)S(1)}, u32[]{:S(2)}, u32[]{:S(2)}) collective-permute-start(bf16[128,1536]{1,0:T(8,128)(2,1)S(1)} %get-tuple-element.21), channel_id=1, source_target_pairs={{0,192},{64,0},{128,64},{192,128},{1,193},{65,1},{129,65},{193,129... | collective-permute-start | bytes 1179656 | tf_op jit(solution)/shard_map/ppermute | solution.py:29
  218.2 6.1 %collective-permute-start.40 = (bf16[48,768]{1,0:T(8,128)(2,1)S(1)}, bf16[48,768]{1,0:T(8,128)(2,1)S(1)}, u32[]{:S(2)}, u32[]{:S(2)}) collective-permute-start(bf16[48,768]{1,0:T(8,128)(2,1)S(1)} %get-tuple-element.31), channel_id=1, source_target_pairs={{0,16},{8,24},{16,0},{24,8},{1,17},{9,25},{17,1},{25,9},{2,18},{10... | collective-permute-start | bytes 221192 | tf_op jit(solution)/shard_map/ppermute | solution.py:29
  222.0 5.2 %collective-permute-start.39 = (bf16[48,768]{1,0:T(8,128)(2,1)S(1)}, bf16[48,768]{1,0:T(8,128)(2,1)S(1)}, u32[]{:S(2)}, u32[]{:S(2)}) collective-permute-start(bf16[48,768]{1,0:T(8,128)(2,1)S(1)} %get-tuple-element.32), channel_id=1, source_target_pairs={{0,24},{8,0},{16,8},{24,16},{1,25},{9,1},{17,9},{25,17},{2,26},{10... | collective-permute-start | bytes 221192 | tf_op jit(solution)/shard_map/ppermute | solution.py:29
  224.3 11.1 %collective-permute-start.37 = (bf16[48,768]{1,0:T(8,128)(2,1)S(1)}, bf16[48,768]{1,0:T(8,128)(2,1)S(1)}, u32[]{:S(2)}, u32[]{:S(2)}) collective-permute-start(bf16[48,768]{1,0:T(8,128)(2,1)S(1)} %fusion.9), channel_id=1, source_target_pairs={{0,0},{2,64},{4,128},{6,192},{64,2},{66,66},{68,130},{70,194},{128... | collective-permute-start | bytes 221192 | tf_op jit(solution)/shard_map/ppermute | solution.py:34
  228.1 9.6 %collective-permute-start.41 = (bf16[48,768]{1,0:T(8,128)(2,1)S(1)}, bf16[48,768]{1,0:T(8,128)(2,1)S(1)}, u32[]{:S(2)}, u32[]{:S(2)}) collective-permute-start(bf16[48,768]{1,0:T(8,128)(2,1)S(1)} %fusion.2), channel_id=1, source_target_pairs={{0,0},{2,64},{4,128},{6,192},{64,2},{66,66},{68,130},{70,194},{128... | collective-permute-start | bytes 221192 | tf_op jit(solution)/shard_map/ppermute | solution.py:34
  (8 other events, 46.7 us)
Sparse Core Ops, SparseCore 0:
  28.8 48.6 all-gather.2
  141.4 41.9 reduce-scatter.1

commit v2 on v1

v2 whole, which is shorter than its diff:
```python
import functools

import jax
import jax.numpy as jnp
from jax import lax
from jax.experimental import pallas as pl
from jax.experimental.pallas import tpu as pltpu
from jax.sharding import Mesh, PartitionSpec as P

D = 1536
FD = 768
TD = 128
RB = 48
BF = jnp.bfloat16
F32 = jnp.float32
Z = ("zh", "zl")
X_STEPS = (0, 1, -1, 2)
Z_STEPS = tuple((r, h) for r in (0, 1, -1, 2) for h in (0, 4))
RING = tuple((k, (0, 1, 2, 3)) for k in (0, -1, 1, -2, 2, -3, 3)) + ((-4, (0, 1)), (4, (2, 3)))
SIZES = {"y": 4, "x": 4, "c": 2, Z: 8}
ANY = pl.BlockSpec(memory_space=pl.ANY)
VM = pl.BlockSpec(memory_space=pltpu.VMEM)
SM = pl.BlockSpec(memory_space=pltpu.SMEM)
PARAMS = pltpu.CompilerParams(vmem_limit_bytes=60 * 1024 * 1024)


def shift(value, axis, by):
    n = SIZES[axis]
    return lax.ppermute(value, axis, [(i, (i + by) % n) for i in range(n)])


def turn(value):
    pairs = [(y * 4 + z, z * 4 + y) for y in range(4) for z in range(4)]
    return lax.ppermute(value, ("y", "zl"), pairs)


def row_block(z, x):
    return ((z % 4) * 8 + (z // 4) * 4 + x) * RB


def rows_at(ref, z, x):
    return ref.at[pl.ds(pl.multiple_of(row_block(z, x), 16), RB)]


def norm_kernel(x_ref, gain_ref, bias_ref, grad_ref, out_ref):
    centred = x_ref[...].astype(F32)
    centred = centred - jnp.mean(centred, axis=-1, keepdims=True)
    variance = jnp.mean(centred * centred, axis=-1, keepdims=True)
    normed = centred * lax.rsqrt(variance + 1e-05)
    out_ref[0] = (normed * gain_ref[...] + bias_ref[...]).astype(BF)
    out_ref[1] = grad_ref[...]


def token_copies(toks, me, kind, dst, sems):
    copies = []
    for i in range(8):
        owner = (i % 4) * 2 + (me[2] if i < 4 else 1 - me[2])
        at = dst.at[pl.ds(i * TD, TD)]
        copies.append(pltpu.make_async_copy(toks.at[owner, kind], at, sems.at[i]))
    return copies


def win_copies(pieces, me, dst, sems):
    copies = []
    for i in range(4):
        for j, (r, h) in enumerate(Z_STEPS):
            at = rows_at(dst, (me[1] - r + h + 8) % 8, i)
            copies.append(pltpu.make_async_copy(pieces.at[i, j], at, sems.at[i * 8 + j]))
    return copies


def main_kernel(me, *refs):
    toks, wins, wos = refs[0], refs[1], refs[2:11]
    bias_ref, gp_ref, dwo_ref, dwin_ref = refs[11:15]
    n_s, g_s, win_s, wo_s, act_s, dwo_s, dwin_s, sem_n, sem_g, sem_i, sem_o = refs[15:]
    n_copies = token_copies(toks, me, 0, n_s, sem_n)
    g_copies = token_copies(toks, me, 1, g_s, sem_g)
    i_copies = win_copies(wins, me, win_s, sem_i)
    o_copies = []
    for piece, (away, xs) in zip(wos, RING):
        for k, i in enumerate(xs):
            at = rows_at(wo_s, (me[1] + away + 8) % 8, (me[0] - X_STEPS[i] + 4) % 4)
            o_copies.append(pltpu.make_async_copy(piece.at[k], at, sem_o.at[len(o_copies)]))
    for copy in n_copies + i_copies + g_copies + o_copies:
        copy.start()
    for copy in n_copies + i_copies + g_copies + o_copies:
        copy.wait()

    def hidden(j, carry):
        cols = pl.ds(pl.multiple_of(j * 256, 256), 256)
        pre = jnp.dot(n_s[...], win_s[:, cols], preferred_element_type=F32) + bias_ref[:, cols]
        ga = 0.5 * jnp.dot(g_s[...], wo_s[:, cols], preferred_element_type=F32)
        s = jax.nn.sigmoid(pre)
        act_s[:, cols] = (pre * s).astype(BF)
        gp_ref[:, cols] = (ga * s * (1.0 + pre * (1.0 - s))).astype(BF)
        return carry

    lax.fori_loop(0, 3, hidden, 0)
    dims = (((0,), (0,)), ((), ()))

    def out_grad(zl, carry):
        rows = pl.ds(pl.multiple_of(zl * 384, 384), 384)
        dwo = lax.dot_general(g_s[:, rows], act_s[...], dims, preferred_element_type=F32)
        dwo_s[rows, :] = (0.5 * dwo).astype(BF)
        for zh in range(2):
            for i, xs in enumerate(X_STEPS):
                src = rows_at(dwo_s, zh * 4 + zl, (me[0] + xs + 4) % 4)
                dst = dwo_ref.at[zh * 4 + zl, i]
                pltpu.make_async_copy(src, dst, sem_o.at[zl * 8 + zh * 4 + i]).start()
        return carry

    def in_grad(zl, carry):
        rows = pl.ds(pl.multiple_of(zl * 384, 384), 384)
        dwin = lax.dot_general(n_s[:, rows], gp_ref[...], dims, preferred_element_type=F32)
        dwin_s[rows, :] = dwin.astype(BF)
        for zh in range(2):
            away = (zh * 4 + zl - me[1] + 8) % 8
            quarter = away % 4
            place = 2 * (quarter ^ (quarter // 2)) + ((away + 1) // 4) % 2
            for x in range(4):
                src = rows_at(dwin_s, zh * 4 + zl, x)
                dst = dwin_ref.at[x, place]
                pltpu.make_async_copy(src, dst, sem_i.at[zl * 8 + zh * 4 + x]).start()
        return carry

    lax.fori_loop(0, 4, out_grad, 0)
    lax.fori_loop(0, 4, in_grad, 0)
    for k in range(32):
        pltpu.make_async_copy(dwo_s.at[pl.ds(0, RB)], dwo_ref.at[0, 0], sem_o.at[k]).wait()
        pltpu.make_async_copy(dwin_s.at[pl.ds(0, RB)], dwin_ref.at[0, 0], sem_i.at[k]).wait()


def dx_kernel(me, *refs):
    gp_ref, wins, outs = refs[0], refs[1], refs[3:5]
    win_s, sem_i = refs[5:]
    copies = win_copies(wins, me, win_s, sem_i)
    for copy in copies:
        copy.start()
    for copy in copies:
        copy.wait()

    def step(j, carry):
        cols = pl.ds(pl.multiple_of(j * 512, 512), 512)
        dx = lax.dot_general(
            gp_ref[...], win_s[cols, :], (((1,), (1,)), ((), ())), preferred_element_type=F32
        ).astype(BF)
        outs[0][:, cols] = dx[:512]
        outs[1][:, cols] = dx[512:]
        return carry

    lax.fori_loop(0, 3, step, 0)


def final_kernel(x_ref, gain_ref, grad_ref, dx_ref, out_ref):
    centred = x_ref[...].astype(F32)
    centred = centred - jnp.mean(centred, axis=-1, keepdims=True)
    variance = jnp.mean(centred * centred, axis=-1, keepdims=True)
    inv_scale = lax.rsqrt(variance + 1e-05)
    normed = centred * inv_scale
    total = add_up([dx_ref[i] for i in range(4)])
    scaled = total * gain_ref[...]
    first = jnp.mean(scaled, axis=-1, keepdims=True)
    second = jnp.mean(scaled * normed, axis=-1, keepdims=True)
    result = grad_ref[...].astype(F32) + inv_scale * (scaled - first - normed * second)
    out_ref[...] = result.astype(BF)


def cost(flops, moved):
    return pl.CostEstimate(flops=flops, bytes_accessed=moved, transcendentals=0)


def add_up(parts):
    total = parts[0].astype(F32)
    for part in parts[1:]:
        total = total + part.astype(F32)
    return total


def on_device(inputs, norm_gain, norm_bias, w_in, bias_in, w_out, grad_out):
    me = jnp.stack([lax.axis_index(a) for a in ("x", Z, "c")]).astype(jnp.int32)

    wo_own = turn(w_out.T)
    win_own = turn(w_in)
    bias = turn(bias_in).reshape(1, FD)
    tok = pl.pallas_call(
        norm_kernel,
        out_shape=jax.ShapeDtypeStruct((2, TD, D), BF),
        in_specs=[VM] * 4,
        out_specs=VM,
        compiler_params=PARAMS,
        cost_estimate=cost(10 * TD * D, 8 * TD * D),
    )(inputs, norm_gain, norm_bias, grad_out)

    wo_own, win_own, tok = lax.optimization_barrier((wo_own, win_own, tok))
    wo_x = [wo_own] + [shift(wo_own, "x", s) for s in X_STEPS[1:]]
    win_far = shift(win_own, Z, 4)
    *wo_x, win_far = lax.optimization_barrier((*wo_x, win_far))
    toks = lax.all_gather(tok, ("y", "c"), axis=0, tiled=False)

    win_h = jnp.stack([win_own, win_far])
    win_z = [win_h] + [shift(win_h, Z, r) for r in (1, -1, 2)]
    wo_h = jnp.stack(wo_x)
    ahead, back = shift(wo_h, Z, 1), shift(wo_h, Z, -1)
    ahead, back, *win_z = lax.optimization_barrier((ahead, back, *win_z))
    win_z = jnp.broadcast_to(jnp.concatenate(win_z)[None], (4, 8, RB, FD))
    wins = lax.all_to_all(win_z, "x", 0, 0, tiled=True)
    wos = [wo_h, ahead, back]
    for _ in range(2):
        ahead, back = shift(ahead, Z, 1), shift(back, Z, -1)
        wos += [ahead, back]
    wos += [shift(ahead[:2], Z, 1), shift(back[2:], Z, -1)]

    mm = 2 * 1024 * FD * D
    gp, dwo, dws = pl.pallas_call(
        main_kernel,
        out_shape=(
            jax.ShapeDtypeStruct((1024, FD), BF),
            jax.ShapeDtypeStruct((8, 4, RB, FD), BF),
            jax.ShapeDtypeStruct((4, 8, RB, FD), BF),
        ),
        in_specs=[SM] + [ANY] * 11 + [VM],
        out_specs=(VM, ANY, ANY),
        scratch_shapes=[
            pltpu.VMEM((1024, D), BF),
            pltpu.VMEM((1024, D), BF),
            pltpu.VMEM((D, FD), BF),
            pltpu.VMEM((D, FD), BF),
            pltpu.VMEM((1024, FD), BF),
            pltpu.VMEM((D, FD), BF),
            pltpu.VMEM((D, FD), BF),
            pltpu.SemaphoreType.DMA((8,)),
            pltpu.SemaphoreType.DMA((8,)),
            pltpu.SemaphoreType.DMA((32,)),
            pltpu.SemaphoreType.DMA((32,)),
        ],
        compiler_params=PARAMS,
        cost_estimate=cost(4 * mm, 20 << 20),
    )(me, toks, wins, *wos, bias)

    dwo_z = lax.psum_scatter(dwo, Z, scatter_dimension=0, tiled=False)
    note = shift(dws[0, 0, :16], "c", 1)
    dx_own, dx_other = pl.pallas_call(
        dx_kernel,
        out_shape=[jax.ShapeDtypeStruct((512, D), BF)] * 2,
        in_specs=[SM, VM] + [ANY] * 2,
        out_specs=[VM] * 2,
        scratch_shapes=[pltpu.VMEM((D, FD), BF), pltpu.SemaphoreType.DMA((32,))],
        compiler_params=PARAMS,
        cost_estimate=cost(mm, 7 << 20),
    )(me, gp, wins, note)

    dws = lax.all_to_all(dws, "x", 0, 0, tiled=True)
    dx_c = add_up([dx_own, shift(dx_other, "c", 1)]).astype(BF)
    dx_y = lax.all_to_all(dx_c, "y", 0, 0, tiled=True).reshape(4, TD, D)
    dwin_x = add_up([dws[i] for i in range(4)]).astype(BF)
    pairs = [dwin_x[2 * i : 2 * i + 2] for i in range(4)]
    dwin_z = add_up([pairs[0]] + [shift(pairs[i], Z, r) for i, r in ((1, 1), (2, -1), (3, 2))]).astype(BF)
    dwin = add_up([dwin_z[0], shift(dwin_z[1], Z, 4)]).astype(BF)
    grad_w_in = turn(dwin).astype(F32)

    dwo_sum = add_up([dwo_z[0]] + [shift(dwo_z[i], "x", X_STEPS[i]) for i in range(1, 4)]).astype(BF)
    grad_w_out = turn(dwo_sum).astype(F32).T

    grad_in = pl.pallas_call(
        final_kernel,
        out_shape=jax.ShapeDtypeStruct((TD, D), BF),
        in_specs=[VM] * 4,
        out_specs=VM,
        compiler_params=PARAMS,
        cost_estimate=cost(20 * TD * D, 14 * TD * D),
    )(inputs, norm_gain, grad_out, dx_y)
    return grad_in, grad_w_in, grad_w_out


def solution(mesh):
    fine = Mesh(mesh.devices.reshape(4, 2, 4, 4, 2), ("y", "zh", "x", "zl", "c"))
    dp, tensor = ("y", "zh", "x"), ("zl", "c")
    rows = P(dp + tensor, None)
    return jax.shard_map(
        on_device,
        mesh=fine,
        in_specs=(rows, P(), P(), P(dp, tensor), P(tensor), P(tensor, dp), rows),
        out_specs=(rows, P(dp, tensor), P(tensor, dp)),
        check_vma=False,
    )
```

time: 248 us -> 196 us (0.79)
  waiting for transfers between devices: 94.4 us -> 60 us
  starting transfers between devices: 86.2 us -> 72.5 us
  Pallas kernels: 36.8 us -> 33.8 us
    ppermute x37 -> x24, waiting for transfers between devices: 83.4 us -> 32 us  [shift(): return lax.ppermute(value, axis, [(i, (i + by) % n) for i in range(n)])]
    ppermute x37 -> x24, starting transfers between devices: 62.3 us -> 38.6 us  [shift(): return lax.ppermute(value, axis, [(i, (i + by) % n) for i in range(n)])]
    all_to_all x0 -> x3, starting transfers between devices: none -> 14.2 us  [the longest x1 5.64 us: on_device(): dws = lax.all_to_all(dws, 'x', 0, 0, tiled=True)]
    all_to_all x0 -> x3, waiting for transfers between devices: none -> 10.1 us  [the longest x1 10.1 us: on_device(): dws = lax.all_to_all(dws, 'x', 0, 0, tiled=True)]
    reduce_scatter x1, waiting for transfers between devices: 0.01 us -> 7.93 us  [on_device(): dwo_z = lax.psum_scatter(dwo, Z, scatter_dimension=0, tiled=False)]
    pallas_call x2 -> x1, Pallas kernels: 26.5 us -> 20.1 us  [on_device(): pl.pallas_call(main_kernel, out_shape=(jax.ShapeDtypeStruct((1024, FD), B...]
    ppermute x5, starting transfers between devices: 23.9 us -> 19.6 us  [turn(): return lax.ppermute(value, ('y', 'zl'), pairs)]
    unnamed x31 -> x28, local copies, waits for them, and re-layouts: 5.66 us -> 3.23 us
  transfers between devices with their start and end apart: 44 -> 34, of which waited for: 19 -> 14; matrix products, arithmetic and copies ran while one was open for 3% -> 5% of each run, Pallas kernels for 8% -> 7%
where the time goes in v2:
time: 196 us; the launch traced here: 194 us
  starting transfers between devices  72.5 us (37%)
  waiting for transfers between devices  60 us (31%)
  Pallas kernels  33.8 us (17%)
  between operations  14.4 us (7%)
  local copies, waits for them, and re-layouts  7.25 us (4%)
  other arithmetic  6.44 us (3%)
    ppermute x24, starting transfers between devices, shift(): return lax.ppermute(value, axis, [(i, (i + by) % n) for i in range(n)])  38.6 us
    ppermute x24, waiting for transfers between devices, shift(): return lax.ppermute(value, axis, [(i, (i + by) % n) for i in range(n)])  32 us
    pallas_call x1, Pallas kernels, on_device(): pl.pallas_call(main_kernel, out_shape=(jax.ShapeDtypeStruct((1024, FD), B...  20.1 us
    ppermute x5, starting transfers between devices, turn(): return lax.ppermute(value, ('y', 'zl'), pairs)  19.6 us
    all_to_all x1, waiting for transfers between devices, on_device(): dws = lax.all_to_all(dws, 'x', 0, 0, tiled=True)  10.1 us
    ppermute x5, waiting for transfers between devices, turn(): return lax.ppermute(value, ('y', 'zl'), pairs)  9.91 us
    pallas_call x1, Pallas kernels, on_device(): pl.pallas_call(dx_kernel, out_shape=[jax.ShapeDtypeStruct((512, D), BF)]...  8.14 us
    reduce_scatter x1, waiting for transfers between devices, on_device(): dwo_z = lax.psum_scatter(dwo, Z, scatter_dimension=0, tiled=False)  7.93 us
  transfers between devices with their start and end apart: 34, of which 14 were waited for; matrix products, arithmetic and copies ran while one was open for 5% of the time, Pallas kernels for 7%

profile of v2, /device:TPU:16, one launch (start us, length us, event | category | flops | bytes accessed | tf_op | source)
XLA Modules:
  0.0 194.4 jit_solution(10556343801875421608)
XLA Ops:
  7.2 5.0 %collective-permute-start.1 = (bf16[48,768]{1,0:T(8,128)(2,1)}, bf16[48,768]{1,0:T(8,128)(2,1)S(1)}, u32[]{:S(2)}, u32[]{:S(2)}) collective-permute-start(bf16[48,768]{1,0:T(8,128)(2,1)} %param.10), channel_id=1, source_target_pairs={{0,0},{2,64},{4,128},{6,192},{64,2},{66,66},{68,130},{70,194},{128... | collective-permute-start | bytes 221192 | tf_op jit(solution)/shard_map/ppermute | solution.py:34
  12.2 4.2 %collective-permute-start = (bf16[48,768]{1,0:T(8,128)(2,1)}, bf16[48,768]{1,0:T(8,128)(2,1)S(1)}, u32[]{:S(2)}, u32[]{:S(2)}) collective-permute-start(bf16[48,768]{1,0:T(8,128)(2,1)} %bitcast.52), channel_id=1, source_target_pairs={{0,0},{2,64},{4,128},{6,192},{64,2},{66,66},{68,130},{70,194},{128... | collective-permute-start | bytes 221192 | tf_op jit(solution)/shard_map/ppermute | solution.py:34
  16.4 2.4 %shard_map.94 = bf16[2,128,1536]{2,1,0:T(8,128)(2,1)} custom-call(bf16[128,1536]{1,0:T(8,128)(2,1)} %x_ref.3, f32[1536]{0:T(1024)} %gain_ref.3, f32[1536]{0:T(1024)} %bias_ref.1, bf16[128,1536]{1,0:T(8,128)(2,1)} %grad_ref.3), custom_call_target="tpu_custom_call" | custom-call | flops 1966080 | bytes 1572864 | tf_op jit(solution)/shard_map/pallas_call | solution.py:185
  18.8 4.0 %collective-permute-done = bf16[48,768]{1,0:T(8,128)(2,1)S(1)} collective-permute-done((bf16[48,768]{1,0:T(8,128)(2,1)}, bf16[48,768]{1,0:T(8,128)(2,1)S(1)}, u32[]{:S(2)}, u32[]{:S(2)}) %collective-permute-start) | collective-permute-done | bytes 73760 | tf_op jit(solution)/shard_map/ppermute | solution.py:34
  22.7 6.0 %collective-permute-start.5 = (bf16[48,768]{1,0:T(8,128)(2,1)S(1)}, bf16[48,768]{1,0:T(8,128)(2,1)S(1)}, u32[]{:S(2)}, u32[]{:S(2)}) collective-permute-start(bf16[48,768]{1,0:T(8,128)(2,1)S(1)} %collective-permute-done.1), channel_id=1, source_target_pairs={{0,32},{2,34},{4,36},{6,38},{32,0},{34,2},{36,4},{38,6},{1,33},{3,... | collective-permute-start | bytes 221192 | tf_op jit(solution)/shard_map/ppermute | solution.py:29
  28.8 3.0 %collective-permute-start.4 = (bf16[48,768]{1,0:T(8,128)(2,1)S(1)}, bf16[48,768]{1,0:T(8,128)(2,1)S(1)}, u32[]{:S(2)}, u32[]{:S(2)}) collective-permute-start(bf16[48,768]{1,0:T(8,128)(2,1)S(1)} %collective-permute-done), channel_id=1, source_target_pairs={{0,16},{8,24},{16,0},{24,8},{1,17},{9,25},{17,1},{25,9},{2,18},{10... | collective-permute-start | bytes 221192 | tf_op jit(solution)/shard_map/ppermute | solution.py:29
  31.8 1.1 collective-permute-start.3
  32.9 0.9 collective-permute-start.2
  33.8 0.9 collective-permute-done.4
  34.7 1.4 collective-permute-done.3
  36.1 2.4 %collective-permute-done.2 = bf16[48,768]{1,0:T(8,128)(2,1)S(1)} collective-permute-done((bf16[48,768]{1,0:T(8,128)(2,1)S(1)}, bf16[48,768]{1,0:T(8,128)(2,1)S(1)}, u32[]{:S(2)}, u32[]{:S(2)}) %collective-permute-start.2) | collective-permute-done | bytes 73760 | tf_op jit(solution)/shard_map/ppermute | solution.py:29
  38.5 1.2 collective-permute-start.7
  39.7 0.9 collective-permute-start.6
  40.7 1.6 collective-permute-start.10
  42.3 1.1 collective-permute-start.9
  43.4 2.0 %collective-permute-start.8 = (bf16[2,48,768]{2,1,0:T(8,128)(2,1)S(1)}, bf16[2,48,768]{2,1,0:T(8,128)(2,1)S(1)}, u32[]{:S(2)}, u32[]{:S(2)}) collective-permute-start(bf16[2,48,768]{2,1,0:T(8,128)(2,1)S(1)} %pad_maximum_fusion.2), channel_id=1, source_target_pairs={{0,2},{2,4},{4,6},{6,32},{32,34},{34,36},{36,38},{38,0},{1,3},{3,5... | collective-permute-start | bytes 442376 | tf_op jit(solution)/shard_map/ppermute | solution.py:29
  45.5 8.3 %collective-permute-done.10 = bf16[2,48,768]{2,1,0:T(8,128)(2,1)S(1)} collective-permute-done((bf16[2,48,768]{2,1,0:T(8,128)(2,1)S(1)}, bf16[2,48,768]{2,1,0:T(8,128)(2,1)S(1)}, u32[]{:S(2)}, u32[]{:S(2)}) %collective-permute-start.10) | collective-permute-done | bytes 147488 | tf_op jit(solution)/shard_map/ppermute | solution.py:29
  53.8 2.9 %collective-permute-done.8 = bf16[2,48,768]{2,1,0:T(8,128)(2,1)S(1)} collective-permute-done((bf16[2,48,768]{2,1,0:T(8,128)(2,1)S(1)}, bf16[2,48,768]{2,1,0:T(8,128)(2,1)S(1)}, u32[]{:S(2)}, u32[]{:S(2)}) %collective-permute-start.8) | collective-permute-done | bytes 147488 | tf_op jit(solution)/shard_map/ppermute | solution.py:29
  56.7 1.7 broadcast_in_dim.2
  58.4 3.8 %all-to-all-start = ((bf16[4,8,48,768]{3,2,1,0:T(8,128)(2,1)}), bf16[4,8,48,768]{3,2,1,0:T(8,128)(2,1)S(1)}, u32[]{:S(2)}, u32[]{:S(2)}) async-start(bf16[4,8,48,768]{3,2,1,0:T(8,128)(2,1)} %broadcast_in_dim.2), calls=%async_computation | async-start | bytes 4718592 | tf_op jit(solution)/shard_map/all_to_all | solution.py:206
  62.4 3.2 %collective-permute-start.12 = (bf16[4,48,768]{2,1,0:T(8,128)(2,1)S(1)}, bf16[4,48,768]{2,1,0:T(8,128)(2,1)S(1)}, u32[]{:S(2)}, u32[]{:S(2)}) collective-permute-start(bf16[4,48,768]{2,1,0:T(8,128)(2,1)S(1)} %collective-permute-done.7.refs_4_), channel_id=1, source_target_pairs={{0,38},{2,0},{4,2},{6,4},{32,6},{34,32},{36,34},{38,36},{1,39},{3,... | collective-permute-start | bytes 884744 | tf_op jit(solution)/shard_map/ppermute | solution.py:29
  65.6 4.8 %collective-permute-done.11.refs_5_ = bf16[4,48,768]{2,1,0:T(8,128)(2,1)S(1)} collective-permute-done((bf16[4,48,768]{2,1,0:T(8,128)(2,1)S(1)}, bf16[4,48,768]{2,1,0:T(8,128)(2,1)S(1)}, u32[]{:S(2)}, u32[]{:S(2)}) %collective-permute-start.11) | collective-permute-done | bytes 294944 | tf_op jit(solution)/shard_map/ppermute | solution.py:29
  70.4 3.2 %collective-permute-start.14 = (bf16[4,48,768]{2,1,0:T(8,128)(2,1)S(1)}, bf16[4,48,768]{2,1,0:T(8,128)(2,1)S(1)}, u32[]{:S(2)}, u32[]{:S(2)}) collective-permute-start(bf16[4,48,768]{2,1,0:T(8,128)(2,1)S(1)} %collective-permute-done.12.refs_6_), channel_id=1, source_target_pairs={{0,38},{2,0},{4,2},{6,4},{32,6},{34,32},{36,34},{38,36},{1,39},{3,... | collective-permute-start | bytes 884744 | tf_op jit(solution)/shard_map/ppermute | solution.py:29
  73.6 5.5 %collective-permute-done.13.refs_7_ = bf16[4,48,768]{2,1,0:T(8,128)(2,1)S(1)} collective-permute-done((bf16[4,48,768]{2,1,0:T(8,128)(2,1)S(1)}, bf16[4,48,768]{2,1,0:T(8,128)(2,1)S(1)}, u32[]{:S(2)}, u32[]{:S(2)}) %collective-permute-start.13) | collective-permute-done | bytes 294944 | tf_op jit(solution)/shard_map/ppermute | solution.py:29
  79.3 3.5 %collective-permute-start.16 = (bf16[2,48,768]{2,1,0:T(8,128)(2,1)S(1)}, bf16[2,48,768]{2,1,0:T(8,128)(2,1)S(1)}, u32[]{:S(2)}, u32[]{:S(2)}) collective-permute-start(bf16[2,48,768]{2,1,0:T(8,128)(2,1)S(1)} %slice.89), channel_id=1, source_target_pairs={{0,38},{2,0},{4,2},{6,4},{32,6},{34,32},{36,34},{38,36},{1,39},{3,... | collective-permute-start | bytes 442376 | tf_op jit(solution)/shard_map/ppermute | solution.py:29
  82.8 2.2 %collective-permute-start.17 = (f32[768]{0:T(1024)S(1)}, f32[768]{0:T(1024)S(1)}, u32[]{:S(2)}, u32[]{:S(2)}) collective-permute-start(f32[768]{0:T(1024)S(1)} %copy-done.13), channel_id=1, source_target_pairs={{0,0},{2,64},{4,128},{6,192},{64,2},{66,66},{68,130},{70,194},{128... | collective-permute-start | bytes 9224 | tf_op jit(solution)/shard_map/ppermute | solution.py:34
  85.6 5.9 %collective-permute-done.17 = f32[768]{0:T(1024)S(1)} collective-permute-done((f32[768]{0:T(1024)S(1)}, f32[768]{0:T(1024)S(1)}, u32[]{:S(2)}, u32[]{:S(2)}) %collective-permute-start.17) | collective-permute-done | bytes 3104 | tf_op jit(solution)/shard_map/ppermute | solution.py:34
  92.9 0.8 copy-done.1
  93.6 20.1 %shard_map.95 = (bf16[1024,768]{1,0:T(8,128)(2,1)}, bf16[8,4,48,768]{3,2,1,0:T(8,128)(2,1)}, bf16[4,8,48,768]{3,2,1,0:T(8,128)(2,1)}) custom-call(s32[3]{0:T(128)} %pad_add_fusion.me, bf16[8,2,128,1536]{3,2,1,0:T(8,128)(2,1)} %bitcast.51, bf16[4,8,48,768]{3,2,1,0:T(8,128)(2,1)} %copy-done.1, bf16[4,48,768]{2,1,0:T(8,128)(2,1)} %copy-done.3, ...), custom_call_target="tpu_custom_call" | custom-call | flops 9663676416 | bytes 20971520 | tf_op jit(solution)/shard_map/pallas_call | solution.py:214
  113.8 5.6 %all-to-all-start.2 = ((bf16[4,8,48,768]{3,2,1,0:T(8,128)(2,1)}), bf16[4,8,48,768]{3,2,1,0:T(8,128)(2,1)S(1)}, u32[]{:S(2)}, u32[]{:S(2)}) async-start(bf16[4,8,48,768]{3,2,1,0:T(8,128)(2,1)} %get-tuple-element.37), calls=%async_computation.2 | async-start | bytes 4718592 | tf_op jit(solution)/shard_map/all_to_all | solution.py:252
  120.2 1.2 collective-permute-done.18.refs_2_
  122.0 8.1 %shard_map.96 = (bf16[512,1536]{1,0:T(8,128)(2,1)}, bf16[512,1536]{1,0:T(8,128)(2,1)}) custom-call(s32[3]{0:T(128)} %pad_add_fusion.me, bf16[1024,768]{1,0:T(8,128)(2,1)} %get-tuple-element.36.refs_0_, bf16[4,8,48,768]{3,2,1,0:T(8,128)(2,1)} %copy-done.1, bf16[16,768]{1,0:T(8,128)(2,1)} %copy-done.12), custom_call_target="tpu_custom_call" | custom-call | flops 2415919104 | bytes 7340032 | tf_op jit(solution)/shard_map/pallas_call | solution.py:242
  130.4 10.1 %all-to-all-done.2 = bf16[4,8,48,768]{3,2,1,0:T(8,128)(2,1)S(1)} async-done(((bf16[4,8,48,768]{3,2,1,0:T(8,128)(2,1)}), bf16[4,8,48,768]{3,2,1,0:T(8,128)(2,1)S(1)}, u32[]{:S(2)}, u32[]{:S(2)}) %all-to-all-start.2) | async-done | bytes 2359328 | tf_op jit(solution)/shard_map/all_to_all | solution.py:252
  141.0 3.1 %collective-permute-start.21 = (bf16[2,48,768]{2,1,0:T(8,128)(2,1)S(1)}, bf16[2,48,768]{2,1,0:T(8,128)(2,1)S(1)}, u32[]{:S(2)}, u32[]{:S(2)}) collective-permute-start(bf16[2,48,768]{2,1,0:T(8,128)(2,1)S(1)} %get-tuple-element.43), channel_id=1, source_target_pairs={{0,38},{2,0},{4,2},{6,4},{32,6},{34,32},{36,34},{38,36},{1,39},{3,... | collective-permute-start | bytes 442376 | tf_op jit(solution)/shard_map/ppermute | solution.py:29
  144.1 3.0 %add_convert_fusion = bf16[512,1536]{1,0:T(8,128)(2,1)} fusion(bf16[512,1536]{1,0:T(8,128)(2,1)} %collective-permute-done.19, bf16[512,1536]{1,0:T(8,128)(2,1)S(1)} %copy-done.2), kind=kLoop, calls=%fused_computation | loop fusion | flops 3145728 | bytes 4718592 | tf_op jit(solution)/shard_map/convert_element_type | solution.py:253
  147.1 4.8 %all-to-all-start.1 = ((bf16[4,128,1536]{2,1,0:T(8,128)(2,1)}), bf16[4,128,1536]{2,1,0:T(8,128)(2,1)S(1)}, u32[]{:S(2)}, u32[]{:S(2)}) async-start(bf16[4,128,1536]{2,1,0:T(8,128)(2,1)} %bitcast.12), calls=%async_computation.1 | async-start | bytes 3145728 | tf_op jit(solution)/shard_map/all_to_all | solution.py:254
  151.9 3.8 %collective-permute-done.22 = bf16[2,48,768]{2,1,0:T(8,128)(2,1)S(1)} collective-permute-done((bf16[2,48,768]{2,1,0:T(8,128)(2,1)S(1)}, bf16[2,48,768]{2,1,0:T(8,128)(2,1)S(1)}, u32[]{:S(2)}, u32[]{:S(2)}) %collective-permute-start.22) | collective-permute-done | bytes 147488 | tf_op jit(solution)/shard_map/ppermute | solution.py:29
  155.9 7.9 %reduce-scatter.2.cloned.1.call-done = bf16[1,4,48,768]{3,2,1,0:T(8,128)(2,1)} async-done(((bf16[8,4,48,768]{3,2,1,0:T(8,128)(2,1)}), bf16[1,4,48,768]{3,2,1,0:T(8,128)(2,1)}) %reduce-scatter.2.cloned.1.call-update) | async-done | bytes 294928 | tf_op jit(solution)/shard_map/reduce_scatter | solution.py:240
  163.8 1.0 slice_bitcast_fusion.6
  164.8 2.4 %collective-permute-start.25 = (bf16[48,768]{1,0:T(8,128)(2,1)S(1)}, bf16[48,768]{1,0:T(8,128)(2,1)S(1)}, u32[]{:S(2)}, u32[]{:S(2)}) collective-permute-start(bf16[48,768]{1,0:T(8,128)(2,1)S(1)} %get-tuple-element.44), channel_id=1, source_target_pairs={{0,8},{8,16},{16,24},{24,0},{1,9},{9,17},{17,25},{25,1},{2,10},{10... | collective-permute-start | bytes 221192 | tf_op jit(solution)/shard_map/ppermute | solution.py:29
  167.2 3.0 %collective-permute-start.27 = (bf16[48,768]{1,0:T(8,128)(2,1)S(1)}, bf16[48,768]{1,0:T(8,128)(2,1)S(1)}, u32[]{:S(2)}, u32[]{:S(2)}) collective-permute-start(bf16[48,768]{1,0:T(8,128)(2,1)S(1)} %get-tuple-element.45), channel_id=1, source_target_pairs={{0,16},{8,24},{16,0},{24,8},{1,17},{9,25},{17,1},{25,9},{2,18},{10... | collective-permute-start | bytes 221192 | tf_op jit(solution)/shard_map/ppermute | solution.py:29
  170.2 1.5 collective-permute-start.26
  171.7 1.9 collective-permute-start.24
  173.7 0.9 collective-permute-done.26
  174.6 0.9 fusion.5
  175.5 6.4 %collective-permute-start.28 = (bf16[48,768]{1,0:T(8,128)(2,1)S(1)}, bf16[48,768]{1,0:T(8,128)(2,1)S(1)}, u32[]{:S(2)}, u32[]{:S(2)}) collective-permute-start(bf16[48,768]{1,0:T(8,128)(2,1)S(1)} %fusion.5), channel_id=1, source_target_pairs={{0,0},{2,64},{4,128},{6,192},{64,2},{66,66},{68,130},{70,194},{128... | collective-permute-start | bytes 221192 | tf_op jit(solution)/shard_map/ppermute | solution.py:34
  182.6 1.2 copy-done
  183.7 3.1 %shard_map.97 = bf16[128,1536]{1,0:T(8,128)(2,1)} custom-call(bf16[128,1536]{1,0:T(8,128)(2,1)} %x_ref.3, f32[1536]{0:T(1024)} %gain_ref.3, bf16[128,1536]{1,0:T(8,128)(2,1)} %grad_ref.3, bf16[4,128,1536]{2,1,0:T(8,128)(2,1)} %copy-done), custom_call_target="tpu_custom_call" | custom-call | flops 3932160 | bytes 2752512 | tf_op jit(solution)/shard_map/pallas_call | solution.py:264
  (73 shorter events, 6.1 us)
Async XLA Ops:
  7.2 85.0 %all-gather.3.cloned.1.call-start = ((), (), s32[]{:S(2)}) async-start(), calls=%async_computation.5 | async-start | bytes 7077888 | tf_op jit(solution)/shard_map/all_gather | solution.py:198
  7.2 11.5 %collective-permute-start.1 = (bf16[48,768]{1,0:T(8,128)(2,1)}, bf16[48,768]{1,0:T(8,128)(2,1)S(1)}, u32[]{:S(2)}, u32[]{:S(2)}) collective-permute-start(bf16[48,768]{1,0:T(8,128)(2,1)} %param.10), channel_id=1, source_target_pairs={{0,0},{2,64},{4,128},{6,192},{64,2},{66,66},{68,130},{70,194},{128... | collective-permute-start | bytes 221192 | tf_op jit(solution)/shard_map/ppermute | solution.py:34
  12.2 10.5 %collective-permute-start = (bf16[48,768]{1,0:T(8,128)(2,1)}, bf16[48,768]{1,0:T(8,128)(2,1)S(1)}, u32[]{:S(2)}, u32[]{:S(2)}) collective-permute-start(bf16[48,768]{1,0:T(8,128)(2,1)} %bitcast.52), channel_id=1, source_target_pairs={{0,0},{2,64},{4,128},{6,192},{64,2},{66,66},{68,130},{70,194},{128... | collective-permute-start | bytes 221192 | tf_op jit(solution)/shard_map/ppermute | solution.py:34
  22.7 11.1 %collective-permute-start.5 = (bf16[48,768]{1,0:T(8,128)(2,1)S(1)}, bf16[48,768]{1,0:T(8,128)(2,1)S(1)}, u32[]{:S(2)}, u32[]{:S(2)}) collective-permute-start(bf16[48,768]{1,0:T(8,128)(2,1)S(1)} %collective-permute-done.1), channel_id=1, source_target_pairs={{0,32},{2,34},{4,36},{6,38},{32,0},{34,2},{36,4},{38,6},{1,33},{3,... | collective-permute-start | bytes 221192 | tf_op jit(solution)/shard_map/ppermute | solution.py:29
  28.8 6.0 %collective-permute-start.4 = (bf16[48,768]{1,0:T(8,128)(2,1)S(1)}, bf16[48,768]{1,0:T(8,128)(2,1)S(1)}, u32[]{:S(2)}, u32[]{:S(2)}) collective-permute-start(bf16[48,768]{1,0:T(8,128)(2,1)S(1)} %collective-permute-done), channel_id=1, source_target_pairs={{0,16},{8,24},{16,0},{24,8},{1,17},{9,25},{17,1},{25,9},{2,18},{10... | collective-permute-start | bytes 221192 | tf_op jit(solution)/shard_map/ppermute | solution.py:29
  31.8 4.4 %collective-permute-start.3 = (bf16[48,768]{1,0:T(8,128)(2,1)S(1)}, bf16[48,768]{1,0:T(8,128)(2,1)S(1)}, u32[]{:S(2)}, u32[]{:S(2)}) collective-permute-start(bf16[48,768]{1,0:T(8,128)(2,1)S(1)} %collective-permute-done), channel_id=1, source_target_pairs={{0,24},{8,0},{16,8},{24,16},{1,25},{9,1},{17,9},{25,17},{2,26},{10... | collective-permute-start | bytes 221192 | tf_op jit(solution)/shard_map/ppermute | solution.py:29
  32.9 5.6 %collective-permute-start.2 = (bf16[48,768]{1,0:T(8,128)(2,1)S(1)}, bf16[48,768]{1,0:T(8,128)(2,1)S(1)}, u32[]{:S(2)}, u32[]{:S(2)}) collective-permute-start(bf16[48,768]{1,0:T(8,128)(2,1)S(1)} %collective-permute-done), channel_id=1, source_target_pairs={{0,8},{8,16},{16,24},{24,0},{1,9},{9,17},{17,25},{25,1},{2,10},{10... | collective-permute-start | bytes 221192 | tf_op jit(solution)/shard_map/ppermute | solution.py:29
  38.5 19.9 %copy-start.3 = (bf16[4,48,768]{2,1,0:T(8,128)(2,1)}, bf16[4,48,768]{2,1,0:T(8,128)(2,1)S(1)}, u32[]{:S(2)}) copy-start(bf16[4,48,768]{2,1,0:T(8,128)(2,1)S(1)} %pad_maximum_fusion.1.refs_2_) | copy-start | bytes 884740
  38.5 18.1 %collective-permute-start.7 = (bf16[4,48,768]{2,1,0:T(8,128)(2,1)S(1)}, bf16[4,48,768]{2,1,0:T(8,128)(2,1)S(1)}, u32[]{:S(2)}, u32[]{:S(2)}) collective-permute-start(bf16[4,48,768]{2,1,0:T(8,128)(2,1)S(1)} %pad_maximum_fusion.1.refs_2_), channel_id=1, source_target_pairs={{0,38},{2,0},{4,2},{6,4},{32,6},{34,32},{36,34},{38,36},{1,39},{3,... | collective-permute-start | bytes 884744 | tf_op jit(solution)/shard_map/ppermute | solution.py:29
  39.7 16.9 %collective-permute-start.6 = (bf16[4,48,768]{2,1,0:T(8,128)(2,1)S(1)}, bf16[4,48,768]{2,1,0:T(8,128)(2,1)S(1)}, u32[]{:S(2)}, u32[]{:S(2)}) collective-permute-start(bf16[4,48,768]{2,1,0:T(8,128)(2,1)S(1)} %pad_maximum_fusion.1.refs_2_), channel_id=1, source_target_pairs={{0,2},{2,4},{4,6},{6,32},{32,34},{34,36},{36,38},{38,0},{1,3},{3,5... | collective-permute-start | bytes 884744 | tf_op jit(solution)/shard_map/ppermute | solution.py:29
  40.7 13.1 %collective-permute-start.10 = (bf16[2,48,768]{2,1,0:T(8,128)(2,1)S(1)}, bf16[2,48,768]{2,1,0:T(8,128)(2,1)S(1)}, u32[]{:S(2)}, u32[]{:S(2)}) collective-permute-start(bf16[2,48,768]{2,1,0:T(8,128)(2,1)S(1)} %pad_maximum_fusion.2), channel_id=1, source_target_pairs={{0,4},{2,6},{4,32},{6,34},{32,36},{34,38},{36,0},{38,2},{1,5},{3,7... | collective-permute-start | bytes 442376 | tf_op jit(solution)/shard_map/ppermute | solution.py:29
  42.3 11.4 %collective-permute-start.9 = (bf16[2,48,768]{2,1,0:T(8,128)(2,1)S(1)}, bf16[2,48,768]{2,1,0:T(8,128)(2,1)S(1)}, u32[]{:S(2)}, u32[]{:S(2)}) collective-permute-start(bf16[2,48,768]{2,1,0:T(8,128)(2,1)S(1)} %pad_maximum_fusion.2), channel_id=1, source_target_pairs={{0,38},{2,0},{4,2},{6,4},{32,6},{34,32},{36,34},{38,36},{1,39},{3,... | collective-permute-start | bytes 442376 | tf_op jit(solution)/shard_map/ppermute | solution.py:29
  43.4 13.2 %collective-permute-start.8 = (bf16[2,48,768]{2,1,0:T(8,128)(2,1)S(1)}, bf16[2,48,768]{2,1,0:T(8,128)(2,1)S(1)}, u32[]{:S(2)}, u32[]{:S(2)}) collective-permute-start(bf16[2,48,768]{2,1,0:T(8,128)(2,1)S(1)} %pad_maximum_fusion.2), channel_id=1, source_target_pairs={{0,2},{2,4},{4,6},{6,32},{32,34},{34,36},{36,38},{38,0},{1,3},{3,5... | collective-permute-start | bytes 442376 | tf_op jit(solution)/shard_map/ppermute | solution.py:29
  56.6 5.7 %copy-start.6 = (bf16[4,48,768]{2,1,0:T(8,128)(2,1)}, bf16[4,48,768]{2,1,0:T(8,128)(2,1)S(1)}, u32[]{:S(2)}) copy-start(bf16[4,48,768]{2,1,0:T(8,128)(2,1)S(1)} %collective-permute-done.7.refs_4_) | copy-start | bytes 884740
  56.6 5.6 %copy-start.7 = (bf16[4,48,768]{2,1,0:T(8,128)(2,1)}, bf16[4,48,768]{2,1,0:T(8,128)(2,1)S(1)}, u32[]{:S(2)}) copy-start(bf16[4,48,768]{2,1,0:T(8,128)(2,1)S(1)} %collective-permute-done.6.refs_3_) | copy-start | bytes 884740
  58.4 24.4 %copy-start.13 = (f32[768]{0:T(1024)S(1)}, f32[768]{0:T(1024)}, u32[]{:S(2)}) copy-start(f32[768]{0:T(1024)} %param.11) | copy-start | bytes 9220
  58.4 33.8 %all-to-all-start = ((bf16[4,8,48,768]{3,2,1,0:T(8,128)(2,1)}), bf16[4,8,48,768]{3,2,1,0:T(8,128)(2,1)S(1)}, u32[]{:S(2)}, u32[]{:S(2)}) async-start(bf16[4,8,48,768]{3,2,1,0:T(8,128)(2,1)} %broadcast_in_dim.2), calls=%async_computation | async-start | bytes 4718592 | tf_op jit(solution)/shard_map/all_to_all | solution.py:206
  62.2 101.6 %reduce-scatter.2.cloned.1.call-start = ((), (), s32[]{:S(2)}) async-start(), calls=%async_computation.4 | async-start | bytes 2654208 | tf_op jit(solution)/shard_map/reduce_scatter | solution.py:240
  62.3 8.1 %collective-permute-start.11 = (bf16[4,48,768]{2,1,0:T(8,128)(2,1)S(1)}, bf16[4,48,768]{2,1,0:T(8,128)(2,1)S(1)}, u32[]{:S(2)}, u32[]{:S(2)}) collective-permute-start(bf16[4,48,768]{2,1,0:T(8,128)(2,1)S(1)} %collective-permute-done.6.refs_3_), channel_id=1, source_target_pairs={{0,2},{2,4},{4,6},{6,32},{32,34},{34,36},{36,38},{38,0},{1,3},{3,5... | collective-permute-start | bytes 884744 | tf_op jit(solution)/shard_map/ppermute | solution.py:29
  62.4 8.0 %collective-permute-start.12 = (bf16[4,48,768]{2,1,0:T(8,128)(2,1)S(1)}, bf16[4,48,768]{2,1,0:T(8,128)(2,1)S(1)}, u32[]{:S(2)}, u32[]{:S(2)}) collective-permute-start(bf16[4,48,768]{2,1,0:T(8,128)(2,1)S(1)} %collective-permute-done.7.refs_4_), channel_id=1, source_target_pairs={{0,38},{2,0},{4,2},{6,4},{32,6},{34,32},{36,34},{38,36},{1,39},{3,... | collective-permute-start | bytes 884744 | tf_op jit(solution)/shard_map/ppermute | solution.py:29
  70.4 3.2 %copy-start.8 = (bf16[4,48,768]{2,1,0:T(8,128)(2,1)}, bf16[4,48,768]{2,1,0:T(8,128)(2,1)S(1)}, u32[]{:S(2)}) copy-start(bf16[4,48,768]{2,1,0:T(8,128)(2,1)S(1)} %collective-permute-done.11.refs_5_) | copy-start | bytes 884740
  70.4 8.8 %collective-permute-start.13 = (bf16[4,48,768]{2,1,0:T(8,128)(2,1)S(1)}, bf16[4,48,768]{2,1,0:T(8,128)(2,1)S(1)}, u32[]{:S(2)}, u32[]{:S(2)}) collective-permute-start(bf16[4,48,768]{2,1,0:T(8,128)(2,1)S(1)} %collective-permute-done.11.refs_5_), channel_id=1, source_target_pairs={{0,2},{2,4},{4,6},{6,32},{32,34},{34,36},{36,38},{38,0},{1,3},{3,5... | collective-permute-start | bytes 884744 | tf_op jit(solution)/shard_map/ppermute | solution.py:29
  70.4 12.4 %copy-start.9 = (bf16[4,48,768]{2,1,0:T(8,128)(2,1)}, bf16[4,48,768]{2,1,0:T(8,128)(2,1)S(1)}, u32[]{:S(2)}) copy-start(bf16[4,48,768]{2,1,0:T(8,128)(2,1)S(1)} %collective-permute-done.12.refs_6_) | copy-start | bytes 884740
  70.4 8.8 %collective-permute-start.14 = (bf16[4,48,768]{2,1,0:T(8,128)(2,1)S(1)}, bf16[4,48,768]{2,1,0:T(8,128)(2,1)S(1)}, u32[]{:S(2)}, u32[]{:S(2)}) collective-permute-start(bf16[4,48,768]{2,1,0:T(8,128)(2,1)S(1)} %collective-permute-done.12.refs_6_), channel_id=1, source_target_pairs={{0,38},{2,0},{4,2},{6,4},{32,6},{34,32},{36,34},{38,36},{1,39},{3,... | collective-permute-start | bytes 884744 | tf_op jit(solution)/shard_map/ppermute | solution.py:29
  79.1 13.1 %copy-start.4 = (bf16[4,48,768]{2,1,0:T(8,128)(2,1)}, bf16[4,48,768]{2,1,0:T(8,128)(2,1)S(1)}, u32[]{:S(2)}) copy-start(bf16[4,48,768]{2,1,0:T(8,128)(2,1)S(1)} %collective-permute-done.13.refs_7_) | copy-start | bytes 884740
  79.2 13.0 %collective-permute-start.15 = (bf16[2,48,768]{2,1,0:T(8,128)(2,1)S(1)}, bf16[2,48,768]{2,1,0:T(8,128)(2,1)S(1)}, u32[]{:S(2)}, u32[]{:S(2)}) collective-permute-start(bf16[2,48,768]{2,1,0:T(8,128)(2,1)S(1)} %slice.88), channel_id=1, source_target_pairs={{0,2},{2,4},{4,6},{6,32},{32,34},{34,36},{36,38},{38,0},{1,3},{3,5... | collective-permute-start | bytes 442376 | tf_op jit(solution)/shard_map/ppermute | solution.py:29
  79.3 13.0 %copy-start.5 = (bf16[4,48,768]{2,1,0:T(8,128)(2,1)}, bf16[4,48,768]{2,1,0:T(8,128)(2,1)S(1)}, u32[]{:S(2)}) copy-start(bf16[4,48,768]{2,1,0:T(8,128)(2,1)S(1)} %collective-permute-done.14.refs_8_) | copy-start | bytes 884740
  79.3 12.9 %collective-permute-start.16 = (bf16[2,48,768]{2,1,0:T(8,128)(2,1)S(1)}, bf16[2,48,768]{2,1,0:T(8,128)(2,1)S(1)}, u32[]{:S(2)}, u32[]{:S(2)}) collective-permute-start(bf16[2,48,768]{2,1,0:T(8,128)(2,1)S(1)} %slice.89), channel_id=1, source_target_pairs={{0,38},{2,0},{4,2},{6,4},{32,6},{34,32},{36,34},{38,36},{1,39},{3,... | collective-permute-start | bytes 442376 | tf_op jit(solution)/shard_map/ppermute | solution.py:29
  82.8 8.8 %collective-permute-start.17 = (f32[768]{0:T(1024)S(1)}, f32[768]{0:T(1024)S(1)}, u32[]{:S(2)}, u32[]{:S(2)}) collective-permute-start(f32[768]{0:T(1024)S(1)} %copy-done.13), channel_id=1, source_target_pairs={{0,0},{2,64},{4,128},{6,192},{64,2},{66,66},{68,130},{70,194},{128... | collective-permute-start | bytes 9224 | tf_op jit(solution)/shard_map/ppermute | solution.py:34
  92.1 0.7 copy-start.10
  92.2 0.7 copy-start.11
  92.2 1.5 copy-start.1
  113.8 26.7 %all-to-all-start.2 = ((bf16[4,8,48,768]{3,2,1,0:T(8,128)(2,1)}), bf16[4,8,48,768]{3,2,1,0:T(8,128)(2,1)S(1)}, u32[]{:S(2)}, u32[]{:S(2)}) async-start(bf16[4,8,48,768]{3,2,1,0:T(8,128)(2,1)} %get-tuple-element.37), calls=%async_computation.2 | async-start | bytes 4718592 | tf_op jit(solution)/shard_map/all_to_all | solution.py:252
  120.2 1.2 collective-permute-start.18
  121.4 0.6 copy-start.12
  130.1 14.0 %collective-permute-start.19 = (bf16[512,1536]{1,0:T(8,128)(2,1)}, bf16[512,1536]{1,0:T(8,128)(2,1)}, u32[]{:S(2)}, u32[]{:S(2)}) collective-permute-start(bf16[512,1536]{1,0:T(8,128)(2,1)} %get-tuple-element.39), channel_id=1, source_target_pairs={{0,1},{1,0},{2,3},{3,2},{4,5},{5,4},{6,7},{7,6},{8,9},{9,8},{10,11... | collective-permute-start | bytes 4718600 | tf_op jit(solution)/shard_map/ppermute | solution.py:29
  140.5 3.7 %copy-start.2 = (bf16[512,1536]{1,0:T(8,128)(2,1)S(1)}, bf16[512,1536]{1,0:T(8,128)(2,1)}, u32[]{:S(2)}) copy-start(bf16[512,1536]{1,0:T(8,128)(2,1)} %get-tuple-element.38) | copy-start | bytes 4718596
  140.8 11.1 %collective-permute-start.20 = (bf16[2,48,768]{2,1,0:T(8,128)(2,1)S(1)}, bf16[2,48,768]{2,1,0:T(8,128)(2,1)S(1)}, u32[]{:S(2)}, u32[]{:S(2)}) collective-permute-start(bf16[2,48,768]{2,1,0:T(8,128)(2,1)S(1)} %get-tuple-element.41), channel_id=1, source_target_pairs={{0,2},{2,4},{4,6},{6,32},{32,34},{34,36},{36,38},{38,0},{1,3},{3,5... | collective-permute-start | bytes 442376 | tf_op jit(solution)/shard_map/ppermute | solution.py:29
  140.9 14.8 %collective-permute-start.22 = (bf16[2,48,768]{2,1,0:T(8,128)(2,1)S(1)}, bf16[2,48,768]{2,1,0:T(8,128)(2,1)S(1)}, u32[]{:S(2)}, u32[]{:S(2)}) collective-permute-start(bf16[2,48,768]{2,1,0:T(8,128)(2,1)S(1)} %get-tuple-element.42), channel_id=1, source_target_pairs={{0,4},{2,6},{4,32},{6,34},{32,36},{34,38},{36,0},{38,2},{1,5},{3,7... | collective-permute-start | bytes 442376 | tf_op jit(solution)/shard_map/ppermute | solution.py:29
  141.0 14.7 %collective-permute-start.21 = (bf16[2,48,768]{2,1,0:T(8,128)(2,1)S(1)}, bf16[2,48,768]{2,1,0:T(8,128)(2,1)S(1)}, u32[]{:S(2)}, u32[]{:S(2)}) collective-permute-start(bf16[2,48,768]{2,1,0:T(8,128)(2,1)S(1)} %get-tuple-element.43), channel_id=1, source_target_pairs={{0,38},{2,0},{4,2},{6,4},{32,6},{34,32},{36,34},{38,36},{1,39},{3,... | collective-permute-start | bytes 442376 | tf_op jit(solution)/shard_map/ppermute | solution.py:29
  147.1 35.4 %all-to-all-start.1 = ((bf16[4,128,1536]{2,1,0:T(8,128)(2,1)}), bf16[4,128,1536]{2,1,0:T(8,128)(2,1)S(1)}, u32[]{:S(2)}, u32[]{:S(2)}) async-start(bf16[4,128,1536]{2,1,0:T(8,128)(2,1)} %bitcast.12), calls=%async_computation.1 | async-start | bytes 3145728 | tf_op jit(solution)/shard_map/all_to_all | solution.py:254
  155.8 15.9 %collective-permute-start.23 = (bf16[48,768]{1,0:T(8,128)(2,1)S(1)}, bf16[48,768]{1,0:T(8,128)(2,1)S(1)}, u32[]{:S(2)}, u32[]{:S(2)}) collective-permute-start(bf16[48,768]{1,0:T(8,128)(2,1)S(1)} %slice_bitcast_fusion.8), channel_id=1, source_target_pairs={{0,32},{2,34},{4,36},{6,38},{32,0},{34,2},{36,4},{38,6},{1,33},{3,... | collective-permute-start | bytes 221192 | tf_op jit(solution)/shard_map/ppermute | solution.py:29
  164.8 8.9 %collective-permute-start.25 = (bf16[48,768]{1,0:T(8,128)(2,1)S(1)}, bf16[48,768]{1,0:T(8,128)(2,1)S(1)}, u32[]{:S(2)}, u32[]{:S(2)}) collective-permute-start(bf16[48,768]{1,0:T(8,128)(2,1)S(1)} %get-tuple-element.44), channel_id=1, source_target_pairs={{0,8},{8,16},{16,24},{24,0},{1,9},{9,17},{17,25},{25,1},{2,10},{10... | collective-permute-start | bytes 221192 | tf_op jit(solution)/shard_map/ppermute | solution.py:29
  167.2 6.5 %collective-permute-start.27 = (bf16[48,768]{1,0:T(8,128)(2,1)S(1)}, bf16[48,768]{1,0:T(8,128)(2,1)S(1)}, u32[]{:S(2)}, u32[]{:S(2)}) collective-permute-start(bf16[48,768]{1,0:T(8,128)(2,1)S(1)} %get-tuple-element.45), channel_id=1, source_target_pairs={{0,16},{8,24},{16,0},{24,8},{1,17},{9,25},{17,1},{25,9},{2,18},{10... | collective-permute-start | bytes 221192 | tf_op jit(solution)/shard_map/ppermute | solution.py:29
  170.2 4.4 %collective-permute-start.26 = (bf16[48,768]{1,0:T(8,128)(2,1)S(1)}, bf16[48,768]{1,0:T(8,128)(2,1)S(1)}, u32[]{:S(2)}, u32[]{:S(2)}) collective-permute-start(bf16[48,768]{1,0:T(8,128)(2,1)S(1)} %get-tuple-element.46), channel_id=1, source_target_pairs={{0,24},{8,0},{16,8},{24,16},{1,25},{9,1},{17,9},{25,17},{2,26},{10... | collective-permute-start | bytes 221192 | tf_op jit(solution)/shard_map/ppermute | solution.py:29
  171.7 10.1 %collective-permute-start.24 = (bf16[48,768]{1,0:T(8,128)(2,1)S(1)}, bf16[48,768]{1,0:T(8,128)(2,1)S(1)}, u32[]{:S(2)}, u32[]{:S(2)}) collective-permute-start(bf16[48,768]{1,0:T(8,128)(2,1)S(1)} %fusion.6), channel_id=1, source_target_pairs={{0,0},{2,64},{4,128},{6,192},{64,2},{66,66},{68,130},{70,194},{128... | collective-permute-start | bytes 221192 | tf_op jit(solution)/shard_map/ppermute | solution.py:34
  175.5 11.4 %collective-permute-start.28 = (bf16[48,768]{1,0:T(8,128)(2,1)S(1)}, bf16[48,768]{1,0:T(8,128)(2,1)S(1)}, u32[]{:S(2)}, u32[]{:S(2)}) collective-permute-start(bf16[48,768]{1,0:T(8,128)(2,1)S(1)} %fusion.5), channel_id=1, source_target_pairs={{0,0},{2,64},{4,128},{6,192},{64,2},{66,66},{68,130},{70,194},{128... | collective-permute-start | bytes 221192 | tf_op jit(solution)/shard_map/ppermute | solution.py:34
  182.6 1.2 copy-start
Sparse Core Ops, SparseCore 0:
  22.9 43.8 all-gather.2
  113.9 49.8 reduce-scatter.1

commit v3 on v2

--- a/solution.py
+++ b/solution.py
@@ -29,9 +29,14 @@
     return lax.ppermute(value, axis, [(i, (i + by) % n) for i in range(n)])
 
 
-def turn(value):
-    pairs = [(y * 4 + z, z * 4 + y) for y in range(4) for z in range(4)]
-    return lax.ppermute(value, ("y", "zl"), pairs)
+def turn(value, far=0):
+    pairs = [
+        (y * 8 + h * 4 + z, z * 8 + (h ^ far) * 4 + y)
+        for y in range(4)
+        for h in range(2)
+        for z in range(4)
+    ]
+    return lax.ppermute(value, ("y", "zh", "zl"), pairs)
 
 
 def row_block(z, x):
@@ -71,8 +76,8 @@
 
 def main_kernel(me, *refs):
     toks, wins, wos = refs[0], refs[1], refs[2:11]
-    bias_ref, gp_ref, dwo_ref, dwin_ref = refs[11:15]
-    n_s, g_s, win_s, wo_s, act_s, dwo_s, dwin_s, sem_n, sem_g, sem_i, sem_o = refs[15:]
+    bias_ref, gp_ref, dwo_ref = refs[11:14]
+    n_s, g_s, win_s, wo_s, act_s, dwo_s, sem_n, sem_g, sem_i, sem_o = refs[14:]
     n_copies = token_copies(toks, me, 0, n_s, sem_n)
     g_copies = token_copies(toks, me, 1, g_s, sem_g)
     i_copies = win_copies(wins, me, win_s, sem_i)
@@ -109,8 +114,22 @@
                 pltpu.make_async_copy(src, dst, sem_o.at[zl * 8 + zh * 4 + i]).start()
         return carry
 
+    lax.fori_loop(0, 4, out_grad, 0)
+    for k in range(32):
+        pltpu.make_async_copy(dwo_s.at[pl.ds(0, RB)], dwo_ref.at[0, 0], sem_o.at[k]).wait()
+
+
+def dwin_kernel(me, *refs):
+    toks, gp_ref, dwin_ref, n_s, dwin_s, sem_n, sem_i = refs
+    copies = token_copies(toks, me, 0, n_s, sem_n)
+    for copy in copies:
+        copy.start()
+    for copy in copies:
+        copy.wait()
+
     def in_grad(zl, carry):
         rows = pl.ds(pl.multiple_of(zl * 384, 384), 384)
+        dims = (((0,), (0,)), ((), ()))
         dwin = lax.dot_general(n_s[:, rows], gp_ref[...], dims, preferred_element_type=F32)
         dwin_s[rows, :] = dwin.astype(BF)
         for zh in range(2):
@@ -123,16 +142,14 @@
                 pltpu.make_async_copy(src, dst, sem_i.at[zl * 8 + zh * 4 + x]).start()
         return carry
 
-    lax.fori_loop(0, 4, out_grad, 0)
     lax.fori_loop(0, 4, in_grad, 0)
     for k in range(32):
-        pltpu.make_async_copy(dwo_s.at[pl.ds(0, RB)], dwo_ref.at[0, 0], sem_o.at[k]).wait()
         pltpu.make_async_copy(dwin_s.at[pl.ds(0, RB)], dwin_ref.at[0, 0], sem_i.at[k]).wait()
 
 
 def dx_kernel(me, *refs):
-    gp_ref, wins, outs = refs[0], refs[1], refs[3:5]
-    win_s, sem_i = refs[5:]
+    gp_ref, wins, outs = refs[0], refs[1], refs[3:6]
+    win_s, sem_i = refs[6:]
     copies = win_copies(wins, me, win_s, sem_i)
     for copy in copies:
         copy.start()
@@ -145,13 +162,14 @@
             gp_ref[...], win_s[cols, :], (((1,), (1,)), ((), ())), preferred_element_type=F32
         ).astype(BF)
         outs[0][:, cols] = dx[:512]
-        outs[1][:, cols] = dx[512:]
+        for i in range(2):
+            outs[1 + i][:, cols] = dx[512 + 256 * i : 512 + 256 * (i + 1)]
         return carry
 
     lax.fori_loop(0, 3, step, 0)
 
 
-def final_kernel(x_ref, gain_ref, grad_ref, dx_ref, out_ref):
+def final_kernel(x_ref, gain_ref, grad_ref, dx_ref, after_ref, out_ref):
     centred = x_ref[...].astype(F32)
     centred = centred - jnp.mean(centred, axis=-1, keepdims=True)
     variance = jnp.mean(centred * centred, axis=-1, keepdims=True)
@@ -179,9 +197,10 @@
 def on_device(inputs, norm_gain, norm_bias, w_in, bias_in, w_out, grad_out):
     me = jnp.stack([lax.axis_index(a) for a in ("x", Z, "c")]).astype(jnp.int32)
 
-    wo_own = turn(w_out.T)
-    win_own = turn(w_in)
-    bias = turn(bias_in).reshape(1, FD)
+    both = turn(jnp.stack([w_in, w_out.T]))
+    win_far = turn(w_in, 1)
+    bias = turn(bias_in)
+
     tok = pl.pallas_call(
         norm_kernel,
         out_shape=jax.ShapeDtypeStruct((2, TD, D), BF),
@@ -191,17 +210,16 @@
         cost_estimate=cost(10 * TD * D, 8 * TD * D),
     )(inputs, norm_gain, norm_bias, grad_out)
 
-    wo_own, win_own, tok = lax.optimization_barrier((wo_own, win_own, tok))
-    wo_x = [wo_own] + [shift(wo_own, "x", s) for s in X_STEPS[1:]]
-    win_far = shift(win_own, Z, 4)
-    *wo_x, win_far = lax.optimization_barrier((*wo_x, win_far))
+    me, bias, both, win_far, tok = lax.optimization_barrier((me, bias, both, win_far, tok))
     toks = lax.all_gather(tok, ("y", "c"), axis=0, tiled=False)
 
-    win_h = jnp.stack([win_own, win_far])
+    wo_x = [both[1]] + [shift(both[1], "x", s) for s in X_STEPS[1:]]
+    win_h = jnp.stack([both[0], win_far])
     win_z = [win_h] + [shift(win_h, Z, r) for r in (1, -1, 2)]
+    *wo_x, w0, w1, w2, w3 = lax.optimization_barrier((*wo_x, *win_z))
+    win_z = [w0, w1, w2, w3]
     wo_h = jnp.stack(wo_x)
     ahead, back = shift(wo_h, Z, 1), shift(wo_h, Z, -1)
-    ahead, back, *win_z = lax.optimization_barrier((ahead, back, *win_z))
     win_z = jnp.broadcast_to(jnp.concatenate(win_z)[None], (4, 8, RB, FD))
     wins = lax.all_to_all(win_z, "x", 0, 0, tiled=True)
     wos = [wo_h, ahead, back]
@@ -209,17 +227,17 @@
         ahead, back = shift(ahead, Z, 1), shift(back, Z, -1)
         wos += [ahead, back]
     wos += [shift(ahead[:2], Z, 1), shift(back[2:], Z, -1)]
+    bias = bias.reshape(1, FD)
 
     mm = 2 * 1024 * FD * D
-    gp, dwo, dws = pl.pallas_call(
+    gp, dwo = pl.pallas_call(
         main_kernel,
         out_shape=(
             jax.ShapeDtypeStruct((1024, FD), BF),
             jax.ShapeDtypeStruct((8, 4, RB, FD), BF),
-            jax.ShapeDtypeStruct((4, 8, RB, FD), BF),
         ),
         in_specs=[SM] + [ANY] * 11 + [VM],
-        out_specs=(VM, ANY, ANY),
+        out_specs=(VM, ANY),
         scratch_shapes=[
             pltpu.VMEM((1024, D), BF),
             pltpu.VMEM((1024, D), BF),
@@ -227,48 +245,68 @@
             pltpu.VMEM((D, FD), BF),
             pltpu.VMEM((1024, FD), BF),
             pltpu.VMEM((D, FD), BF),
-            pltpu.VMEM((D, FD), BF),
             pltpu.SemaphoreType.DMA((8,)),
             pltpu.SemaphoreType.DMA((8,)),
             pltpu.SemaphoreType.DMA((32,)),
             pltpu.SemaphoreType.DMA((32,)),
         ],
         compiler_params=PARAMS,
-        cost_estimate=cost(4 * mm, 20 << 20),
+        cost_estimate=cost(3 * mm, 20 << 20),
     )(me, toks, wins, *wos, bias)
 
     dwo_z = lax.psum_scatter(dwo, Z, scatter_dimension=0, tiled=False)
+
+    dws = pl.pallas_call(
+        dwin_kernel,
+        out_shape=jax.ShapeDtypeStruct((4, 8, RB, FD), BF),
+        in_specs=[SM, ANY, VM],
+        out_specs=ANY,
+        scratch_shapes=[
+            pltpu.VMEM((1024, D), BF),
+            pltpu.VMEM((D, FD), BF),
+            pltpu.SemaphoreType.DMA((8,)),
+            pltpu.SemaphoreType.DMA((32,)),
+        ],
+        compiler_params=PARAMS,
+        cost_estimate=cost(mm, 7 << 20),
+    )(me, toks, gp)
     note = shift(dws[0, 0, :16], "c", 1)
-    dx_own, dx_other = pl.pallas_call(
+    dws = lax.all_to_all(dws, "x", 0, 0, tiled=True)
+
+    dx_own, *dx_other = pl.pallas_call(
         dx_kernel,
-        out_shape=[jax.ShapeDtypeStruct((512, D), BF)] * 2,
+        out_shape=[jax.ShapeDtypeStruct((512, D), BF)] + [jax.ShapeDtypeStruct((256, D), BF)] * 2,
         in_specs=[SM, VM] + [ANY] * 2,
-        out_specs=[VM] * 2,
+        out_specs=[VM] * 3,
         scratch_shapes=[pltpu.VMEM((D, FD), BF), pltpu.SemaphoreType.DMA((32,))],
         compiler_params=PARAMS,
         cost_estimate=cost(mm, 7 << 20),
     )(me, gp, wins, note)
 
-    dws = lax.all_to_all(dws, "x", 0, 0, tiled=True)
-    dx_c = add_up([dx_own, shift(dx_other, "c", 1)]).astype(BF)
+    swapped = jnp.concatenate([shift(part, "c", 1) for part in dx_other])
+    dx_c = add_up([dx_own, swapped]).astype(BF)
     dx_y = lax.all_to_all(dx_c, "y", 0, 0, tiled=True).reshape(4, TD, D)
     dwin_x = add_up([dws[i] for i in range(4)]).astype(BF)
     pairs = [dwin_x[2 * i : 2 * i + 2] for i in range(4)]
-    dwin_z = add_up([pairs[0]] + [shift(pairs[i], Z, r) for i, r in ((1, 1), (2, -1), (3, 2))]).astype(BF)
-    dwin = add_up([dwin_z[0], shift(dwin_z[1], Z, 4)]).astype(BF)
-    grad_w_in = turn(dwin).astype(F32)
-
-    dwo_sum = add_up([dwo_z[0]] + [shift(dwo_z[i], "x", X_STEPS[i]) for i in range(1, 4)]).astype(BF)
-    grad_w_out = turn(dwo_sum).astype(F32).T
+    moved = [shift(pairs[i], Z, r) for i, r in ((1, 1), (2, -1), (3, 2))]
+    sent = [shift(dwo_z[i], "x", X_STEPS[i]) for i in range(1, 4)]
+    *sent, m0, m1, m2 = lax.optimization_barrier((*sent, *moved))
+    moved = [m0, m1, m2]
+    dwin_z = add_up([pairs[0]] + moved).astype(BF)
+    dwo_sum = add_up([dwo_z[0]] + sent).astype(BF)
+    sums = jnp.stack([dwin_z[0], dwo_sum])
+    near, far = turn(sums), turn(dwin_z[1], 1)
+    grad_w_in = add_up([near[0], far])
+    grad_w_out = near[1].astype(F32).T
 
     grad_in = pl.pallas_call(
         final_kernel,
         out_shape=jax.ShapeDtypeStruct((TD, D), BF),
-        in_specs=[VM] * 4,
+        in_specs=[VM] * 4 + [ANY],
         out_specs=VM,
         compiler_params=PARAMS,
         cost_estimate=cost(20 * TD * D, 14 * TD * D),
-    )(inputs, norm_gain, grad_out, dx_y)
+    )(inputs, norm_gain, grad_out, dx_y, sums)
     return grad_in, grad_w_in, grad_w_out
 
 

time: 196 us -> 180 us (0.918)
  waiting for transfers between devices: 60 us -> 48.5 us
  starting transfers between devices: 72.5 us -> 64.5 us
  Pallas kernels: 33.8 us -> 38.2 us
    ppermute x24 -> x23, starting transfers between devices: 38.6 us -> 24.6 us  [shift(): return lax.ppermute(value, axis, [(i, (i + by) % n) for i in range(n)])]
    reduce_scatter x1, waiting for transfers between devices: 7.93 us -> 0.01 us  [on_device(): dwo_z = lax.psum_scatter(dwo, Z, scatter_dimension=0, tiled=False)]
    pallas_call x0 -> x1, Pallas kernels: none -> 7.76 us  [on_device(): pl.pallas_call(dwin_kernel, out_shape=jax.ShapeDtypeStruct((4, 8, RB, FD)...]
    ppermute x24 -> x23, waiting for transfers between devices: 32 us -> 39.5 us  [shift(): return lax.ppermute(value, axis, [(i, (i + by) % n) for i in range(n)])]
    ppermute x5, waiting for transfers between devices: 9.91 us -> 2.89 us  [turn(): return lax.ppermute(value, ('y', 'zh', 'zl'), pairs)]
    ppermute x5, starting transfers between devices: 19.6 us -> 24.7 us  [turn(): return lax.ppermute(value, ('y', 'zh', 'zl'), pairs)]
    all_to_all x1, waiting for transfers between devices: 10.1 us -> 6.13 us  [on_device(): dws = lax.all_to_all(dws, 'x', 0, 0, tiled=True)]
    pallas_call x1, Pallas kernels: 20.1 us -> 16.9 us  [on_device(): pl.pallas_call(main_kernel, out_shape=(jax.ShapeDtypeStruct((1024, FD), B...]
  transfers between devices with their start and end apart: 34 -> 33, of which waited for: 14 -> 17; matrix products, arithmetic and copies ran while one was open for 5% -> 5% of each run, Pallas kernels for 7% -> 12%
where the time goes in v3:
time: 180 us; the launch traced here: 179 us
  starting transfers between devices  64.5 us (36%)
  waiting for transfers between devices  48.5 us (27%)
  Pallas kernels  38.2 us (21%)
  between operations  14.3 us (8%)
  other arithmetic  7.36 us (4%)
  local copies, waits for them, and re-layouts  6.01 us (3%)
    ppermute x23, waiting for transfers between devices, shift(): return lax.ppermute(value, axis, [(i, (i + by) % n) for i in range(n)])  39.5 us
    ppermute x5, starting transfers between devices, turn(): return lax.ppermute(value, ('y', 'zh', 'zl'), pairs)  24.7 us
    ppermute x23, starting transfers between devices, shift(): return lax.ppermute(value, axis, [(i, (i + by) % n) for i in range(n)])  24.6 us
    pallas_call x1, Pallas kernels, on_device(): pl.pallas_call(main_kernel, out_shape=(jax.ShapeDtypeStruct((1024, FD), B...  16.9 us
    pallas_call x1, Pallas kernels, on_device(): pl.pallas_call(dx_kernel, out_shape=[jax.ShapeDtypeStruct((512, D), BF)]...  8 us
    pallas_call x1, Pallas kernels, on_device(): pl.pallas_call(dwin_kernel, out_shape=jax.ShapeDtypeStruct((4, 8, RB, FD)...  7.76 us
    all_to_all x1, starting transfers between devices, on_device(): dx_y = lax.all_to_all(dx_c, 'y', 0, 0, tiled=True).reshape(4, TD, D)  6.4 us
    all_to_all x1, waiting for transfers between devices, on_device(): dws = lax.all_to_all(dws, 'x', 0, 0, tiled=True)  6.13 us
  transfers between devices with their start and end apart: 33, of which 17 were waited for; matrix products, arithmetic and copies ran while one was open for 5% of the time, Pallas kernels for 12%

profile of v3, /device:TPU:16, one launch (start us, length us, event | category | flops | bytes accessed | tf_op | source)
XLA Modules:
  0.0 178.9 jit_solution(17610365542021112555)
XLA Ops:
  7.2 0.9 pad_maximum_fusion.2
  8.1 5.0 %collective-permute-start.1 = (bf16[2,48,768]{2,1,0:T(8,128)(2,1)S(1)}, bf16[2,48,768]{2,1,0:T(8,128)(2,1)S(1)}, u32[]{:S(2)}, u32[]{:S(2)}) collective-permute-start(bf16[2,48,768]{2,1,0:T(8,128)(2,1)S(1)} %pad_maximum_fusion.2), channel_id=1, source_target_pairs={{0,0},{2,64},{4,128},{6,192},{32,32},{34,96},{36,160},{38,224},{64... | collective-permute-start | bytes 442376 | tf_op jit(solution)/shard_map/ppermute | solution.py:39
  13.1 7.2 %collective-permute-start.2 = (bf16[48,768]{1,0:T(8,128)(2,1)}, bf16[48,768]{1,0:T(8,128)(2,1)S(1)}, u32[]{:S(2)}, u32[]{:S(2)}) collective-permute-start(bf16[48,768]{1,0:T(8,128)(2,1)} %param.10), channel_id=1, source_target_pairs={{0,32},{2,96},{4,160},{6,224},{32,0},{34,64},{36,128},{38,192},{64... | collective-permute-start | bytes 221192 | tf_op jit(solution)/shard_map/ppermute | solution.py:39
  20.3 3.1 %collective-permute-start = (f32[768]{0:T(1024)}, f32[768]{0:T(1024)S(1)}, u32[]{:S(2)}, u32[]{:S(2)}) collective-permute-start(f32[768]{0:T(1024)} %param.11), channel_id=1, source_target_pairs={{0,0},{2,64},{4,128},{6,192},{32,32},{34,96},{36,160},{38,224},{64... | collective-permute-start | bytes 9224 | tf_op jit(solution)/shard_map/ppermute | solution.py:39
  24.1 2.4 %shard_map.94 = bf16[2,128,1536]{2,1,0:T(8,128)(2,1)} custom-call(bf16[128,1536]{1,0:T(8,128)(2,1)} %x_ref.3, f32[1536]{0:T(1024)} %gain_ref.3, f32[1536]{0:T(1024)} %bias_ref.1, bf16[128,1536]{1,0:T(8,128)(2,1)} %grad_ref.3), custom_call_target="tpu_custom_call" | custom-call | flops 1966080 | bytes 1572864 | tf_op jit(solution)/shard_map/pallas_call | solution.py:204
  26.5 2.8 %collective-permute-done = f32[768]{0:T(1024)S(1)} collective-permute-done((f32[768]{0:T(1024)}, f32[768]{0:T(1024)S(1)}, u32[]{:S(2)}, u32[]{:S(2)}) %collective-permute-start) | collective-permute-done | bytes 3104 | tf_op jit(solution)/shard_map/ppermute | solution.py:39
  29.4 3.1 %collective-permute-start.5 = (bf16[48,768]{1,0:T(8,128)(2,1)S(1)}, bf16[48,768]{1,0:T(8,128)(2,1)S(1)}, u32[]{:S(2)}, u32[]{:S(2)}) collective-permute-start(bf16[48,768]{1,0:T(8,128)(2,1)S(1)} %get-tuple-element.35), channel_id=1, source_target_pairs={{0,16},{8,24},{16,0},{24,8},{1,17},{9,25},{17,1},{25,9},{2,18},{10... | collective-permute-start | bytes 221192 | tf_op jit(solution)/shard_map/ppermute | solution.py:29
  32.6 2.8 %collective-permute-start.7 = (bf16[2,48,768]{2,1,0:T(8,128)(2,1)S(1)}, bf16[2,48,768]{2,1,0:T(8,128)(2,1)S(1)}, u32[]{:S(2)}, u32[]{:S(2)}) collective-permute-start(bf16[2,48,768]{2,1,0:T(8,128)(2,1)S(1)} %pad_maximum_fusion.3), channel_id=1, source_target_pairs={{0,38},{2,0},{4,2},{6,4},{32,6},{34,32},{36,34},{38,36},{1,39},{3,... | collective-permute-start | bytes 442376 | tf_op jit(solution)/shard_map/ppermute | solution.py:29
  35.4 1.1 collective-permute-start.4
  36.5 0.9 collective-permute-start.3
  37.4 2.3 %collective-permute-done.4 = bf16[48,768]{1,0:T(8,128)(2,1)S(1)} collective-permute-done((bf16[48,768]{1,0:T(8,128)(2,1)S(1)}, bf16[48,768]{1,0:T(8,128)(2,1)S(1)}, u32[]{:S(2)}, u32[]{:S(2)}) %collective-permute-start.4) | collective-permute-done | bytes 73760 | tf_op jit(solution)/shard_map/ppermute | solution.py:29
  39.7 2.4 %collective-permute-done.3 = bf16[48,768]{1,0:T(8,128)(2,1)S(1)} collective-permute-done((bf16[48,768]{1,0:T(8,128)(2,1)S(1)}, bf16[48,768]{1,0:T(8,128)(2,1)S(1)}, u32[]{:S(2)}, u32[]{:S(2)}) %collective-permute-start.3) | collective-permute-done | bytes 73760 | tf_op jit(solution)/shard_map/ppermute | solution.py:29
  42.1 1.2 collective-permute-done.8
  43.3 1.0 collective-permute-done.6
  44.3 1.6 broadcast_in_dim.2
  46.0 3.6 %all-to-all-start = ((bf16[4,8,48,768]{3,2,1,0:T(8,128)(2,1)}), bf16[4,8,48,768]{3,2,1,0:T(8,128)(2,1)S(1)}, u32[]{:S(2)}, u32[]{:S(2)}) async-start(bf16[4,8,48,768]{3,2,1,0:T(8,128)(2,1)} %broadcast_in_dim.2), calls=%async_computation | async-start | bytes 4718592 | tf_op jit(solution)/shard_map/all_to_all | solution.py:224
  49.7 1.2 collective-permute-start.10
  50.9 0.9 collective-permute-start.9
  51.9 6.5 %collective-permute-done.10.refs_4_ = bf16[4,48,768]{2,1,0:T(8,128)(2,1)S(1)} collective-permute-done((bf16[4,48,768]{2,1,0:T(8,128)(2,1)S(1)}, bf16[4,48,768]{2,1,0:T(8,128)(2,1)S(1)}, u32[]{:S(2)}, u32[]{:S(2)}) %collective-permute-start.10) | collective-permute-done | bytes 294944 | tf_op jit(solution)/shard_map/ppermute | solution.py:29
  58.3 1.5 collective-permute-start.12
  60.3 5.6 %collective-permute-done.12.refs_6_ = bf16[4,48,768]{2,1,0:T(8,128)(2,1)S(1)} collective-permute-done((bf16[4,48,768]{2,1,0:T(8,128)(2,1)S(1)}, bf16[4,48,768]{2,1,0:T(8,128)(2,1)S(1)}, u32[]{:S(2)}, u32[]{:S(2)}) %collective-permute-start.12) | collective-permute-done | bytes 294944 | tf_op jit(solution)/shard_map/ppermute | solution.py:29
  66.0 1.8 %collective-permute-start.14 = (bf16[4,48,768]{2,1,0:T(8,128)(2,1)S(1)}, bf16[4,48,768]{2,1,0:T(8,128)(2,1)S(1)}, u32[]{:S(2)}, u32[]{:S(2)}) collective-permute-start(bf16[4,48,768]{2,1,0:T(8,128)(2,1)S(1)} %collective-permute-done.12.refs_6_), channel_id=1, source_target_pairs={{0,38},{2,0},{4,2},{6,4},{32,6},{34,32},{36,34},{38,36},{1,39},{3,... | collective-permute-start | bytes 884744 | tf_op jit(solution)/shard_map/ppermute | solution.py:29
  68.1 5.0 %collective-permute-done.14.refs_8_ = bf16[4,48,768]{2,1,0:T(8,128)(2,1)S(1)} collective-permute-done((bf16[4,48,768]{2,1,0:T(8,128)(2,1)S(1)}, bf16[4,48,768]{2,1,0:T(8,128)(2,1)S(1)}, u32[]{:S(2)}, u32[]{:S(2)}) %collective-permute-start.14) | collective-permute-done | bytes 294944 | tf_op jit(solution)/shard_map/ppermute | solution.py:29
  73.1 2.7 %collective-permute-start.16 = (bf16[2,48,768]{2,1,0:T(8,128)(2,1)S(1)}, bf16[2,48,768]{2,1,0:T(8,128)(2,1)S(1)}, u32[]{:S(2)}, u32[]{:S(2)}) collective-permute-start(bf16[2,48,768]{2,1,0:T(8,128)(2,1)S(1)} %slice.108), channel_id=1, source_target_pairs={{0,38},{2,0},{4,2},{6,4},{32,6},{34,32},{36,34},{38,36},{1,39},{3,... | collective-permute-start | bytes 442376 | tf_op jit(solution)/shard_map/ppermute | solution.py:29
  76.7 1.8 %collective-permute-done.16.refs_10_ = bf16[2,48,768]{2,1,0:T(8,128)(2,1)S(1)} collective-permute-done((bf16[2,48,768]{2,1,0:T(8,128)(2,1)S(1)}, bf16[2,48,768]{2,1,0:T(8,128)(2,1)S(1)}, u32[]{:S(2)}, u32[]{:S(2)}) %collective-permute-start.16) | collective-permute-done | bytes 147488 | tf_op jit(solution)/shard_map/ppermute | solution.py:29
  78.5 4.1 %collective-permute-done.15.refs_9_ = bf16[2,48,768]{2,1,0:T(8,128)(2,1)} collective-permute-done((bf16[2,48,768]{2,1,0:T(8,128)(2,1)S(1)}, bf16[2,48,768]{2,1,0:T(8,128)(2,1)}, u32[]{:S(2)}, u32[]{:S(2)}) %collective-permute-start.15) | collective-permute-done | bytes 147488 | tf_op jit(solution)/shard_map/ppermute | solution.py:29
  82.6 1.4 copy-done
  83.9 16.9 %shard_map.95 = (bf16[1024,768]{1,0:T(8,128)(2,1)}, bf16[8,4,48,768]{3,2,1,0:T(8,128)(2,1)}) custom-call(s32[3]{0:T(128)} %pad_add_fusion.me, bf16[8,2,128,1536]{3,2,1,0:T(8,128)(2,1)} %bitcast.56, bf16[4,8,48,768]{3,2,1,0:T(8,128)(2,1)} %copy-done, bf16[4,48,768]{2,1,0:T(8,128)(2,1)} %copy-done.2, bf16[4,48,768]{2,1,0:T(8,128)(2,1)} %copy-done.6, ...), custom_call_target="tpu_custom_call" | custom-call | flops 7247757312 | bytes 20971520 | tf_op jit(solution)/shard_map/pallas_call | solution.py:233
  100.9 7.8 %shard_map.96 = bf16[4,8,48,768]{3,2,1,0:T(8,128)(2,1)} custom-call(s32[3]{0:T(128)} %pad_add_fusion.me, bf16[8,2,128,1536]{3,2,1,0:T(8,128)(2,1)} %bitcast.57, bf16[1024,768]{1,0:T(8,128)(2,1)} %get-tuple-element.40.refs_1_.refs_0_), custom_call_target="tpu_custom_call" | custom-call | flops 2415919104 | bytes 7340032 | tf_op jit(solution)/shard_map/pallas_call | solution.py:259
  108.7 5.1 %all-to-all-start.2 = ((bf16[4,8,48,768]{3,2,1,0:T(8,128)(2,1)}), bf16[4,8,48,768]{3,2,1,0:T(8,128)(2,1)S(1)}, u32[]{:S(2)}, u32[]{:S(2)}) async-start(bf16[4,8,48,768]{3,2,1,0:T(8,128)(2,1)} %shard_map.96), calls=%async_computation.2 | async-start | bytes 4718592 | tf_op jit(solution)/shard_map/all_to_all | solution.py:274
  114.5 1.2 collective-permute-done.17.refs_2_
  116.3 8.0 %shard_map.97 = (bf16[512,1536]{1,0:T(8,128)(2,1)}, bf16[256,1536]{1,0:T(8,128)(2,1)}, bf16[256,1536]{1,0:T(8,128)(2,1)}) custom-call(s32[3]{0:T(128)} %pad_add_fusion.me, bf16[1024,768]{1,0:T(8,128)(2,1)} %get-tuple-element.40.refs_1_.refs_0_, bf16[4,8,48,768]{3,2,1,0:T(8,128)(2,1)} %copy-done, bf16[16,768]{1,0:T(8,128)(2,1)} %copy-done.10), custom_call_target="tpu_custom_call" | custom-call | flops 2415919104 | bytes 7340032 | tf_op jit(solution)/shard_map/pallas_call | solution.py:276
  124.9 2.0 %collective-permute-done.18 = bf16[256,1536]{1,0:T(8,128)(2,1)S(1)} collective-permute-done((bf16[256,1536]{1,0:T(8,128)(2,1)}, bf16[256,1536]{1,0:T(8,128)(2,1)S(1)}, u32[]{:S(2)}, u32[]{:S(2)}) %collective-permute-start.18) | collective-permute-done | bytes 786464 | tf_op jit(solution)/shard_map/ppermute | solution.py:29
  126.9 1.1 collective-permute-done.19
  128.0 3.0 %add_convert_fusion = bf16[512,1536]{1,0:T(8,128)(2,1)} fusion(bf16[512,1536]{1,0:T(8,128)(2,1)} %get-tuple-element.41, bf16[256,1536]{1,0:T(8,128)(2,1)S(1)} %collective-permute-done.19, bf16[256,1536]{1,0:T(8,128)(2,1)S(1)} %collective-permute-done.18), kind=kLoop, calls=%fused_computation | loop fusion | flops 5505024 | bytes 4718592 | tf_op jit(solution)/shard_map/convert_element_type | solution.py:287
  131.0 6.1 %all-to-all-done.2 = bf16[4,8,48,768]{3,2,1,0:T(8,128)(2,1)S(1)} async-done(((bf16[4,8,48,768]{3,2,1,0:T(8,128)(2,1)}), bf16[4,8,48,768]{3,2,1,0:T(8,128)(2,1)S(1)}, u32[]{:S(2)}, u32[]{:S(2)}) %all-to-all-start.2) | async-done | bytes 2359328 | tf_op jit(solution)/shard_map/all_to_all | solution.py:274
  137.1 6.4 %all-to-all-start.1 = ((bf16[4,128,1536]{2,1,0:T(8,128)(2,1)}), bf16[4,128,1536]{2,1,0:T(8,128)(2,1)}, u32[]{:S(2)}, u32[]{:S(2)}) async-start(bf16[4,128,1536]{2,1,0:T(8,128)(2,1)} %bitcast.58), calls=%async_computation.1 | async-start | bytes 3145728 | tf_op jit(solution)/shard_map/all_to_all | solution.py:288
  144.0 1.8 %collective-permute-start.24 = (bf16[2,48,768]{2,1,0:T(8,128)(2,1)S(1)}, bf16[2,48,768]{2,1,0:T(8,128)(2,1)S(1)}, u32[]{:S(2)}, u32[]{:S(2)}) collective-permute-start(bf16[2,48,768]{2,1,0:T(8,128)(2,1)S(1)} %get-tuple-element.52), channel_id=1, source_target_pairs={{0,38},{2,0},{4,2},{6,4},{32,6},{34,32},{36,34},{38,36},{1,39},{3,... | collective-permute-start | bytes 442376 | tf_op jit(solution)/shard_map/ppermute | solution.py:29
  146.1 1.0 slice_bitcast_fusion.8
  147.0 1.2 collective-permute-start.22
  148.2 2.2 %collective-permute-start.21 = (bf16[48,768]{1,0:T(8,128)(2,1)S(1)}, bf16[48,768]{1,0:T(8,128)(2,1)S(1)}, u32[]{:S(2)}, u32[]{:S(2)}) collective-permute-start(bf16[48,768]{1,0:T(8,128)(2,1)S(1)} %get-tuple-element.55), channel_id=1, source_target_pairs={{0,24},{8,0},{16,8},{24,16},{1,25},{9,1},{17,9},{25,17},{2,26},{10... | collective-permute-start | bytes 221192 | tf_op jit(solution)/shard_map/ppermute | solution.py:29
  150.4 1.1 collective-permute-done.25
  151.5 1.2 collective-permute-start.20
  153.0 4.0 %collective-permute-done.20 = bf16[48,768]{1,0:T(8,128)(2,1)S(1)} collective-permute-done((bf16[48,768]{1,0:T(8,128)(2,1)S(1)}, bf16[48,768]{1,0:T(8,128)(2,1)S(1)}, u32[]{:S(2)}, u32[]{:S(2)}) %collective-permute-start.20) | collective-permute-done | bytes 73760 | tf_op jit(solution)/shard_map/ppermute | solution.py:29
  157.1 0.9 fusion.6
  158.1 1.9 %collective-permute-start.26 = (bf16[2,48,768]{2,1,0:T(8,128)(2,1)S(1)}, bf16[2,48,768]{2,1,0:T(8,128)(2,1)S(1)}, u32[]{:S(2)}, u32[]{:S(2)}) collective-permute-start(bf16[2,48,768]{2,1,0:T(8,128)(2,1)S(1)} %pad_maximum_fusion.4.after_ref), channel_id=1, source_target_pairs={{0,0},{2,64},{4,128},{6,192},{32,32},{34,96},{36,160},{38,224},{64... | collective-permute-start | bytes 442376 | tf_op jit(solution)/shard_map/ppermute | solution.py:39
  160.0 7.5 %collective-permute-start.27 = (bf16[48,768]{1,0:T(8,128)(2,1)S(1)}, bf16[48,768]{1,0:T(8,128)(2,1)S(1)}, u32[]{:S(2)}, u32[]{:S(2)}) collective-permute-start(bf16[48,768]{1,0:T(8,128)(2,1)S(1)} %get-tuple-element.57), channel_id=1, source_target_pairs={{0,32},{2,96},{4,160},{6,224},{32,0},{34,64},{36,128},{38,192},{64... | collective-permute-start | bytes 221192 | tf_op jit(solution)/shard_map/ppermute | solution.py:39
  167.5 3.1 %shard_map.98 = bf16[128,1536]{1,0:T(8,128)(2,1)} custom-call(bf16[128,1536]{1,0:T(8,128)(2,1)} %x_ref.3, f32[1536]{0:T(1024)} %gain_ref.3, bf16[128,1536]{1,0:T(8,128)(2,1)} %grad_ref.3, bf16[4,128,1536]{2,1,0:T(8,128)(2,1)} %all-to-all-done.1.dx_ref, bf16[2,48,768]{2,1,0:T(8,128)(2,1)} %copy-done.1), custom_call_target="tpu_custom_call" | custom-call | flops 3932160 | bytes 2752512 | tf_op jit(solution)/shard_map/pallas_call | solution.py:302
  (68 shorter events, 7.2 us)
Async XLA Ops:
  7.2 75.4 %all-gather.3.cloned.1.call-start = ((), (), s32[]{:S(2)}) async-start(), calls=%async_computation.5 | async-start | bytes 7077888 | tf_op jit(solution)/shard_map/all_gather | solution.py:214
  8.1 21.2 %collective-permute-start.1 = (bf16[2,48,768]{2,1,0:T(8,128)(2,1)S(1)}, bf16[2,48,768]{2,1,0:T(8,128)(2,1)S(1)}, u32[]{:S(2)}, u32[]{:S(2)}) collective-permute-start(bf16[2,48,768]{2,1,0:T(8,128)(2,1)S(1)} %pad_maximum_fusion.2), channel_id=1, source_target_pairs={{0,0},{2,64},{4,128},{6,192},{32,32},{34,96},{36,160},{38,224},{64... | collective-permute-start | bytes 442376 | tf_op jit(solution)/shard_map/ppermute | solution.py:39
  13.1 16.2 %collective-permute-start.2 = (bf16[48,768]{1,0:T(8,128)(2,1)}, bf16[48,768]{1,0:T(8,128)(2,1)S(1)}, u32[]{:S(2)}, u32[]{:S(2)}) collective-permute-start(bf16[48,768]{1,0:T(8,128)(2,1)} %param.10), channel_id=1, source_target_pairs={{0,32},{2,96},{4,160},{6,224},{32,0},{34,64},{36,128},{38,192},{64... | collective-permute-start | bytes 221192 | tf_op jit(solution)/shard_map/ppermute | solution.py:39
  20.3 9.0 %collective-permute-start = (f32[768]{0:T(1024)}, f32[768]{0:T(1024)S(1)}, u32[]{:S(2)}, u32[]{:S(2)}) collective-permute-start(f32[768]{0:T(1024)} %param.11), channel_id=1, source_target_pairs={{0,0},{2,64},{4,128},{6,192},{32,32},{34,96},{36,160},{38,224},{64... | collective-permute-start | bytes 9224 | tf_op jit(solution)/shard_map/ppermute | solution.py:39
  29.4 7.2 %collective-permute-start.5 = (bf16[48,768]{1,0:T(8,128)(2,1)S(1)}, bf16[48,768]{1,0:T(8,128)(2,1)S(1)}, u32[]{:S(2)}, u32[]{:S(2)}) collective-permute-start(bf16[48,768]{1,0:T(8,128)(2,1)S(1)} %get-tuple-element.35), channel_id=1, source_target_pairs={{0,16},{8,24},{16,0},{24,8},{1,17},{9,25},{17,1},{25,9},{2,18},{10... | collective-permute-start | bytes 221192 | tf_op jit(solution)/shard_map/ppermute | solution.py:29
  32.5 10.8 %collective-permute-start.8 = (bf16[2,48,768]{2,1,0:T(8,128)(2,1)S(1)}, bf16[2,48,768]{2,1,0:T(8,128)(2,1)S(1)}, u32[]{:S(2)}, u32[]{:S(2)}) collective-permute-start(bf16[2,48,768]{2,1,0:T(8,128)(2,1)S(1)} %pad_maximum_fusion.3), channel_id=1, source_target_pairs={{0,4},{2,6},{4,32},{6,34},{32,36},{34,38},{36,0},{38,2},{1,5},{3,7... | collective-permute-start | bytes 442376 | tf_op jit(solution)/shard_map/ppermute | solution.py:29
  32.6 10.7 %collective-permute-start.7 = (bf16[2,48,768]{2,1,0:T(8,128)(2,1)S(1)}, bf16[2,48,768]{2,1,0:T(8,128)(2,1)S(1)}, u32[]{:S(2)}, u32[]{:S(2)}) collective-permute-start(bf16[2,48,768]{2,1,0:T(8,128)(2,1)S(1)} %pad_maximum_fusion.3), channel_id=1, source_target_pairs={{0,38},{2,0},{4,2},{6,4},{32,6},{34,32},{36,34},{38,36},{1,39},{3,... | collective-permute-start | bytes 442376 | tf_op jit(solution)/shard_map/ppermute | solution.py:29
  35.4 8.9 %collective-permute-start.6 = (bf16[2,48,768]{2,1,0:T(8,128)(2,1)S(1)}, bf16[2,48,768]{2,1,0:T(8,128)(2,1)S(1)}, u32[]{:S(2)}, u32[]{:S(2)}) collective-permute-start(bf16[2,48,768]{2,1,0:T(8,128)(2,1)S(1)} %pad_maximum_fusion.3), channel_id=1, source_target_pairs={{0,2},{2,4},{4,6},{6,32},{32,34},{34,36},{36,38},{38,0},{1,3},{3,5... | collective-permute-start | bytes 442376 | tf_op jit(solution)/shard_map/ppermute | solution.py:29
  35.4 4.4 %collective-permute-start.4 = (bf16[48,768]{1,0:T(8,128)(2,1)S(1)}, bf16[48,768]{1,0:T(8,128)(2,1)S(1)}, u32[]{:S(2)}, u32[]{:S(2)}) collective-permute-start(bf16[48,768]{1,0:T(8,128)(2,1)S(1)} %get-tuple-element.35), channel_id=1, source_target_pairs={{0,24},{8,0},{16,8},{24,16},{1,25},{9,1},{17,9},{25,17},{2,26},{10... | collective-permute-start | bytes 221192 | tf_op jit(solution)/shard_map/ppermute | solution.py:29
  36.5 5.6 %collective-permute-start.3 = (bf16[48,768]{1,0:T(8,128)(2,1)S(1)}, bf16[48,768]{1,0:T(8,128)(2,1)S(1)}, u32[]{:S(2)}, u32[]{:S(2)}) collective-permute-start(bf16[48,768]{1,0:T(8,128)(2,1)S(1)} %get-tuple-element.35), channel_id=1, source_target_pairs={{0,8},{8,16},{16,24},{24,0},{1,9},{9,17},{17,25},{25,1},{2,10},{10... | collective-permute-start | bytes 221192 | tf_op jit(solution)/shard_map/ppermute | solution.py:29
  46.0 36.5 %all-to-all-start = ((bf16[4,8,48,768]{3,2,1,0:T(8,128)(2,1)}), bf16[4,8,48,768]{3,2,1,0:T(8,128)(2,1)S(1)}, u32[]{:S(2)}, u32[]{:S(2)}) async-start(bf16[4,8,48,768]{3,2,1,0:T(8,128)(2,1)} %broadcast_in_dim.2), calls=%async_computation | async-start | bytes 4718592 | tf_op jit(solution)/shard_map/all_to_all | solution.py:224
  49.6 96.4 %reduce-scatter.2.cloned.1.call-start = ((), (), s32[]{:S(2)}) async-start(), calls=%async_computation.4 | async-start | bytes 2654208 | tf_op jit(solution)/shard_map/reduce_scatter | solution.py:257
  49.7 32.8 %copy-start.2 = (bf16[4,48,768]{2,1,0:T(8,128)(2,1)}, bf16[4,48,768]{2,1,0:T(8,128)(2,1)S(1)}, u32[]{:S(2)}) copy-start(bf16[4,48,768]{2,1,0:T(8,128)(2,1)S(1)} %pad_maximum_fusion.1.refs_2_) | copy-start | bytes 884740
  49.7 8.6 %collective-permute-start.10 = (bf16[4,48,768]{2,1,0:T(8,128)(2,1)S(1)}, bf16[4,48,768]{2,1,0:T(8,128)(2,1)S(1)}, u32[]{:S(2)}, u32[]{:S(2)}) collective-permute-start(bf16[4,48,768]{2,1,0:T(8,128)(2,1)S(1)} %pad_maximum_fusion.1.refs_2_), channel_id=1, source_target_pairs={{0,38},{2,0},{4,2},{6,4},{32,6},{34,32},{36,34},{38,36},{1,39},{3,... | collective-permute-start | bytes 884744 | tf_op jit(solution)/shard_map/ppermute | solution.py:29
  50.9 8.9 %collective-permute-start.9 = (bf16[4,48,768]{2,1,0:T(8,128)(2,1)S(1)}, bf16[4,48,768]{2,1,0:T(8,128)(2,1)S(1)}, u32[]{:S(2)}, u32[]{:S(2)}) collective-permute-start(bf16[4,48,768]{2,1,0:T(8,128)(2,1)S(1)} %pad_maximum_fusion.1.refs_2_), channel_id=1, source_target_pairs={{0,2},{2,4},{4,6},{6,32},{32,34},{34,36},{36,38},{38,0},{1,3},{3,5... | collective-permute-start | bytes 884744 | tf_op jit(solution)/shard_map/ppermute | solution.py:29
  58.3 2.0 %copy-start.5 = (bf16[4,48,768]{2,1,0:T(8,128)(2,1)}, bf16[4,48,768]{2,1,0:T(8,128)(2,1)S(1)}, u32[]{:S(2)}) copy-start(bf16[4,48,768]{2,1,0:T(8,128)(2,1)S(1)} %collective-permute-done.10.refs_4_) | copy-start | bytes 884740
  58.3 7.7 %collective-permute-start.12 = (bf16[4,48,768]{2,1,0:T(8,128)(2,1)S(1)}, bf16[4,48,768]{2,1,0:T(8,128)(2,1)S(1)}, u32[]{:S(2)}, u32[]{:S(2)}) collective-permute-start(bf16[4,48,768]{2,1,0:T(8,128)(2,1)S(1)} %collective-permute-done.10.refs_4_), channel_id=1, source_target_pairs={{0,38},{2,0},{4,2},{6,4},{32,6},{34,32},{36,34},{38,36},{1,39},{3,... | collective-permute-start | bytes 884744 | tf_op jit(solution)/shard_map/ppermute | solution.py:29
  59.8 8.0 %copy-start.6 = (bf16[4,48,768]{2,1,0:T(8,128)(2,1)}, bf16[4,48,768]{2,1,0:T(8,128)(2,1)S(1)}, u32[]{:S(2)}) copy-start(bf16[4,48,768]{2,1,0:T(8,128)(2,1)S(1)} %collective-permute-done.9.refs_3_) | copy-start | bytes 884740
  59.8 8.0 %collective-permute-start.11 = (bf16[4,48,768]{2,1,0:T(8,128)(2,1)S(1)}, bf16[4,48,768]{2,1,0:T(8,128)(2,1)S(1)}, u32[]{:S(2)}, u32[]{:S(2)}) collective-permute-start(bf16[4,48,768]{2,1,0:T(8,128)(2,1)S(1)} %collective-permute-done.9.refs_3_), channel_id=1, source_target_pairs={{0,2},{2,4},{4,6},{6,32},{32,34},{34,36},{36,38},{38,0},{1,3},{3,5... | collective-permute-start | bytes 884744 | tf_op jit(solution)/shard_map/ppermute | solution.py:29
  66.0 2.1 %copy-start.7 = (bf16[4,48,768]{2,1,0:T(8,128)(2,1)}, bf16[4,48,768]{2,1,0:T(8,128)(2,1)S(1)}, u32[]{:S(2)}) copy-start(bf16[4,48,768]{2,1,0:T(8,128)(2,1)S(1)} %collective-permute-done.12.refs_6_) | copy-start | bytes 884740
  66.0 7.1 %collective-permute-start.14 = (bf16[4,48,768]{2,1,0:T(8,128)(2,1)S(1)}, bf16[4,48,768]{2,1,0:T(8,128)(2,1)S(1)}, u32[]{:S(2)}, u32[]{:S(2)}) collective-permute-start(bf16[4,48,768]{2,1,0:T(8,128)(2,1)S(1)} %collective-permute-done.12.refs_6_), channel_id=1, source_target_pairs={{0,38},{2,0},{4,2},{6,4},{32,6},{34,32},{36,34},{38,36},{1,39},{3,... | collective-permute-start | bytes 884744 | tf_op jit(solution)/shard_map/ppermute | solution.py:29
  67.8 8.0 %copy-start.8 = (bf16[4,48,768]{2,1,0:T(8,128)(2,1)}, bf16[4,48,768]{2,1,0:T(8,128)(2,1)S(1)}, u32[]{:S(2)}) copy-start(bf16[4,48,768]{2,1,0:T(8,128)(2,1)S(1)} %collective-permute-done.11.refs_5_) | copy-start | bytes 884740
  67.8 8.0 %collective-permute-start.13 = (bf16[4,48,768]{2,1,0:T(8,128)(2,1)S(1)}, bf16[4,48,768]{2,1,0:T(8,128)(2,1)S(1)}, u32[]{:S(2)}, u32[]{:S(2)}) collective-permute-start(bf16[4,48,768]{2,1,0:T(8,128)(2,1)S(1)} %collective-permute-done.11.refs_5_), channel_id=1, source_target_pairs={{0,2},{2,4},{4,6},{6,32},{32,34},{34,36},{36,38},{38,0},{1,3},{3,5... | collective-permute-start | bytes 884744 | tf_op jit(solution)/shard_map/ppermute | solution.py:29
  73.1 9.5 %copy-start.3 = (bf16[4,48,768]{2,1,0:T(8,128)(2,1)}, bf16[4,48,768]{2,1,0:T(8,128)(2,1)S(1)}, u32[]{:S(2)}) copy-start(bf16[4,48,768]{2,1,0:T(8,128)(2,1)S(1)} %collective-permute-done.14.refs_8_) | copy-start | bytes 884740
  73.1 5.4 %collective-permute-start.16 = (bf16[2,48,768]{2,1,0:T(8,128)(2,1)S(1)}, bf16[2,48,768]{2,1,0:T(8,128)(2,1)S(1)}, u32[]{:S(2)}, u32[]{:S(2)}) collective-permute-start(bf16[2,48,768]{2,1,0:T(8,128)(2,1)S(1)} %slice.108), channel_id=1, source_target_pairs={{0,38},{2,0},{4,2},{6,4},{32,6},{34,32},{36,34},{38,36},{1,39},{3,... | collective-permute-start | bytes 442376 | tf_op jit(solution)/shard_map/ppermute | solution.py:29
  75.8 6.8 %copy-start.4 = (bf16[4,48,768]{2,1,0:T(8,128)(2,1)}, bf16[4,48,768]{2,1,0:T(8,128)(2,1)S(1)}, u32[]{:S(2)}) copy-start(bf16[4,48,768]{2,1,0:T(8,128)(2,1)S(1)} %collective-permute-done.13.refs_7_) | copy-start | bytes 884740
  75.8 6.7 %collective-permute-start.15 = (bf16[2,48,768]{2,1,0:T(8,128)(2,1)S(1)}, bf16[2,48,768]{2,1,0:T(8,128)(2,1)}, u32[]{:S(2)}, u32[]{:S(2)}) collective-permute-start(bf16[2,48,768]{2,1,0:T(8,128)(2,1)S(1)} %slice.107), channel_id=1, source_target_pairs={{0,2},{2,4},{4,6},{6,32},{32,34},{34,36},{36,38},{38,0},{1,3},{3,5... | collective-permute-start | bytes 442376 | tf_op jit(solution)/shard_map/ppermute | solution.py:29
  78.5 4.1 %copy-start.9 = (bf16[2,48,768]{2,1,0:T(8,128)(2,1)}, bf16[2,48,768]{2,1,0:T(8,128)(2,1)S(1)}, u32[]{:S(2)}) copy-start(bf16[2,48,768]{2,1,0:T(8,128)(2,1)S(1)} %collective-permute-done.16.refs_10_) | copy-start | bytes 442372
  82.5 1.4 copy-start
  108.7 28.5 %all-to-all-start.2 = ((bf16[4,8,48,768]{3,2,1,0:T(8,128)(2,1)}), bf16[4,8,48,768]{3,2,1,0:T(8,128)(2,1)S(1)}, u32[]{:S(2)}, u32[]{:S(2)}) async-start(bf16[4,8,48,768]{3,2,1,0:T(8,128)(2,1)} %shard_map.96), calls=%async_computation.2 | async-start | bytes 4718592 | tf_op jit(solution)/shard_map/all_to_all | solution.py:274
  114.5 1.2 collective-permute-start.17
  115.7 0.6 copy-start.10
  124.3 2.6 %collective-permute-start.18 = (bf16[256,1536]{1,0:T(8,128)(2,1)}, bf16[256,1536]{1,0:T(8,128)(2,1)S(1)}, u32[]{:S(2)}, u32[]{:S(2)}) collective-permute-start(bf16[256,1536]{1,0:T(8,128)(2,1)} %get-tuple-element.42), channel_id=1, source_target_pairs={{0,1},{1,0},{2,3},{3,2},{4,5},{5,4},{6,7},{7,6},{8,9},{9,8},{10,11... | collective-permute-start | bytes 2359304 | tf_op jit(solution)/shard_map/ppermute | solution.py:29
  124.6 3.4 %collective-permute-start.19 = (bf16[256,1536]{1,0:T(8,128)(2,1)}, bf16[256,1536]{1,0:T(8,128)(2,1)S(1)}, u32[]{:S(2)}, u32[]{:S(2)}) collective-permute-start(bf16[256,1536]{1,0:T(8,128)(2,1)} %get-tuple-element.43), channel_id=1, source_target_pairs={{0,1},{1,0},{2,3},{3,2},{4,5},{5,4},{6,7},{7,6},{8,9},{9,8},{10,11... | collective-permute-start | bytes 2359304 | tf_op jit(solution)/shard_map/ppermute | solution.py:29
  137.1 30.4 %all-to-all-start.1 = ((bf16[4,128,1536]{2,1,0:T(8,128)(2,1)}), bf16[4,128,1536]{2,1,0:T(8,128)(2,1)}, u32[]{:S(2)}, u32[]{:S(2)}) async-start(bf16[4,128,1536]{2,1,0:T(8,128)(2,1)} %bitcast.58), calls=%async_computation.1 | async-start | bytes 3145728 | tf_op jit(solution)/shard_map/all_to_all | solution.py:288
  143.9 7.6 %collective-permute-start.25 = (bf16[2,48,768]{2,1,0:T(8,128)(2,1)S(1)}, bf16[2,48,768]{2,1,0:T(8,128)(2,1)S(1)}, u32[]{:S(2)}, u32[]{:S(2)}) collective-permute-start(bf16[2,48,768]{2,1,0:T(8,128)(2,1)S(1)} %get-tuple-element.51), channel_id=1, source_target_pairs={{0,4},{2,6},{4,32},{6,34},{32,36},{34,38},{36,0},{38,2},{1,5},{3,7... | collective-permute-start | bytes 442376 | tf_op jit(solution)/shard_map/ppermute | solution.py:29
  144.0 8.7 %collective-permute-start.24 = (bf16[2,48,768]{2,1,0:T(8,128)(2,1)S(1)}, bf16[2,48,768]{2,1,0:T(8,128)(2,1)S(1)}, u32[]{:S(2)}, u32[]{:S(2)}) collective-permute-start(bf16[2,48,768]{2,1,0:T(8,128)(2,1)S(1)} %get-tuple-element.52), channel_id=1, source_target_pairs={{0,38},{2,0},{4,2},{6,4},{32,6},{34,32},{36,34},{38,36},{1,39},{3,... | collective-permute-start | bytes 442376 | tf_op jit(solution)/shard_map/ppermute | solution.py:29
  145.8 7.2 %collective-permute-start.23 = (bf16[2,48,768]{2,1,0:T(8,128)(2,1)S(1)}, bf16[2,48,768]{2,1,0:T(8,128)(2,1)S(1)}, u32[]{:S(2)}, u32[]{:S(2)}) collective-permute-start(bf16[2,48,768]{2,1,0:T(8,128)(2,1)S(1)} %get-tuple-element.53), channel_id=1, source_target_pairs={{0,2},{2,4},{4,6},{6,32},{32,34},{34,36},{36,38},{38,0},{1,3},{3,5... | collective-permute-start | bytes 442376 | tf_op jit(solution)/shard_map/ppermute | solution.py:29
  147.0 5.9 %collective-permute-start.22 = (bf16[48,768]{1,0:T(8,128)(2,1)S(1)}, bf16[48,768]{1,0:T(8,128)(2,1)S(1)}, u32[]{:S(2)}, u32[]{:S(2)}) collective-permute-start(bf16[48,768]{1,0:T(8,128)(2,1)S(1)} %get-tuple-element.54), channel_id=1, source_target_pairs={{0,16},{8,24},{16,0},{24,8},{1,17},{9,25},{17,1},{25,9},{2,18},{10... | collective-permute-start | bytes 221192 | tf_op jit(solution)/shard_map/ppermute | solution.py:29
  148.2 4.8 %collective-permute-start.21 = (bf16[48,768]{1,0:T(8,128)(2,1)S(1)}, bf16[48,768]{1,0:T(8,128)(2,1)S(1)}, u32[]{:S(2)}, u32[]{:S(2)}) collective-permute-start(bf16[48,768]{1,0:T(8,128)(2,1)S(1)} %get-tuple-element.55), channel_id=1, source_target_pairs={{0,24},{8,0},{16,8},{24,16},{1,25},{9,1},{17,9},{25,17},{2,26},{10... | collective-permute-start | bytes 221192 | tf_op jit(solution)/shard_map/ppermute | solution.py:29
  151.5 5.6 %collective-permute-start.20 = (bf16[48,768]{1,0:T(8,128)(2,1)S(1)}, bf16[48,768]{1,0:T(8,128)(2,1)S(1)}, u32[]{:S(2)}, u32[]{:S(2)}) collective-permute-start(bf16[48,768]{1,0:T(8,128)(2,1)S(1)} %get-tuple-element.56), channel_id=1, source_target_pairs={{0,8},{8,16},{16,24},{24,0},{1,9},{9,17},{17,25},{25,1},{2,10},{10... | collective-permute-start | bytes 221192 | tf_op jit(solution)/shard_map/ppermute | solution.py:29
  158.1 9.4 %copy-start.1 = (bf16[2,48,768]{2,1,0:T(8,128)(2,1)}, bf16[2,48,768]{2,1,0:T(8,128)(2,1)S(1)}, u32[]{:S(2)}) copy-start(bf16[2,48,768]{2,1,0:T(8,128)(2,1)S(1)} %pad_maximum_fusion.4.after_ref) | copy-start | bytes 442372
  158.1 12.6 %collective-permute-start.26 = (bf16[2,48,768]{2,1,0:T(8,128)(2,1)S(1)}, bf16[2,48,768]{2,1,0:T(8,128)(2,1)S(1)}, u32[]{:S(2)}, u32[]{:S(2)}) collective-permute-start(bf16[2,48,768]{2,1,0:T(8,128)(2,1)S(1)} %pad_maximum_fusion.4.after_ref), channel_id=1, source_target_pairs={{0,0},{2,64},{4,128},{6,192},{32,32},{34,96},{36,160},{38,224},{64... | collective-permute-start | bytes 442376 | tf_op jit(solution)/shard_map/ppermute | solution.py:39
  160.0 11.4 %collective-permute-start.27 = (bf16[48,768]{1,0:T(8,128)(2,1)S(1)}, bf16[48,768]{1,0:T(8,128)(2,1)S(1)}, u32[]{:S(2)}, u32[]{:S(2)}) collective-permute-start(bf16[48,768]{1,0:T(8,128)(2,1)S(1)} %get-tuple-element.57), channel_id=1, source_target_pairs={{0,32},{2,96},{4,160},{6,224},{32,0},{34,64},{36,128},{38,192},{64... | collective-permute-start | bytes 221192 | tf_op jit(solution)/shard_map/ppermute | solution.py:39
Sparse Core Ops, SparseCore 0:
  29.5 40.5 all-gather.2
  101.0 43.3 reduce-scatter.1

commit v4 on v3

--- a/solution.py
+++ b/solution.py
@@ -91,30 +91,25 @@
     for copy in n_copies + i_copies + g_copies + o_copies:
         copy.wait()
 
-    def hidden(j, carry):
-        cols = pl.ds(pl.multiple_of(j * 256, 256), 256)
-        pre = jnp.dot(n_s[...], win_s[:, cols], preferred_element_type=F32) + bias_ref[:, cols]
-        ga = 0.5 * jnp.dot(g_s[...], wo_s[:, cols], preferred_element_type=F32)
-        s = jax.nn.sigmoid(pre)
-        act_s[:, cols] = (pre * s).astype(BF)
-        gp_ref[:, cols] = (ga * s * (1.0 + pre * (1.0 - s))).astype(BF)
-        return carry
-
-    lax.fori_loop(0, 3, hidden, 0)
+    pre = jnp.dot(n_s[...], win_s[...], preferred_element_type=F32) + bias_ref[...]
+    ga = 0.5 * jnp.dot(g_s[...], wo_s[...], preferred_element_type=F32)
+    s = jax.nn.sigmoid(pre)
+    act_s[...] = (pre * s).astype(BF)
+    gp_ref[...] = (ga * s * (1.0 + pre * (1.0 - s))).astype(BF)
     dims = (((0,), (0,)), ((), ()))
 
-    def out_grad(zl, carry):
-        rows = pl.ds(pl.multiple_of(zl * 384, 384), 384)
+    def out_grad(half, carry):
+        rows = pl.ds(pl.multiple_of(half * 768, 768), 768)
         dwo = lax.dot_general(g_s[:, rows], act_s[...], dims, preferred_element_type=F32)
         dwo_s[rows, :] = (0.5 * dwo).astype(BF)
-        for zh in range(2):
+        for zl, zh in ((half * 2, 0), (half * 2, 1), (half * 2 + 1, 0), (half * 2 + 1, 1)):
             for i, xs in enumerate(X_STEPS):
                 src = rows_at(dwo_s, zh * 4 + zl, (me[0] + xs + 4) % 4)
                 dst = dwo_ref.at[zh * 4 + zl, i]
                 pltpu.make_async_copy(src, dst, sem_o.at[zl * 8 + zh * 4 + i]).start()
         return carry
 
-    lax.fori_loop(0, 4, out_grad, 0)
+    lax.fori_loop(0, 2, out_grad, 0)
     for k in range(32):
         pltpu.make_async_copy(dwo_s.at[pl.ds(0, RB)], dwo_ref.at[0, 0], sem_o.at[k]).wait()
 
@@ -127,12 +122,12 @@
     for copy in copies:
         copy.wait()
 
-    def in_grad(zl, carry):
-        rows = pl.ds(pl.multiple_of(zl * 384, 384), 384)
+    def in_grad(half, carry):
+        rows = pl.ds(pl.multiple_of(half * 768, 768), 768)
         dims = (((0,), (0,)), ((), ()))
         dwin = lax.dot_general(n_s[:, rows], gp_ref[...], dims, preferred_element_type=F32)
         dwin_s[rows, :] = dwin.astype(BF)
-        for zh in range(2):
+        for zl, zh in ((half * 2, 0), (half * 2, 1), (half * 2 + 1, 0), (half * 2 + 1, 1)):
             away = (zh * 4 + zl - me[1] + 8) % 8
             quarter = away % 4
             place = 2 * (quarter ^ (quarter // 2)) + ((away + 1) // 4) % 2
@@ -142,7 +137,7 @@
                 pltpu.make_async_copy(src, dst, sem_i.at[zl * 8 + zh * 4 + x]).start()
         return carry
 
-    lax.fori_loop(0, 4, in_grad, 0)
+    lax.fori_loop(0, 2, in_grad, 0)
     for k in range(32):
         pltpu.make_async_copy(dwin_s.at[pl.ds(0, RB)], dwin_ref.at[0, 0], sem_i.at[k]).wait()
 
@@ -157,7 +152,7 @@
         copy.wait()
 
     def step(j, carry):
-        cols = pl.ds(pl.multiple_of(j * 512, 512), 512)
+        cols = pl.ds(pl.multiple_of(j * 768, 768), 768)
         dx = lax.dot_general(
             gp_ref[...], win_s[cols, :], (((1,), (1,)), ((), ())), preferred_element_type=F32
         ).astype(BF)
@@ -166,7 +161,7 @@
             outs[1 + i][:, cols] = dx[512 + 256 * i : 512 + 256 * (i + 1)]
         return carry
 
-    lax.fori_loop(0, 3, step, 0)
+    lax.fori_loop(0, 2, step, 0)
 
 
 def final_kernel(x_ref, gain_ref, grad_ref, dx_ref, after_ref, out_ref):
@@ -270,7 +265,7 @@
         compiler_params=PARAMS,
         cost_estimate=cost(mm, 7 << 20),
     )(me, toks, gp)
-    note = shift(dws[0, 0, :16], "c", 1)
+    note = dws
     dws = lax.all_to_all(dws, "x", 0, 0, tiled=True)
 
     dx_own, *dx_other = pl.pallas_call(

time: 180 us -> 179 us (level)
    all_to_all x1, waiting for transfers between devices: 6.13 us -> 8.89 us  [on_device(): dws = lax.all_to_all(dws, 'x', 0, 0, tiled=True)]
    ppermute x23 -> x22, waiting for transfers between devices: 39.5 us -> 38.1 us  [shift(): return lax.ppermute(value, axis, [(i, (i + by) % n) for i in range(n)])]
    ppermute x23 -> x22, starting transfers between devices: 24.6 us -> 24.8 us  [shift(): return lax.ppermute(value, axis, [(i, (i + by) % n) for i in range(n)])]
  transfers between devices with their start and end apart: 33 -> 32, of which waited for: 17 -> 18; matrix products, arithmetic and copies ran while one was open for 5% -> 5% of each run, Pallas kernels for 12% -> 12%
where the time goes in v4:
time: 179 us; the launch traced here: 178 us
  starting transfers between devices  64.4 us (36%)
  waiting for transfers between devices  50.3 us (28%)
  Pallas kernels  37 us (21%)
  between operations  14.3 us (8%)
  other arithmetic  7.35 us (4%)
  local copies, waits for them, and re-layouts  4.67 us (3%)
    ppermute x22, waiting for transfers between devices, shift(): return lax.ppermute(value, axis, [(i, (i + by) % n) for i in range(n)])  38.1 us
    ppermute x22, starting transfers between devices, shift(): return lax.ppermute(value, axis, [(i, (i + by) % n) for i in range(n)])  24.8 us
    ppermute x5, starting transfers between devices, turn(): return lax.ppermute(value, ('y', 'zh', 'zl'), pairs)  24.3 us
    pallas_call x1, Pallas kernels, on_device(): pl.pallas_call(main_kernel, out_shape=(jax.ShapeDtypeStruct((1024, FD), B...  16.2 us
    all_to_all x1, waiting for transfers between devices, on_device(): dws = lax.all_to_all(dws, 'x', 0, 0, tiled=True)  8.89 us
    pallas_call x1, Pallas kernels, on_device(): pl.pallas_call(dx_kernel, out_shape=[jax.ShapeDtypeStruct((512, D), BF)]...  7.78 us
    pallas_call x1, Pallas kernels, on_device(): pl.pallas_call(dwin_kernel, out_shape=jax.ShapeDtypeStruct((4, 8, RB, FD)...  7.55 us
    all_to_all x1, starting transfers between devices, on_device(): dx_y = lax.all_to_all(dx_c, 'y', 0, 0, tiled=True).reshape(4, TD, D)  6.42 us
  transfers between devices with their start and end apart: 32, of which 18 were waited for; matrix products, arithmetic and copies ran while one was open for 5% of the time, Pallas kernels for 12%

profile of v4, /device:TPU:16, one launch (start us, length us, event | category | flops | bytes accessed | tf_op | source)
XLA Modules:
  0.0 177.9 jit_solution(1037413037488840079)
XLA Ops:
  7.2 0.9 pad_maximum_fusion.2
  8.1 5.0 %collective-permute-start.1 = (bf16[2,48,768]{2,1,0:T(8,128)(2,1)S(1)}, bf16[2,48,768]{2,1,0:T(8,128)(2,1)S(1)}, u32[]{:S(2)}, u32[]{:S(2)}) collective-permute-start(bf16[2,48,768]{2,1,0:T(8,128)(2,1)S(1)} %pad_maximum_fusion.2), channel_id=1, source_target_pairs={{0,0},{2,64},{4,128},{6,192},{32,32},{34,96},{36,160},{38,224},{64... | collective-permute-start | bytes 442376 | tf_op jit(solution)/shard_map/ppermute | solution.py:39
  13.1 7.2 %collective-permute-start.2 = (bf16[48,768]{1,0:T(8,128)(2,1)}, bf16[48,768]{1,0:T(8,128)(2,1)S(1)}, u32[]{:S(2)}, u32[]{:S(2)}) collective-permute-start(bf16[48,768]{1,0:T(8,128)(2,1)} %param.10), channel_id=1, source_target_pairs={{0,32},{2,96},{4,160},{6,224},{32,0},{34,64},{36,128},{38,192},{64... | collective-permute-start | bytes 221192 | tf_op jit(solution)/shard_map/ppermute | solution.py:39
  20.3 3.1 %collective-permute-start = (f32[768]{0:T(1024)}, f32[768]{0:T(1024)S(1)}, u32[]{:S(2)}, u32[]{:S(2)}) collective-permute-start(f32[768]{0:T(1024)} %param.11), channel_id=1, source_target_pairs={{0,0},{2,64},{4,128},{6,192},{32,32},{34,96},{36,160},{38,224},{64... | collective-permute-start | bytes 9224 | tf_op jit(solution)/shard_map/ppermute | solution.py:39
  24.1 2.3 %shard_map.94 = bf16[2,128,1536]{2,1,0:T(8,128)(2,1)} custom-call(bf16[128,1536]{1,0:T(8,128)(2,1)} %x_ref.3, f32[1536]{0:T(1024)} %gain_ref.3, f32[1536]{0:T(1024)} %bias_ref.1, bf16[128,1536]{1,0:T(8,128)(2,1)} %grad_ref.3), custom_call_target="tpu_custom_call" | custom-call | flops 1966080 | bytes 1572864 | tf_op jit(solution)/shard_map/pallas_call | solution.py:199
  26.5 2.9 %collective-permute-done = f32[768]{0:T(1024)S(1)} collective-permute-done((f32[768]{0:T(1024)}, f32[768]{0:T(1024)S(1)}, u32[]{:S(2)}, u32[]{:S(2)}) %collective-permute-start) | collective-permute-done | bytes 3104 | tf_op jit(solution)/shard_map/ppermute | solution.py:39
  29.4 3.1 %collective-permute-start.5 = (bf16[48,768]{1,0:T(8,128)(2,1)S(1)}, bf16[48,768]{1,0:T(8,128)(2,1)S(1)}, u32[]{:S(2)}, u32[]{:S(2)}) collective-permute-start(bf16[48,768]{1,0:T(8,128)(2,1)S(1)} %get-tuple-element.35), channel_id=1, source_target_pairs={{0,16},{8,24},{16,0},{24,8},{1,17},{9,25},{17,1},{25,9},{2,18},{10... | collective-permute-start | bytes 221192 | tf_op jit(solution)/shard_map/ppermute | solution.py:29
  32.6 2.8 %collective-permute-start.7 = (bf16[2,48,768]{2,1,0:T(8,128)(2,1)S(1)}, bf16[2,48,768]{2,1,0:T(8,128)(2,1)S(1)}, u32[]{:S(2)}, u32[]{:S(2)}) collective-permute-start(bf16[2,48,768]{2,1,0:T(8,128)(2,1)S(1)} %pad_maximum_fusion.3), channel_id=1, source_target_pairs={{0,38},{2,0},{4,2},{6,4},{32,6},{34,32},{36,34},{38,36},{1,39},{3,... | collective-permute-start | bytes 442376 | tf_op jit(solution)/shard_map/ppermute | solution.py:29
  35.4 1.1 collective-permute-start.4
  36.5 0.9 collective-permute-start.3
  37.4 2.3 %collective-permute-done.4 = bf16[48,768]{1,0:T(8,128)(2,1)S(1)} collective-permute-done((bf16[48,768]{1,0:T(8,128)(2,1)S(1)}, bf16[48,768]{1,0:T(8,128)(2,1)S(1)}, u32[]{:S(2)}, u32[]{:S(2)}) %collective-permute-start.4) | collective-permute-done | bytes 73760 | tf_op jit(solution)/shard_map/ppermute | solution.py:29
  39.7 2.4 %collective-permute-done.3 = bf16[48,768]{1,0:T(8,128)(2,1)S(1)} collective-permute-done((bf16[48,768]{1,0:T(8,128)(2,1)S(1)}, bf16[48,768]{1,0:T(8,128)(2,1)S(1)}, u32[]{:S(2)}, u32[]{:S(2)}) %collective-permute-start.3) | collective-permute-done | bytes 73760 | tf_op jit(solution)/shard_map/ppermute | solution.py:29
  42.1 1.2 collective-permute-done.8
  43.3 1.0 collective-permute-done.6
  44.3 1.7 broadcast_in_dim.2
  46.0 3.6 %all-to-all-start = ((bf16[4,8,48,768]{3,2,1,0:T(8,128)(2,1)}), bf16[4,8,48,768]{3,2,1,0:T(8,128)(2,1)S(1)}, u32[]{:S(2)}, u32[]{:S(2)}) async-start(bf16[4,8,48,768]{3,2,1,0:T(8,128)(2,1)} %broadcast_in_dim.2), calls=%async_computation | async-start | bytes 4718592 | tf_op jit(solution)/shard_map/all_to_all | solution.py:219
  49.7 1.2 collective-permute-start.10
  50.9 0.9 collective-permute-start.9
  51.9 6.5 %collective-permute-done.10.refs_4_ = bf16[4,48,768]{2,1,0:T(8,128)(2,1)S(1)} collective-permute-done((bf16[4,48,768]{2,1,0:T(8,128)(2,1)S(1)}, bf16[4,48,768]{2,1,0:T(8,128)(2,1)S(1)}, u32[]{:S(2)}, u32[]{:S(2)}) %collective-permute-start.10) | collective-permute-done | bytes 294944 | tf_op jit(solution)/shard_map/ppermute | solution.py:29
  58.3 1.5 collective-permute-start.12
  60.3 5.6 %collective-permute-done.12.refs_6_ = bf16[4,48,768]{2,1,0:T(8,128)(2,1)S(1)} collective-permute-done((bf16[4,48,768]{2,1,0:T(8,128)(2,1)S(1)}, bf16[4,48,768]{2,1,0:T(8,128)(2,1)S(1)}, u32[]{:S(2)}, u32[]{:S(2)}) %collective-permute-start.12) | collective-permute-done | bytes 294944 | tf_op jit(solution)/shard_map/ppermute | solution.py:29
  66.0 1.8 %collective-permute-start.14 = (bf16[4,48,768]{2,1,0:T(8,128)(2,1)S(1)}, bf16[4,48,768]{2,1,0:T(8,128)(2,1)S(1)}, u32[]{:S(2)}, u32[]{:S(2)}) collective-permute-start(bf16[4,48,768]{2,1,0:T(8,128)(2,1)S(1)} %collective-permute-done.12.refs_6_), channel_id=1, source_target_pairs={{0,38},{2,0},{4,2},{6,4},{32,6},{34,32},{36,34},{38,36},{1,39},{3,... | collective-permute-start | bytes 884744 | tf_op jit(solution)/shard_map/ppermute | solution.py:29
  68.1 5.0 %collective-permute-done.14.refs_8_ = bf16[4,48,768]{2,1,0:T(8,128)(2,1)S(1)} collective-permute-done((bf16[4,48,768]{2,1,0:T(8,128)(2,1)S(1)}, bf16[4,48,768]{2,1,0:T(8,128)(2,1)S(1)}, u32[]{:S(2)}, u32[]{:S(2)}) %collective-permute-start.14) | collective-permute-done | bytes 294944 | tf_op jit(solution)/shard_map/ppermute | solution.py:29
  73.1 2.7 %collective-permute-start.16 = (bf16[2,48,768]{2,1,0:T(8,128)(2,1)S(1)}, bf16[2,48,768]{2,1,0:T(8,128)(2,1)S(1)}, u32[]{:S(2)}, u32[]{:S(2)}) collective-permute-start(bf16[2,48,768]{2,1,0:T(8,128)(2,1)S(1)} %slice.104), channel_id=1, source_target_pairs={{0,38},{2,0},{4,2},{6,4},{32,6},{34,32},{36,34},{38,36},{1,39},{3,... | collective-permute-start | bytes 442376 | tf_op jit(solution)/shard_map/ppermute | solution.py:29
  76.7 1.8 %collective-permute-done.16.refs_10_ = bf16[2,48,768]{2,1,0:T(8,128)(2,1)S(1)} collective-permute-done((bf16[2,48,768]{2,1,0:T(8,128)(2,1)S(1)}, bf16[2,48,768]{2,1,0:T(8,128)(2,1)S(1)}, u32[]{:S(2)}, u32[]{:S(2)}) %collective-permute-start.16) | collective-permute-done | bytes 147488 | tf_op jit(solution)/shard_map/ppermute | solution.py:29
  78.5 4.1 %collective-permute-done.15.refs_9_ = bf16[2,48,768]{2,1,0:T(8,128)(2,1)} collective-permute-done((bf16[2,48,768]{2,1,0:T(8,128)(2,1)S(1)}, bf16[2,48,768]{2,1,0:T(8,128)(2,1)}, u32[]{:S(2)}, u32[]{:S(2)}) %collective-permute-start.15) | collective-permute-done | bytes 147488 | tf_op jit(solution)/shard_map/ppermute | solution.py:29
  82.6 1.3 copy-done
  83.9 16.2 %shard_map.95 = (bf16[1024,768]{1,0:T(8,128)(2,1)}, bf16[8,4,48,768]{3,2,1,0:T(8,128)(2,1)}) custom-call(s32[3]{0:T(128)} %pad_add_fusion.me, bf16[8,2,128,1536]{3,2,1,0:T(8,128)(2,1)} %bitcast.54, bf16[4,8,48,768]{3,2,1,0:T(8,128)(2,1)} %copy-done, bf16[4,48,768]{2,1,0:T(8,128)(2,1)} %copy-done.2, bf16[4,48,768]{2,1,0:T(8,128)(2,1)} %copy-done.6, ...), custom_call_target="tpu_custom_call" | custom-call | flops 7247757312 | bytes 20971520 | tf_op jit(solution)/shard_map/pallas_call | solution.py:228
  100.1 7.6 %shard_map.96.refs_2_ = bf16[4,8,48,768]{3,2,1,0:T(8,128)(2,1)} custom-call(s32[3]{0:T(128)} %pad_add_fusion.me, bf16[8,2,128,1536]{3,2,1,0:T(8,128)(2,1)} %bitcast.55, bf16[1024,768]{1,0:T(8,128)(2,1)} %get-tuple-element.40.refs_1_.refs_0_), custom_call_target="tpu_custom_call" | custom-call | flops 2415919104 | bytes 7340032 | tf_op jit(solution)/shard_map/pallas_call | solution.py:254
  107.7 5.1 %all-to-all-start.2 = ((bf16[4,8,48,768]{3,2,1,0:T(8,128)(2,1)}), bf16[4,8,48,768]{3,2,1,0:T(8,128)(2,1)S(1)}, u32[]{:S(2)}, u32[]{:S(2)}) async-start(bf16[4,8,48,768]{3,2,1,0:T(8,128)(2,1)} %shard_map.96.refs_2_), calls=%async_computation.2 | async-start | bytes 4718592 | tf_op jit(solution)/shard_map/all_to_all | solution.py:269
  112.8 7.8 %shard_map.97 = (bf16[512,1536]{1,0:T(8,128)(2,1)}, bf16[256,1536]{1,0:T(8,128)(2,1)}, bf16[256,1536]{1,0:T(8,128)(2,1)}) custom-call(s32[3]{0:T(128)} %pad_add_fusion.me, bf16[1024,768]{1,0:T(8,128)(2,1)} %get-tuple-element.40.refs_1_.refs_0_, bf16[4,8,48,768]{3,2,1,0:T(8,128)(2,1)} %copy-done, bf16[4,8,48,768]{3,2,1,0:T(8,128)(2,1)} %shard_map.96.refs_2_), custom_call_target="tpu_custom_call" | custom-call | flops 2415919104 | bytes 7340032 | tf_op jit(solution)/shard_map/pallas_call | solution.py:271
  121.2 2.0 %collective-permute-done.17 = bf16[256,1536]{1,0:T(8,128)(2,1)S(1)} collective-permute-done((bf16[256,1536]{1,0:T(8,128)(2,1)}, bf16[256,1536]{1,0:T(8,128)(2,1)S(1)}, u32[]{:S(2)}, u32[]{:S(2)}) %collective-permute-start.17) | collective-permute-done | bytes 786464 | tf_op jit(solution)/shard_map/ppermute | solution.py:29
  123.2 1.1 collective-permute-done.18
  124.3 3.0 %add_convert_fusion = bf16[512,1536]{1,0:T(8,128)(2,1)} fusion(bf16[512,1536]{1,0:T(8,128)(2,1)} %get-tuple-element.41, bf16[256,1536]{1,0:T(8,128)(2,1)S(1)} %collective-permute-done.18, bf16[256,1536]{1,0:T(8,128)(2,1)S(1)} %collective-permute-done.17), kind=kLoop, calls=%fused_computation | loop fusion | flops 5505024 | bytes 4718592 | tf_op jit(solution)/shard_map/convert_element_type | solution.py:282
  127.3 8.9 %all-to-all-done.2 = bf16[4,8,48,768]{3,2,1,0:T(8,128)(2,1)S(1)} async-done(((bf16[4,8,48,768]{3,2,1,0:T(8,128)(2,1)}), bf16[4,8,48,768]{3,2,1,0:T(8,128)(2,1)S(1)}, u32[]{:S(2)}, u32[]{:S(2)}) %all-to-all-start.2) | async-done | bytes 2359328 | tf_op jit(solution)/shard_map/all_to_all | solution.py:269
  136.1 6.4 %all-to-all-start.1 = ((bf16[4,128,1536]{2,1,0:T(8,128)(2,1)}), bf16[4,128,1536]{2,1,0:T(8,128)(2,1)}, u32[]{:S(2)}, u32[]{:S(2)}) async-start(bf16[4,128,1536]{2,1,0:T(8,128)(2,1)} %bitcast.56), calls=%async_computation.1 | async-start | bytes 3145728 | tf_op jit(solution)/shard_map/all_to_all | solution.py:283
  143.0 1.8 collective-permute-start.23
  145.1 1.0 slice_bitcast_fusion.8
  146.1 3.0 %collective-permute-start.21 = (bf16[48,768]{1,0:T(8,128)(2,1)S(1)}, bf16[48,768]{1,0:T(8,128)(2,1)S(1)}, u32[]{:S(2)}, u32[]{:S(2)}) collective-permute-start(bf16[48,768]{1,0:T(8,128)(2,1)S(1)} %get-tuple-element.54), channel_id=1, source_target_pairs={{0,16},{8,24},{16,0},{24,8},{1,17},{9,25},{17,1},{25,9},{2,18},{10... | collective-permute-start | bytes 221192 | tf_op jit(solution)/shard_map/ppermute | solution.py:29
  149.1 1.2 collective-permute-start.20
  151.1 0.9 collective-permute-done.22
  152.0 1.4 collective-permute-done.20
  153.5 2.6 %collective-permute-done.19 = bf16[48,768]{1,0:T(8,128)(2,1)S(1)} collective-permute-done((bf16[48,768]{1,0:T(8,128)(2,1)S(1)}, bf16[48,768]{1,0:T(8,128)(2,1)S(1)}, u32[]{:S(2)}, u32[]{:S(2)}) %collective-permute-start.19) | collective-permute-done | bytes 73760 | tf_op jit(solution)/shard_map/ppermute | solution.py:29
  156.2 0.9 fusion.6
  157.2 3.1 %collective-permute-start.25 = (bf16[2,48,768]{2,1,0:T(8,128)(2,1)S(1)}, bf16[2,48,768]{2,1,0:T(8,128)(2,1)S(1)}, u32[]{:S(2)}, u32[]{:S(2)}) collective-permute-start(bf16[2,48,768]{2,1,0:T(8,128)(2,1)S(1)} %pad_maximum_fusion.4.after_ref), channel_id=1, source_target_pairs={{0,0},{2,64},{4,128},{6,192},{32,32},{34,96},{36,160},{38,224},{64... | collective-permute-start | bytes 442376 | tf_op jit(solution)/shard_map/ppermute | solution.py:39
  160.3 5.9 %collective-permute-start.26 = (bf16[48,768]{1,0:T(8,128)(2,1)S(1)}, bf16[48,768]{1,0:T(8,128)(2,1)S(1)}, u32[]{:S(2)}, u32[]{:S(2)}) collective-permute-start(bf16[48,768]{1,0:T(8,128)(2,1)S(1)} %get-tuple-element.57), channel_id=1, source_target_pairs={{0,32},{2,96},{4,160},{6,224},{32,0},{34,64},{36,128},{38,192},{64... | collective-permute-start | bytes 221192 | tf_op jit(solution)/shard_map/ppermute | solution.py:39
  166.2 3.1 %shard_map.98 = bf16[128,1536]{1,0:T(8,128)(2,1)} custom-call(bf16[128,1536]{1,0:T(8,128)(2,1)} %x_ref.3, f32[1536]{0:T(1024)} %gain_ref.3, bf16[128,1536]{1,0:T(8,128)(2,1)} %grad_ref.3, bf16[4,128,1536]{2,1,0:T(8,128)(2,1)} %all-to-all-done.1.dx_ref, bf16[2,48,768]{2,1,0:T(8,128)(2,1)} %copy-done.1), custom_call_target="tpu_custom_call" | custom-call | flops 3932160 | bytes 2752512 | tf_op jit(solution)/shard_map/pallas_call | solution.py:297
  170.4 0.7 convert_add_fusion.1
  (63 shorter events, 6.1 us)
Async XLA Ops:
  7.2 75.4 %all-gather.3.cloned.1.call-start = ((), (), s32[]{:S(2)}) async-start(), calls=%async_computation.5 | async-start | bytes 7077888 | tf_op jit(solution)/shard_map/all_gather | solution.py:209
  8.1 21.2 %collective-permute-start.1 = (bf16[2,48,768]{2,1,0:T(8,128)(2,1)S(1)}, bf16[2,48,768]{2,1,0:T(8,128)(2,1)S(1)}, u32[]{:S(2)}, u32[]{:S(2)}) collective-permute-start(bf16[2,48,768]{2,1,0:T(8,128)(2,1)S(1)} %pad_maximum_fusion.2), channel_id=1, source_target_pairs={{0,0},{2,64},{4,128},{6,192},{32,32},{34,96},{36,160},{38,224},{64... | collective-permute-start | bytes 442376 | tf_op jit(solution)/shard_map/ppermute | solution.py:39
  13.1 16.2 %collective-permute-start.2 = (bf16[48,768]{1,0:T(8,128)(2,1)}, bf16[48,768]{1,0:T(8,128)(2,1)S(1)}, u32[]{:S(2)}, u32[]{:S(2)}) collective-permute-start(bf16[48,768]{1,0:T(8,128)(2,1)} %param.10), channel_id=1, source_target_pairs={{0,32},{2,96},{4,160},{6,224},{32,0},{34,64},{36,128},{38,192},{64... | collective-permute-start | bytes 221192 | tf_op jit(solution)/shard_map/ppermute | solution.py:39
  20.3 9.0 %collective-permute-start = (f32[768]{0:T(1024)}, f32[768]{0:T(1024)S(1)}, u32[]{:S(2)}, u32[]{:S(2)}) collective-permute-start(f32[768]{0:T(1024)} %param.11), channel_id=1, source_target_pairs={{0,0},{2,64},{4,128},{6,192},{32,32},{34,96},{36,160},{38,224},{64... | collective-permute-start | bytes 9224 | tf_op jit(solution)/shard_map/ppermute | solution.py:39
  29.4 7.2 %collective-permute-start.5 = (bf16[48,768]{1,0:T(8,128)(2,1)S(1)}, bf16[48,768]{1,0:T(8,128)(2,1)S(1)}, u32[]{:S(2)}, u32[]{:S(2)}) collective-permute-start(bf16[48,768]{1,0:T(8,128)(2,1)S(1)} %get-tuple-element.35), channel_id=1, source_target_pairs={{0,16},{8,24},{16,0},{24,8},{1,17},{9,25},{17,1},{25,9},{2,18},{10... | collective-permute-start | bytes 221192 | tf_op jit(solution)/shard_map/ppermute | solution.py:29
  32.5 10.8 %collective-permute-start.8 = (bf16[2,48,768]{2,1,0:T(8,128)(2,1)S(1)}, bf16[2,48,768]{2,1,0:T(8,128)(2,1)S(1)}, u32[]{:S(2)}, u32[]{:S(2)}) collective-permute-start(bf16[2,48,768]{2,1,0:T(8,128)(2,1)S(1)} %pad_maximum_fusion.3), channel_id=1, source_target_pairs={{0,4},{2,6},{4,32},{6,34},{32,36},{34,38},{36,0},{38,2},{1,5},{3,7... | collective-permute-start | bytes 442376 | tf_op jit(solution)/shard_map/ppermute | solution.py:29
  32.6 10.7 %collective-permute-start.7 = (bf16[2,48,768]{2,1,0:T(8,128)(2,1)S(1)}, bf16[2,48,768]{2,1,0:T(8,128)(2,1)S(1)}, u32[]{:S(2)}, u32[]{:S(2)}) collective-permute-start(bf16[2,48,768]{2,1,0:T(8,128)(2,1)S(1)} %pad_maximum_fusion.3), channel_id=1, source_target_pairs={{0,38},{2,0},{4,2},{6,4},{32,6},{34,32},{36,34},{38,36},{1,39},{3,... | collective-permute-start | bytes 442376 | tf_op jit(solution)/shard_map/ppermute | solution.py:29
  35.4 8.9 %collective-permute-start.6 = (bf16[2,48,768]{2,1,0:T(8,128)(2,1)S(1)}, bf16[2,48,768]{2,1,0:T(8,128)(2,1)S(1)}, u32[]{:S(2)}, u32[]{:S(2)}) collective-permute-start(bf16[2,48,768]{2,1,0:T(8,128)(2,1)S(1)} %pad_maximum_fusion.3), channel_id=1, source_target_pairs={{0,2},{2,4},{4,6},{6,32},{32,34},{34,36},{36,38},{38,0},{1,3},{3,5... | collective-permute-start | bytes 442376 | tf_op jit(solution)/shard_map/ppermute | solution.py:29
  35.4 4.4 %collective-permute-start.4 = (bf16[48,768]{1,0:T(8,128)(2,1)S(1)}, bf16[48,768]{1,0:T(8,128)(2,1)S(1)}, u32[]{:S(2)}, u32[]{:S(2)}) collective-permute-start(bf16[48,768]{1,0:T(8,128)(2,1)S(1)} %get-tuple-element.35), channel_id=1, source_target_pairs={{0,24},{8,0},{16,8},{24,16},{1,25},{9,1},{17,9},{25,17},{2,26},{10... | collective-permute-start | bytes 221192 | tf_op jit(solution)/shard_map/ppermute | solution.py:29
  36.5 5.6 %collective-permute-start.3 = (bf16[48,768]{1,0:T(8,128)(2,1)S(1)}, bf16[48,768]{1,0:T(8,128)(2,1)S(1)}, u32[]{:S(2)}, u32[]{:S(2)}) collective-permute-start(bf16[48,768]{1,0:T(8,128)(2,1)S(1)} %get-tuple-element.35), channel_id=1, source_target_pairs={{0,8},{8,16},{16,24},{24,0},{1,9},{9,17},{17,25},{25,1},{2,10},{10... | collective-permute-start | bytes 221192 | tf_op jit(solution)/shard_map/ppermute | solution.py:29
  46.0 36.5 %all-to-all-start = ((bf16[4,8,48,768]{3,2,1,0:T(8,128)(2,1)}), bf16[4,8,48,768]{3,2,1,0:T(8,128)(2,1)S(1)}, u32[]{:S(2)}, u32[]{:S(2)}) async-start(bf16[4,8,48,768]{3,2,1,0:T(8,128)(2,1)} %broadcast_in_dim.2), calls=%async_computation | async-start | bytes 4718592 | tf_op jit(solution)/shard_map/all_to_all | solution.py:219
  49.6 95.5 %reduce-scatter.2.cloned.1.call-start = ((), (), s32[]{:S(2)}) async-start(), calls=%async_computation.4 | async-start | bytes 2654208 | tf_op jit(solution)/shard_map/reduce_scatter | solution.py:252
  49.7 32.8 %copy-start.2 = (bf16[4,48,768]{2,1,0:T(8,128)(2,1)}, bf16[4,48,768]{2,1,0:T(8,128)(2,1)S(1)}, u32[]{:S(2)}) copy-start(bf16[4,48,768]{2,1,0:T(8,128)(2,1)S(1)} %pad_maximum_fusion.1.refs_2_) | copy-start | bytes 884740
  49.7 8.6 %collective-permute-start.10 = (bf16[4,48,768]{2,1,0:T(8,128)(2,1)S(1)}, bf16[4,48,768]{2,1,0:T(8,128)(2,1)S(1)}, u32[]{:S(2)}, u32[]{:S(2)}) collective-permute-start(bf16[4,48,768]{2,1,0:T(8,128)(2,1)S(1)} %pad_maximum_fusion.1.refs_2_), channel_id=1, source_target_pairs={{0,38},{2,0},{4,2},{6,4},{32,6},{34,32},{36,34},{38,36},{1,39},{3,... | collective-permute-start | bytes 884744 | tf_op jit(solution)/shard_map/ppermute | solution.py:29
  50.9 8.9 %collective-permute-start.9 = (bf16[4,48,768]{2,1,0:T(8,128)(2,1)S(1)}, bf16[4,48,768]{2,1,0:T(8,128)(2,1)S(1)}, u32[]{:S(2)}, u32[]{:S(2)}) collective-permute-start(bf16[4,48,768]{2,1,0:T(8,128)(2,1)S(1)} %pad_maximum_fusion.1.refs_2_), channel_id=1, source_target_pairs={{0,2},{2,4},{4,6},{6,32},{32,34},{34,36},{36,38},{38,0},{1,3},{3,5... | collective-permute-start | bytes 884744 | tf_op jit(solution)/shard_map/ppermute | solution.py:29
  58.3 2.0 %copy-start.5 = (bf16[4,48,768]{2,1,0:T(8,128)(2,1)}, bf16[4,48,768]{2,1,0:T(8,128)(2,1)S(1)}, u32[]{:S(2)}) copy-start(bf16[4,48,768]{2,1,0:T(8,128)(2,1)S(1)} %collective-permute-done.10.refs_4_) | copy-start | bytes 884740
  58.3 7.7 %collective-permute-start.12 = (bf16[4,48,768]{2,1,0:T(8,128)(2,1)S(1)}, bf16[4,48,768]{2,1,0:T(8,128)(2,1)S(1)}, u32[]{:S(2)}, u32[]{:S(2)}) collective-permute-start(bf16[4,48,768]{2,1,0:T(8,128)(2,1)S(1)} %collective-permute-done.10.refs_4_), channel_id=1, source_target_pairs={{0,38},{2,0},{4,2},{6,4},{32,6},{34,32},{36,34},{38,36},{1,39},{3,... | collective-permute-start | bytes 884744 | tf_op jit(solution)/shard_map/ppermute | solution.py:29
  59.8 8.0 %copy-start.6 = (bf16[4,48,768]{2,1,0:T(8,128)(2,1)}, bf16[4,48,768]{2,1,0:T(8,128)(2,1)S(1)}, u32[]{:S(2)}) copy-start(bf16[4,48,768]{2,1,0:T(8,128)(2,1)S(1)} %collective-permute-done.9.refs_3_) | copy-start | bytes 884740
  59.8 8.0 %collective-permute-start.11 = (bf16[4,48,768]{2,1,0:T(8,128)(2,1)S(1)}, bf16[4,48,768]{2,1,0:T(8,128)(2,1)S(1)}, u32[]{:S(2)}, u32[]{:S(2)}) collective-permute-start(bf16[4,48,768]{2,1,0:T(8,128)(2,1)S(1)} %collective-permute-done.9.refs_3_), channel_id=1, source_target_pairs={{0,2},{2,4},{4,6},{6,32},{32,34},{34,36},{36,38},{38,0},{1,3},{3,5... | collective-permute-start | bytes 884744 | tf_op jit(solution)/shard_map/ppermute | solution.py:29
  66.0 2.1 %copy-start.7 = (bf16[4,48,768]{2,1,0:T(8,128)(2,1)}, bf16[4,48,768]{2,1,0:T(8,128)(2,1)S(1)}, u32[]{:S(2)}) copy-start(bf16[4,48,768]{2,1,0:T(8,128)(2,1)S(1)} %collective-permute-done.12.refs_6_) | copy-start | bytes 884740
  66.0 7.1 %collective-permute-start.14 = (bf16[4,48,768]{2,1,0:T(8,128)(2,1)S(1)}, bf16[4,48,768]{2,1,0:T(8,128)(2,1)S(1)}, u32[]{:S(2)}, u32[]{:S(2)}) collective-permute-start(bf16[4,48,768]{2,1,0:T(8,128)(2,1)S(1)} %collective-permute-done.12.refs_6_), channel_id=1, source_target_pairs={{0,38},{2,0},{4,2},{6,4},{32,6},{34,32},{36,34},{38,36},{1,39},{3,... | collective-permute-start | bytes 884744 | tf_op jit(solution)/shard_map/ppermute | solution.py:29
  67.8 8.0 %copy-start.8 = (bf16[4,48,768]{2,1,0:T(8,128)(2,1)}, bf16[4,48,768]{2,1,0:T(8,128)(2,1)S(1)}, u32[]{:S(2)}) copy-start(bf16[4,48,768]{2,1,0:T(8,128)(2,1)S(1)} %collective-permute-done.11.refs_5_) | copy-start | bytes 884740
  67.8 8.0 %collective-permute-start.13 = (bf16[4,48,768]{2,1,0:T(8,128)(2,1)S(1)}, bf16[4,48,768]{2,1,0:T(8,128)(2,1)S(1)}, u32[]{:S(2)}, u32[]{:S(2)}) collective-permute-start(bf16[4,48,768]{2,1,0:T(8,128)(2,1)S(1)} %collective-permute-done.11.refs_5_), channel_id=1, source_target_pairs={{0,2},{2,4},{4,6},{6,32},{32,34},{34,36},{36,38},{38,0},{1,3},{3,5... | collective-permute-start | bytes 884744 | tf_op jit(solution)/shard_map/ppermute | solution.py:29
  73.1 9.5 %copy-start.3 = (bf16[4,48,768]{2,1,0:T(8,128)(2,1)}, bf16[4,48,768]{2,1,0:T(8,128)(2,1)S(1)}, u32[]{:S(2)}) copy-start(bf16[4,48,768]{2,1,0:T(8,128)(2,1)S(1)} %collective-permute-done.14.refs_8_) | copy-start | bytes 884740
  73.1 5.4 %collective-permute-start.16 = (bf16[2,48,768]{2,1,0:T(8,128)(2,1)S(1)}, bf16[2,48,768]{2,1,0:T(8,128)(2,1)S(1)}, u32[]{:S(2)}, u32[]{:S(2)}) collective-permute-start(bf16[2,48,768]{2,1,0:T(8,128)(2,1)S(1)} %slice.104), channel_id=1, source_target_pairs={{0,38},{2,0},{4,2},{6,4},{32,6},{34,32},{36,34},{38,36},{1,39},{3,... | collective-permute-start | bytes 442376 | tf_op jit(solution)/shard_map/ppermute | solution.py:29
  75.8 6.8 %copy-start.4 = (bf16[4,48,768]{2,1,0:T(8,128)(2,1)}, bf16[4,48,768]{2,1,0:T(8,128)(2,1)S(1)}, u32[]{:S(2)}) copy-start(bf16[4,48,768]{2,1,0:T(8,128)(2,1)S(1)} %collective-permute-done.13.refs_7_) | copy-start | bytes 884740
  75.8 6.7 %collective-permute-start.15 = (bf16[2,48,768]{2,1,0:T(8,128)(2,1)S(1)}, bf16[2,48,768]{2,1,0:T(8,128)(2,1)}, u32[]{:S(2)}, u32[]{:S(2)}) collective-permute-start(bf16[2,48,768]{2,1,0:T(8,128)(2,1)S(1)} %slice.103), channel_id=1, source_target_pairs={{0,2},{2,4},{4,6},{6,32},{32,34},{34,36},{36,38},{38,0},{1,3},{3,5... | collective-permute-start | bytes 442376 | tf_op jit(solution)/shard_map/ppermute | solution.py:29
  78.5 4.1 %copy-start.9 = (bf16[2,48,768]{2,1,0:T(8,128)(2,1)}, bf16[2,48,768]{2,1,0:T(8,128)(2,1)S(1)}, u32[]{:S(2)}) copy-start(bf16[2,48,768]{2,1,0:T(8,128)(2,1)S(1)} %collective-permute-done.16.refs_10_) | copy-start | bytes 442372
  82.5 1.4 copy-start
  107.7 28.5 %all-to-all-start.2 = ((bf16[4,8,48,768]{3,2,1,0:T(8,128)(2,1)}), bf16[4,8,48,768]{3,2,1,0:T(8,128)(2,1)S(1)}, u32[]{:S(2)}, u32[]{:S(2)}) async-start(bf16[4,8,48,768]{3,2,1,0:T(8,128)(2,1)} %shard_map.96.refs_2_), calls=%async_computation.2 | async-start | bytes 4718592 | tf_op jit(solution)/shard_map/all_to_all | solution.py:269
  120.6 2.6 %collective-permute-start.17 = (bf16[256,1536]{1,0:T(8,128)(2,1)}, bf16[256,1536]{1,0:T(8,128)(2,1)S(1)}, u32[]{:S(2)}, u32[]{:S(2)}) collective-permute-start(bf16[256,1536]{1,0:T(8,128)(2,1)} %get-tuple-element.42), channel_id=1, source_target_pairs={{0,1},{1,0},{2,3},{3,2},{4,5},{5,4},{6,7},{7,6},{8,9},{9,8},{10,11... | collective-permute-start | bytes 2359304 | tf_op jit(solution)/shard_map/ppermute | solution.py:29
  120.7 3.6 %collective-permute-start.18 = (bf16[256,1536]{1,0:T(8,128)(2,1)}, bf16[256,1536]{1,0:T(8,128)(2,1)S(1)}, u32[]{:S(2)}, u32[]{:S(2)}) collective-permute-start(bf16[256,1536]{1,0:T(8,128)(2,1)} %get-tuple-element.43), channel_id=1, source_target_pairs={{0,1},{1,0},{2,3},{3,2},{4,5},{5,4},{6,7},{7,6},{8,9},{9,8},{10,11... | collective-permute-start | bytes 2359304 | tf_op jit(solution)/shard_map/ppermute | solution.py:29
  136.1 30.0 %all-to-all-start.1 = ((bf16[4,128,1536]{2,1,0:T(8,128)(2,1)}), bf16[4,128,1536]{2,1,0:T(8,128)(2,1)}, u32[]{:S(2)}, u32[]{:S(2)}) async-start(bf16[4,128,1536]{2,1,0:T(8,128)(2,1)} %bitcast.56), calls=%async_computation.1 | async-start | bytes 3145728 | tf_op jit(solution)/shard_map/all_to_all | solution.py:283
  142.9 7.6 %collective-permute-start.24 = (bf16[2,48,768]{2,1,0:T(8,128)(2,1)S(1)}, bf16[2,48,768]{2,1,0:T(8,128)(2,1)S(1)}, u32[]{:S(2)}, u32[]{:S(2)}) collective-permute-start(bf16[2,48,768]{2,1,0:T(8,128)(2,1)S(1)} %get-tuple-element.51), channel_id=1, source_target_pairs={{0,4},{2,6},{4,32},{6,34},{32,36},{34,38},{36,0},{38,2},{1,5},{3,7... | collective-permute-start | bytes 442376 | tf_op jit(solution)/shard_map/ppermute | solution.py:29
  143.0 8.1 %collective-permute-start.23 = (bf16[2,48,768]{2,1,0:T(8,128)(2,1)S(1)}, bf16[2,48,768]{2,1,0:T(8,128)(2,1)S(1)}, u32[]{:S(2)}, u32[]{:S(2)}) collective-permute-start(bf16[2,48,768]{2,1,0:T(8,128)(2,1)S(1)} %get-tuple-element.52), channel_id=1, source_target_pairs={{0,38},{2,0},{4,2},{6,4},{32,6},{34,32},{36,34},{38,36},{1,39},{3,... | collective-permute-start | bytes 442376 | tf_op jit(solution)/shard_map/ppermute | solution.py:29
  144.8 7.3 %collective-permute-start.22 = (bf16[2,48,768]{2,1,0:T(8,128)(2,1)S(1)}, bf16[2,48,768]{2,1,0:T(8,128)(2,1)S(1)}, u32[]{:S(2)}, u32[]{:S(2)}) collective-permute-start(bf16[2,48,768]{2,1,0:T(8,128)(2,1)S(1)} %get-tuple-element.53), channel_id=1, source_target_pairs={{0,2},{2,4},{4,6},{6,32},{32,34},{34,36},{36,38},{38,0},{1,3},{3,5... | collective-permute-start | bytes 442376 | tf_op jit(solution)/shard_map/ppermute | solution.py:29
  146.1 6.0 %collective-permute-start.21 = (bf16[48,768]{1,0:T(8,128)(2,1)S(1)}, bf16[48,768]{1,0:T(8,128)(2,1)S(1)}, u32[]{:S(2)}, u32[]{:S(2)}) collective-permute-start(bf16[48,768]{1,0:T(8,128)(2,1)S(1)} %get-tuple-element.54), channel_id=1, source_target_pairs={{0,16},{8,24},{16,0},{24,8},{1,17},{9,25},{17,1},{25,9},{2,18},{10... | collective-permute-start | bytes 221192 | tf_op jit(solution)/shard_map/ppermute | solution.py:29
  149.1 4.4 %collective-permute-start.20 = (bf16[48,768]{1,0:T(8,128)(2,1)S(1)}, bf16[48,768]{1,0:T(8,128)(2,1)S(1)}, u32[]{:S(2)}, u32[]{:S(2)}) collective-permute-start(bf16[48,768]{1,0:T(8,128)(2,1)S(1)} %get-tuple-element.55), channel_id=1, source_target_pairs={{0,24},{8,0},{16,8},{24,16},{1,25},{9,1},{17,9},{25,17},{2,26},{10... | collective-permute-start | bytes 221192 | tf_op jit(solution)/shard_map/ppermute | solution.py:29
  150.5 5.6 %collective-permute-start.19 = (bf16[48,768]{1,0:T(8,128)(2,1)S(1)}, bf16[48,768]{1,0:T(8,128)(2,1)S(1)}, u32[]{:S(2)}, u32[]{:S(2)}) collective-permute-start(bf16[48,768]{1,0:T(8,128)(2,1)S(1)} %get-tuple-element.56), channel_id=1, source_target_pairs={{0,8},{8,16},{16,24},{24,0},{1,9},{9,17},{17,25},{25,1},{2,10},{10... | collective-permute-start | bytes 221192 | tf_op jit(solution)/shard_map/ppermute | solution.py:29
  157.2 9.0 %copy-start.1 = (bf16[2,48,768]{2,1,0:T(8,128)(2,1)}, bf16[2,48,768]{2,1,0:T(8,128)(2,1)S(1)}, u32[]{:S(2)}) copy-start(bf16[2,48,768]{2,1,0:T(8,128)(2,1)S(1)} %pad_maximum_fusion.4.after_ref) | copy-start | bytes 442372
  157.2 12.5 %collective-permute-start.25 = (bf16[2,48,768]{2,1,0:T(8,128)(2,1)S(1)}, bf16[2,48,768]{2,1,0:T(8,128)(2,1)S(1)}, u32[]{:S(2)}, u32[]{:S(2)}) collective-permute-start(bf16[2,48,768]{2,1,0:T(8,128)(2,1)S(1)} %pad_maximum_fusion.4.after_ref), channel_id=1, source_target_pairs={{0,0},{2,64},{4,128},{6,192},{32,32},{34,96},{36,160},{38,224},{64... | collective-permute-start | bytes 442376 | tf_op jit(solution)/shard_map/ppermute | solution.py:39
  160.3 10.1 %collective-permute-start.26 = (bf16[48,768]{1,0:T(8,128)(2,1)S(1)}, bf16[48,768]{1,0:T(8,128)(2,1)S(1)}, u32[]{:S(2)}, u32[]{:S(2)}) collective-permute-start(bf16[48,768]{1,0:T(8,128)(2,1)S(1)} %get-tuple-element.57), channel_id=1, source_target_pairs={{0,32},{2,96},{4,160},{6,224},{32,0},{34,64},{36,128},{38,192},{64... | collective-permute-start | bytes 221192 | tf_op jit(solution)/shard_map/ppermute | solution.py:39
Sparse Core Ops, SparseCore 0:
  29.5 40.5 all-gather.2
  100.2 44.4 reduce-scatter.1

commit v5 on v4

--- a/solution.py
+++ b/solution.py
@@ -16,7 +16,7 @@
 Z = ("zh", "zl")
 X_STEPS = (0, 1, -1, 2)
 Z_STEPS = tuple((r, h) for r in (0, 1, -1, 2) for h in (0, 4))
-RING = tuple((k, (0, 1, 2, 3)) for k in (0, -1, 1, -2, 2, -3, 3)) + ((-4, (0, 1)), (4, (2, 3)))
+RING = tuple((k, (0, 1, 2, 3)) for k in (0, -1, 1)) + ((-2, (0, 1)), (2, (2, 3)))
 SIZES = {"y": 4, "x": 4, "c": 2, Z: 8}
 ANY = pl.BlockSpec(memory_space=pl.ANY)
 VM = pl.BlockSpec(memory_space=pltpu.VMEM)
@@ -75,17 +75,19 @@
 
 
 def main_kernel(me, *refs):
-    toks, wins, wos = refs[0], refs[1], refs[2:11]
-    bias_ref, gp_ref, dwo_ref = refs[11:14]
-    n_s, g_s, win_s, wo_s, act_s, dwo_s, sem_n, sem_g, sem_i, sem_o = refs[14:]
+    toks, wins, wos = refs[0], refs[1], refs[2:7]
+    bias_ref, gp_ref, dwo_ref = refs[7:10]
+    n_s, g_s, win_s, wo_s, act_s, dwo_s, sem_n, sem_g, sem_i, sem_o = refs[10:]
     n_copies = token_copies(toks, me, 0, n_s, sem_n)
     g_copies = token_copies(toks, me, 1, g_s, sem_g)
     i_copies = win_copies(wins, me, win_s, sem_i)
     o_copies = []
     for piece, (away, xs) in zip(wos, RING):
         for k, i in enumerate(xs):
-            at = rows_at(wo_s, (me[1] + away + 8) % 8, (me[0] - X_STEPS[i] + 4) % 4)
-            o_copies.append(pltpu.make_async_copy(piece.at[k], at, sem_o.at[len(o_copies)]))
+            for h in range(2):
+                z = (me[1] + away + 4 * h + 8) % 8
+                at = rows_at(wo_s, z, (me[0] - X_STEPS[i] + 4) % 4)
+                o_copies.append(pltpu.make_async_copy(piece.at[k, h], at, sem_o.at[len(o_copies)]))
     for copy in n_copies + i_copies + g_copies + o_copies:
         copy.start()
     for copy in n_copies + i_copies + g_copies + o_copies:
@@ -192,8 +194,8 @@
 def on_device(inputs, norm_gain, norm_bias, w_in, bias_in, w_out, grad_out):
     me = jnp.stack([lax.axis_index(a) for a in ("x", Z, "c")]).astype(jnp.int32)
 
-    both = turn(jnp.stack([w_in, w_out.T]))
-    win_far = turn(w_in, 1)
+    weights = jnp.stack([w_in, w_out.T])
+    both, far_both = turn(weights), turn(weights, 1)
     bias = turn(bias_in)
 
     tok = pl.pallas_call(
@@ -205,11 +207,12 @@
         cost_estimate=cost(10 * TD * D, 8 * TD * D),
     )(inputs, norm_gain, norm_bias, grad_out)
 
-    me, bias, both, win_far, tok = lax.optimization_barrier((me, bias, both, win_far, tok))
+    me, bias, both, far_both, tok = lax.optimization_barrier((me, bias, both, far_both, tok))
     toks = lax.all_gather(tok, ("y", "c"), axis=0, tiled=False)
 
-    wo_x = [both[1]] + [shift(both[1], "x", s) for s in X_STEPS[1:]]
-    win_h = jnp.stack([both[0], win_far])
+    wo_pair = jnp.stack([both[1], far_both[1]])
+    wo_x = [wo_pair] + [shift(wo_pair, "x", s) for s in X_STEPS[1:]]
+    win_h = jnp.stack([both[0], far_both[0]])
     win_z = [win_h] + [shift(win_h, Z, r) for r in (1, -1, 2)]
     *wo_x, w0, w1, w2, w3 = lax.optimization_barrier((*wo_x, *win_z))
     win_z = [w0, w1, w2, w3]
@@ -218,9 +221,6 @@
     win_z = jnp.broadcast_to(jnp.concatenate(win_z)[None], (4, 8, RB, FD))
     wins = lax.all_to_all(win_z, "x", 0, 0, tiled=True)
     wos = [wo_h, ahead, back]
-    for _ in range(2):
-        ahead, back = shift(ahead, Z, 1), shift(back, Z, -1)
-        wos += [ahead, back]
     wos += [shift(ahead[:2], Z, 1), shift(back[2:], Z, -1)]
     bias = bias.reshape(1, FD)
 
@@ -231,7 +231,7 @@
             jax.ShapeDtypeStruct((1024, FD), BF),
             jax.ShapeDtypeStruct((8, 4, RB, FD), BF),
         ),
-        in_specs=[SM] + [ANY] * 11 + [VM],
+        in_specs=[SM] + [ANY] * 7 + [VM],
         out_specs=(VM, ANY),
         scratch_shapes=[
             pltpu.VMEM((1024, D), BF),

time: 179 us -> 184 us (1.028)
  waiting for transfers between devices: 50.3 us -> 58.1 us
  starting transfers between devices: 64.4 us -> 61.5 us
    all_to_all x1, waiting for transfers between devices: 8.89 us -> 12.6 us  [on_device(): dws = lax.all_to_all(dws, 'x', 0, 0, tiled=True)]
    ppermute x5, waiting for transfers between devices: 3.23 us -> 6.57 us  [turn(): return lax.ppermute(value, ('y', 'zh', 'zl'), pairs)]
    all_to_all x1, waiting for transfers between devices: 0.01 us -> 2.81 us  [on_device(): wins = lax.all_to_all(win_z, 'x', 0, 0, tiled=True)]
    ppermute x22 -> x18, waiting for transfers between devices: 38.1 us -> 36 us  [shift(): return lax.ppermute(value, axis, [(i, (i + by) % n) for i in range(n)])]
    ppermute x22 -> x18, starting transfers between devices: 24.8 us -> 23.9 us  [shift(): return lax.ppermute(value, axis, [(i, (i + by) % n) for i in range(n)])]
  transfers between devices with their start and end apart: 32 -> 28, of which waited for: 18 -> 15; matrix products, arithmetic and copies ran while one was open for 5% -> 5% of each run, Pallas kernels for 12% -> 11%
where the time goes in v5:
time: 184 us; the launch traced here: 183 us
  starting transfers between devices  61.5 us (33%)
  waiting for transfers between devices  58.1 us (32%)
  Pallas kernels  37 us (20%)
  between operations  14.3 us (8%)
  other arithmetic  7.34 us (4%)
  local copies, waits for them, and re-layouts  4.63 us (3%)
    ppermute x18, waiting for transfers between devices, shift(): return lax.ppermute(value, axis, [(i, (i + by) % n) for i in range(n)])  36 us
    ppermute x18, starting transfers between devices, shift(): return lax.ppermute(value, axis, [(i, (i + by) % n) for i in range(n)])  23.9 us
    ppermute x5, starting transfers between devices, turn(): return lax.ppermute(value, ('y', 'zh', 'zl'), pairs)  22.9 us
    pallas_call x1, Pallas kernels, on_device(): pl.pallas_call(main_kernel, out_shape=(jax.ShapeDtypeStruct((1024, FD), B...  16.1 us
    all_to_all x1, waiting for transfers between devices, on_device(): dws = lax.all_to_all(dws, 'x', 0, 0, tiled=True)  12.6 us
    pallas_call x1, Pallas kernels, on_device(): pl.pallas_call(dx_kernel, out_shape=[jax.ShapeDtypeStruct((512, D), BF)]...  7.84 us
    pallas_call x1, Pallas kernels, on_device(): pl.pallas_call(dwin_kernel, out_shape=jax.ShapeDtypeStruct((4, 8, RB, FD)...  7.56 us
    all_to_all x1, starting transfers between devices, on_device(): dx_y = lax.all_to_all(dx_c, 'y', 0, 0, tiled=True).reshape(4, TD, D)  7.29 us
  transfers between devices with their start and end apart: 28, of which 15 were waited for; matrix products, arithmetic and copies ran while one was open for 5% of the time, Pallas kernels for 11%

profile of v5, /device:TPU:16, one launch (start us, length us, event | category | flops | bytes accessed | tf_op | source)
XLA Modules:
  0.0 182.8 jit_solution(12552591000260489977)
XLA Ops:
  7.2 0.9 pad_maximum_fusion.2
  8.1 6.2 %collective-permute-start.2 = (bf16[2,48,768]{2,1,0:T(8,128)(2,1)S(1)}, bf16[2,48,768]{2,1,0:T(8,128)(2,1)S(1)}, u32[]{:S(2)}, u32[]{:S(2)}) collective-permute-start(bf16[2,48,768]{2,1,0:T(8,128)(2,1)S(1)} %pad_maximum_fusion.2), channel_id=1, source_target_pairs={{0,32},{2,96},{4,160},{6,224},{32,0},{34,64},{36,128},{38,192},{64... | collective-permute-start | bytes 442376 | tf_op jit(solution)/shard_map/ppermute | solution.py:39
  14.3 6.0 %collective-permute-start.1 = (bf16[2,48,768]{2,1,0:T(8,128)(2,1)S(1)}, bf16[2,48,768]{2,1,0:T(8,128)(2,1)S(1)}, u32[]{:S(2)}, u32[]{:S(2)}) collective-permute-start(bf16[2,48,768]{2,1,0:T(8,128)(2,1)S(1)} %pad_maximum_fusion.2), channel_id=1, source_target_pairs={{0,0},{2,64},{4,128},{6,192},{32,32},{34,96},{36,160},{38,224},{64... | collective-permute-start | bytes 442376 | tf_op jit(solution)/shard_map/ppermute | solution.py:39
  20.3 3.2 %collective-permute-start = (f32[768]{0:T(1024)}, f32[768]{0:T(1024)S(1)}, u32[]{:S(2)}, u32[]{:S(2)}) collective-permute-start(f32[768]{0:T(1024)} %param.11), channel_id=1, source_target_pairs={{0,0},{2,64},{4,128},{6,192},{32,32},{34,96},{36,160},{38,224},{64... | collective-permute-start | bytes 9224 | tf_op jit(solution)/shard_map/ppermute | solution.py:39
  23.5 0.6 pad_add_fusion.me
  24.1 2.4 %shard_map.94 = bf16[2,128,1536]{2,1,0:T(8,128)(2,1)} custom-call(bf16[128,1536]{1,0:T(8,128)(2,1)} %x_ref.3, f32[1536]{0:T(1024)} %gain_ref.3, f32[1536]{0:T(1024)} %bias_ref.1, bf16[128,1536]{1,0:T(8,128)(2,1)} %grad_ref.3), custom_call_target="tpu_custom_call" | custom-call | flops 1966080 | bytes 1572864 | tf_op jit(solution)/shard_map/pallas_call | solution.py:201
  26.4 4.1 %collective-permute-done = f32[768]{0:T(1024)S(1)} collective-permute-done((f32[768]{0:T(1024)}, f32[768]{0:T(1024)S(1)}, u32[]{:S(2)}, u32[]{:S(2)}) %collective-permute-start) | collective-permute-done | bytes 3104 | tf_op jit(solution)/shard_map/ppermute | solution.py:39
  30.6 3.1 %collective-permute-start.5 = (bf16[2,48,768]{2,1,0:T(8,128)(2,1)S(1)}, bf16[2,48,768]{2,1,0:T(8,128)(2,1)S(1)}, u32[]{:S(2)}, u32[]{:S(2)}) collective-permute-start(bf16[2,48,768]{2,1,0:T(8,128)(2,1)S(1)} %pad_maximum_fusion.3), channel_id=1, source_target_pairs={{0,16},{8,24},{16,0},{24,8},{1,17},{9,25},{17,1},{25,9},{2,18},{10... | collective-permute-start | bytes 442376 | tf_op jit(solution)/shard_map/ppermute | solution.py:29
  33.8 1.1 collective-permute-start.4
  34.9 0.9 collective-permute-start.3
  35.9 4.0 %collective-permute-start.7 = (bf16[2,48,768]{2,1,0:T(8,128)(2,1)S(1)}, bf16[2,48,768]{2,1,0:T(8,128)(2,1)S(1)}, u32[]{:S(2)}, u32[]{:S(2)}) collective-permute-start(bf16[2,48,768]{2,1,0:T(8,128)(2,1)S(1)} %pad_maximum_fusion.4), channel_id=1, source_target_pairs={{0,38},{2,0},{4,2},{6,4},{32,6},{34,32},{36,34},{38,36},{1,39},{3,... | collective-permute-start | bytes 442376 | tf_op jit(solution)/shard_map/ppermute | solution.py:29
  39.9 1.1 collective-permute-done.4
  41.0 0.6 collective-permute-done.3
  41.6 5.6 %collective-permute-done.8 = bf16[2,48,768]{2,1,0:T(8,128)(2,1)S(1)} collective-permute-done((bf16[2,48,768]{2,1,0:T(8,128)(2,1)S(1)}, bf16[2,48,768]{2,1,0:T(8,128)(2,1)S(1)}, u32[]{:S(2)}, u32[]{:S(2)}) %collective-permute-start.8) | collective-permute-done | bytes 147488 | tf_op jit(solution)/shard_map/ppermute | solution.py:29
  47.2 1.0 collective-permute-done.6
  48.3 1.6 broadcast_in_dim.2
  49.8 3.6 %all-to-all-start = ((bf16[4,8,48,768]{3,2,1,0:T(8,128)(2,1)}), bf16[4,8,48,768]{3,2,1,0:T(8,128)(2,1)S(1)}, u32[]{:S(2)}, u32[]{:S(2)}) async-start(bf16[4,8,48,768]{3,2,1,0:T(8,128)(2,1)} %broadcast_in_dim.2), calls=%async_computation | async-start | bytes 4718592 | tf_op jit(solution)/shard_map/all_to_all | solution.py:222
  53.6 1.5 collective-permute-start.10
  55.1 0.6 collective-permute-start.9
  55.7 11.7 %collective-permute-done.10.refs_4_ = bf16[4,2,48,768]{3,2,1,0:T(8,128)(2,1)S(1)} collective-permute-done((bf16[4,2,48,768]{3,2,1,0:T(8,128)(2,1)S(1)}, bf16[4,2,48,768]{3,2,1,0:T(8,128)(2,1)S(1)}, u32[]{:S(2)}, u32[]{:S(2)}) %collective-permute-start.10) | collective-permute-done | bytes 589856 | tf_op jit(solution)/shard_map/ppermute | solution.py:29
  67.5 2.9 %collective-permute-start.12 = (bf16[2,2,48,768]{3,2,1,0:T(8,128)(2,1)S(1)}, bf16[2,2,48,768]{3,2,1,0:T(8,128)(2,1)S(1)}, u32[]{:S(2)}, u32[]{:S(2)}) collective-permute-start(bf16[2,2,48,768]{3,2,1,0:T(8,128)(2,1)S(1)} %slice.109), channel_id=1, source_target_pairs={{0,38},{2,0},{4,2},{6,4},{32,6},{34,32},{36,34},{38,36},{1,39},{3,... | collective-permute-start | bytes 884744 | tf_op jit(solution)/shard_map/ppermute | solution.py:29
  70.7 0.6 reshape.40.refs_7_
  71.3 3.4 %collective-permute-done.12.refs_6_ = bf16[2,2,48,768]{3,2,1,0:T(8,128)(2,1)S(1)} collective-permute-done((bf16[2,2,48,768]{3,2,1,0:T(8,128)(2,1)S(1)}, bf16[2,2,48,768]{3,2,1,0:T(8,128)(2,1)S(1)}, u32[]{:S(2)}, u32[]{:S(2)}) %collective-permute-start.12) | collective-permute-done | bytes 294944 | tf_op jit(solution)/shard_map/ppermute | solution.py:29
  74.7 4.1 %collective-permute-done.11.refs_5_ = bf16[2,2,48,768]{3,2,1,0:T(8,128)(2,1)} collective-permute-done((bf16[2,2,48,768]{3,2,1,0:T(8,128)(2,1)S(1)}, bf16[2,2,48,768]{3,2,1,0:T(8,128)(2,1)}, u32[]{:S(2)}, u32[]{:S(2)}) %collective-permute-start.11) | collective-permute-done | bytes 294944 | tf_op jit(solution)/shard_map/ppermute | solution.py:29
  78.7 2.8 %all-to-all-done.refs_1_ = bf16[4,8,48,768]{3,2,1,0:T(8,128)(2,1)S(1)} async-done(((bf16[4,8,48,768]{3,2,1,0:T(8,128)(2,1)}), bf16[4,8,48,768]{3,2,1,0:T(8,128)(2,1)S(1)}, u32[]{:S(2)}, u32[]{:S(2)}) %all-to-all-start) | async-done | bytes 2359328 | tf_op jit(solution)/shard_map/all_to_all | solution.py:222
  81.6 1.4 copy-done
  82.9 16.1 %shard_map.95 = (bf16[1024,768]{1,0:T(8,128)(2,1)}, bf16[8,4,48,768]{3,2,1,0:T(8,128)(2,1)}) custom-call(s32[3]{0:T(128)} %pad_add_fusion.me, bf16[8,2,128,1536]{3,2,1,0:T(8,128)(2,1)} %bitcast.51, bf16[4,8,48,768]{3,2,1,0:T(8,128)(2,1)} %copy-done, bf16[4,2,48,768]{3,2,1,0:T(8,128)(2,1)} %copy-done.2, bf16[4,2,48,768]{3,2,1,0:T(8,128)(2,1)} %copy-done.4, ...), custom_call_target="tpu_custom_call" | custom-call | flops 7247757312 | bytes 20971520 | tf_op jit(solution)/shard_map/pallas_call | solution.py:228
  99.1 7.6 %shard_map.96.refs_2_ = bf16[4,8,48,768]{3,2,1,0:T(8,128)(2,1)} custom-call(s32[3]{0:T(128)} %pad_add_fusion.me, bf16[8,2,128,1536]{3,2,1,0:T(8,128)(2,1)} %bitcast.52, bf16[1024,768]{1,0:T(8,128)(2,1)} %get-tuple-element.40.refs_1_.refs_0_), custom_call_target="tpu_custom_call" | custom-call | flops 2415919104 | bytes 7340032 | tf_op jit(solution)/shard_map/pallas_call | solution.py:254
  106.7 3.7 %all-to-all-start.2 = ((bf16[4,8,48,768]{3,2,1,0:T(8,128)(2,1)}), bf16[4,8,48,768]{3,2,1,0:T(8,128)(2,1)S(1)}, u32[]{:S(2)}, u32[]{:S(2)}) async-start(bf16[4,8,48,768]{3,2,1,0:T(8,128)(2,1)} %shard_map.96.refs_2_), calls=%async_computation.2 | async-start | bytes 4718592 | tf_op jit(solution)/shard_map/all_to_all | solution.py:269
  110.4 7.8 %shard_map.97 = (bf16[512,1536]{1,0:T(8,128)(2,1)}, bf16[256,1536]{1,0:T(8,128)(2,1)}, bf16[256,1536]{1,0:T(8,128)(2,1)}) custom-call(s32[3]{0:T(128)} %pad_add_fusion.me, bf16[1024,768]{1,0:T(8,128)(2,1)} %get-tuple-element.40.refs_1_.refs_0_, bf16[4,8,48,768]{3,2,1,0:T(8,128)(2,1)} %copy-done, bf16[4,8,48,768]{3,2,1,0:T(8,128)(2,1)} %shard_map.96.refs_2_), custom_call_target="tpu_custom_call" | custom-call | flops 2415919104 | bytes 7340032 | tf_op jit(solution)/shard_map/pallas_call | solution.py:271
  118.8 2.0 %collective-permute-done.13 = bf16[256,1536]{1,0:T(8,128)(2,1)S(1)} collective-permute-done((bf16[256,1536]{1,0:T(8,128)(2,1)}, bf16[256,1536]{1,0:T(8,128)(2,1)S(1)}, u32[]{:S(2)}, u32[]{:S(2)}) %collective-permute-start.13) | collective-permute-done | bytes 786464 | tf_op jit(solution)/shard_map/ppermute | solution.py:29
  120.8 1.1 collective-permute-done.14
  121.9 3.0 %add_convert_fusion = bf16[512,1536]{1,0:T(8,128)(2,1)} fusion(bf16[512,1536]{1,0:T(8,128)(2,1)} %get-tuple-element.41, bf16[256,1536]{1,0:T(8,128)(2,1)S(1)} %collective-permute-done.14, bf16[256,1536]{1,0:T(8,128)(2,1)S(1)} %collective-permute-done.13), kind=kLoop, calls=%fused_computation | loop fusion | flops 5505024 | bytes 4718592 | tf_op jit(solution)/shard_map/convert_element_type | solution.py:282
  124.9 12.6 %all-to-all-done.2 = bf16[4,8,48,768]{3,2,1,0:T(8,128)(2,1)S(1)} async-done(((bf16[4,8,48,768]{3,2,1,0:T(8,128)(2,1)}), bf16[4,8,48,768]{3,2,1,0:T(8,128)(2,1)S(1)}, u32[]{:S(2)}, u32[]{:S(2)}) %all-to-all-start.2) | async-done | bytes 2359328 | tf_op jit(solution)/shard_map/all_to_all | solution.py:269
  137.5 7.3 %all-to-all-start.1 = ((bf16[4,128,1536]{2,1,0:T(8,128)(2,1)}), bf16[4,128,1536]{2,1,0:T(8,128)(2,1)}, u32[]{:S(2)}, u32[]{:S(2)}) async-start(bf16[4,128,1536]{2,1,0:T(8,128)(2,1)} %bitcast.53), calls=%async_computation.1 | async-start | bytes 3145728 | tf_op jit(solution)/shard_map/all_to_all | solution.py:283
  145.2 5.3 %collective-permute-start.19 = (bf16[2,48,768]{2,1,0:T(8,128)(2,1)S(1)}, bf16[2,48,768]{2,1,0:T(8,128)(2,1)S(1)}, u32[]{:S(2)}, u32[]{:S(2)}) collective-permute-start(bf16[2,48,768]{2,1,0:T(8,128)(2,1)S(1)} %get-tuple-element.52), channel_id=1, source_target_pairs={{0,38},{2,0},{4,2},{6,4},{32,6},{34,32},{36,34},{38,36},{1,39},{3,... | collective-permute-start | bytes 442376 | tf_op jit(solution)/shard_map/ppermute | solution.py:29
  150.5 1.0 slice_bitcast_fusion.8
  151.5 0.6 collective-permute-start.17
  152.1 2.7 %collective-permute-start.16 = (bf16[48,768]{1,0:T(8,128)(2,1)S(1)}, bf16[48,768]{1,0:T(8,128)(2,1)S(1)}, u32[]{:S(2)}, u32[]{:S(2)}) collective-permute-start(bf16[48,768]{1,0:T(8,128)(2,1)S(1)} %get-tuple-element.55), channel_id=1, source_target_pairs={{0,24},{8,0},{16,8},{24,16},{1,25},{9,1},{17,9},{25,17},{2,26},{10... | collective-permute-start | bytes 221192 | tf_op jit(solution)/shard_map/ppermute | solution.py:29
  154.9 2.5 %collective-permute-done.18 = bf16[2,48,768]{2,1,0:T(8,128)(2,1)S(1)} collective-permute-done((bf16[2,48,768]{2,1,0:T(8,128)(2,1)S(1)}, bf16[2,48,768]{2,1,0:T(8,128)(2,1)S(1)}, u32[]{:S(2)}, u32[]{:S(2)}) %collective-permute-start.18) | collective-permute-done | bytes 147488 | tf_op jit(solution)/shard_map/ppermute | solution.py:29
  157.4 2.9 %collective-permute-done.15 = bf16[48,768]{1,0:T(8,128)(2,1)S(1)} collective-permute-done((bf16[48,768]{1,0:T(8,128)(2,1)S(1)}, bf16[48,768]{1,0:T(8,128)(2,1)S(1)}, u32[]{:S(2)}, u32[]{:S(2)}) %collective-permute-start.15) | collective-permute-done | bytes 73760 | tf_op jit(solution)/shard_map/ppermute | solution.py:29
  160.5 0.9 fusion.6
  161.4 1.9 %collective-permute-start.21 = (bf16[2,48,768]{2,1,0:T(8,128)(2,1)S(1)}, bf16[2,48,768]{2,1,0:T(8,128)(2,1)S(1)}, u32[]{:S(2)}, u32[]{:S(2)}) collective-permute-start(bf16[2,48,768]{2,1,0:T(8,128)(2,1)S(1)} %pad_maximum_fusion.5.after_ref), channel_id=1, source_target_pairs={{0,0},{2,64},{4,128},{6,192},{32,32},{34,96},{36,160},{38,224},{64... | collective-permute-start | bytes 442376 | tf_op jit(solution)/shard_map/ppermute | solution.py:39
  163.4 5.7 %collective-permute-start.22 = (bf16[48,768]{1,0:T(8,128)(2,1)S(1)}, bf16[48,768]{1,0:T(8,128)(2,1)S(1)}, u32[]{:S(2)}, u32[]{:S(2)}) collective-permute-start(bf16[48,768]{1,0:T(8,128)(2,1)S(1)} %get-tuple-element.57), channel_id=1, source_target_pairs={{0,32},{2,96},{4,160},{6,224},{32,0},{34,64},{36,128},{38,192},{64... | collective-permute-start | bytes 221192 | tf_op jit(solution)/shard_map/ppermute | solution.py:39
  169.1 3.1 %shard_map.98 = bf16[128,1536]{1,0:T(8,128)(2,1)} custom-call(bf16[128,1536]{1,0:T(8,128)(2,1)} %x_ref.3, f32[1536]{0:T(1024)} %gain_ref.3, bf16[128,1536]{1,0:T(8,128)(2,1)} %grad_ref.3, bf16[4,128,1536]{2,1,0:T(8,128)(2,1)} %all-to-all-done.1.dx_ref, bf16[2,48,768]{2,1,0:T(8,128)(2,1)} %copy-done.1), custom_call_target="tpu_custom_call" | custom-call | flops 3932160 | bytes 2752512 | tf_op jit(solution)/shard_map/pallas_call | solution.py:297
  172.2 2.4 %collective-permute-done.21 = bf16[2,48,768]{2,1,0:T(8,128)(2,1)S(1)} collective-permute-done((bf16[2,48,768]{2,1,0:T(8,128)(2,1)S(1)}, bf16[2,48,768]{2,1,0:T(8,128)(2,1)S(1)}, u32[]{:S(2)}, u32[]{:S(2)}) %collective-permute-start.21) | collective-permute-done | bytes 147488 | tf_op jit(solution)/shard_map/ppermute | solution.py:39
  174.6 0.7 convert_bitcast_fusion
  175.3 0.7 convert_add_fusion.1
  (48 shorter events, 2.0 us)
Async XLA Ops:
  7.2 74.4 %all-gather.3.cloned.1.call-start = ((), (), s32[]{:S(2)}) async-start(), calls=%async_computation.5 | async-start | bytes 7077888 | tf_op jit(solution)/shard_map/all_gather | solution.py:211
  8.1 22.4 %collective-permute-start.2 = (bf16[2,48,768]{2,1,0:T(8,128)(2,1)S(1)}, bf16[2,48,768]{2,1,0:T(8,128)(2,1)S(1)}, u32[]{:S(2)}, u32[]{:S(2)}) collective-permute-start(bf16[2,48,768]{2,1,0:T(8,128)(2,1)S(1)} %pad_maximum_fusion.2), channel_id=1, source_target_pairs={{0,32},{2,96},{4,160},{6,224},{32,0},{34,64},{36,128},{38,192},{64... | collective-permute-start | bytes 442376 | tf_op jit(solution)/shard_map/ppermute | solution.py:39
  14.3 16.3 %collective-permute-start.1 = (bf16[2,48,768]{2,1,0:T(8,128)(2,1)S(1)}, bf16[2,48,768]{2,1,0:T(8,128)(2,1)S(1)}, u32[]{:S(2)}, u32[]{:S(2)}) collective-permute-start(bf16[2,48,768]{2,1,0:T(8,128)(2,1)S(1)} %pad_maximum_fusion.2), channel_id=1, source_target_pairs={{0,0},{2,64},{4,128},{6,192},{32,32},{34,96},{36,160},{38,224},{64... | collective-permute-start | bytes 442376 | tf_op jit(solution)/shard_map/ppermute | solution.py:39
  20.3 10.3 %collective-permute-start = (f32[768]{0:T(1024)}, f32[768]{0:T(1024)S(1)}, u32[]{:S(2)}, u32[]{:S(2)}) collective-permute-start(f32[768]{0:T(1024)} %param.11), channel_id=1, source_target_pairs={{0,0},{2,64},{4,128},{6,192},{32,32},{34,96},{36,160},{38,224},{64... | collective-permute-start | bytes 9224 | tf_op jit(solution)/shard_map/ppermute | solution.py:39
  30.6 9.2 %collective-permute-start.5 = (bf16[2,48,768]{2,1,0:T(8,128)(2,1)S(1)}, bf16[2,48,768]{2,1,0:T(8,128)(2,1)S(1)}, u32[]{:S(2)}, u32[]{:S(2)}) collective-permute-start(bf16[2,48,768]{2,1,0:T(8,128)(2,1)S(1)} %pad_maximum_fusion.3), channel_id=1, source_target_pairs={{0,16},{8,24},{16,0},{24,8},{1,17},{9,25},{17,1},{25,9},{2,18},{10... | collective-permute-start | bytes 442376 | tf_op jit(solution)/shard_map/ppermute | solution.py:29
  33.8 7.3 %collective-permute-start.4 = (bf16[2,48,768]{2,1,0:T(8,128)(2,1)S(1)}, bf16[2,48,768]{2,1,0:T(8,128)(2,1)S(1)}, u32[]{:S(2)}, u32[]{:S(2)}) collective-permute-start(bf16[2,48,768]{2,1,0:T(8,128)(2,1)S(1)} %pad_maximum_fusion.3), channel_id=1, source_target_pairs={{0,24},{8,0},{16,8},{24,16},{1,25},{9,1},{17,9},{25,17},{2,26},{10... | collective-permute-start | bytes 442376 | tf_op jit(solution)/shard_map/ppermute | solution.py:29
  34.9 6.7 %collective-permute-start.3 = (bf16[2,48,768]{2,1,0:T(8,128)(2,1)S(1)}, bf16[2,48,768]{2,1,0:T(8,128)(2,1)S(1)}, u32[]{:S(2)}, u32[]{:S(2)}) collective-permute-start(bf16[2,48,768]{2,1,0:T(8,128)(2,1)S(1)} %pad_maximum_fusion.3), channel_id=1, source_target_pairs={{0,8},{8,16},{16,24},{24,0},{1,9},{9,17},{17,25},{25,1},{2,10},{10... | collective-permute-start | bytes 442376 | tf_op jit(solution)/shard_map/ppermute | solution.py:29
  35.8 11.4 %collective-permute-start.8 = (bf16[2,48,768]{2,1,0:T(8,128)(2,1)S(1)}, bf16[2,48,768]{2,1,0:T(8,128)(2,1)S(1)}, u32[]{:S(2)}, u32[]{:S(2)}) collective-permute-start(bf16[2,48,768]{2,1,0:T(8,128)(2,1)S(1)} %pad_maximum_fusion.4), channel_id=1, source_target_pairs={{0,4},{2,6},{4,32},{6,34},{32,36},{34,38},{36,0},{38,2},{1,5},{3,7... | collective-permute-start | bytes 442376 | tf_op jit(solution)/shard_map/ppermute | solution.py:29
  35.9 11.3 %collective-permute-start.7 = (bf16[2,48,768]{2,1,0:T(8,128)(2,1)S(1)}, bf16[2,48,768]{2,1,0:T(8,128)(2,1)S(1)}, u32[]{:S(2)}, u32[]{:S(2)}) collective-permute-start(bf16[2,48,768]{2,1,0:T(8,128)(2,1)S(1)} %pad_maximum_fusion.4), channel_id=1, source_target_pairs={{0,38},{2,0},{4,2},{6,4},{32,6},{34,32},{36,34},{38,36},{1,39},{3,... | collective-permute-start | bytes 442376 | tf_op jit(solution)/shard_map/ppermute | solution.py:29
  39.9 8.3 %collective-permute-start.6 = (bf16[2,48,768]{2,1,0:T(8,128)(2,1)S(1)}, bf16[2,48,768]{2,1,0:T(8,128)(2,1)S(1)}, u32[]{:S(2)}, u32[]{:S(2)}) collective-permute-start(bf16[2,48,768]{2,1,0:T(8,128)(2,1)S(1)} %pad_maximum_fusion.4), channel_id=1, source_target_pairs={{0,2},{2,4},{4,6},{6,32},{32,34},{34,36},{36,38},{38,0},{1,3},{3,5... | collective-permute-start | bytes 442376 | tf_op jit(solution)/shard_map/ppermute | solution.py:29
  49.8 31.7 %all-to-all-start = ((bf16[4,8,48,768]{3,2,1,0:T(8,128)(2,1)}), bf16[4,8,48,768]{3,2,1,0:T(8,128)(2,1)S(1)}, u32[]{:S(2)}, u32[]{:S(2)}) async-start(bf16[4,8,48,768]{3,2,1,0:T(8,128)(2,1)} %broadcast_in_dim.2), calls=%async_computation | async-start | bytes 4718592 | tf_op jit(solution)/shard_map/all_to_all | solution.py:222
  53.5 97.0 %reduce-scatter.2.cloned.1.call-start = ((), (), s32[]{:S(2)}) async-start(), calls=%async_computation.4 | async-start | bytes 2654208 | tf_op jit(solution)/shard_map/reduce_scatter | solution.py:252
  53.6 28.0 %copy-start.2 = (bf16[4,2,48,768]{3,2,1,0:T(8,128)(2,1)}, bf16[4,2,48,768]{3,2,1,0:T(8,128)(2,1)S(1)}, u32[]{:S(2)}) copy-start(bf16[4,2,48,768]{3,2,1,0:T(8,128)(2,1)S(1)} %pad_maximum_fusion.1.refs_2_) | copy-start | bytes 1769476
  53.6 13.8 %collective-permute-start.10 = (bf16[4,2,48,768]{3,2,1,0:T(8,128)(2,1)S(1)}, bf16[4,2,48,768]{3,2,1,0:T(8,128)(2,1)S(1)}, u32[]{:S(2)}, u32[]{:S(2)}) collective-permute-start(bf16[4,2,48,768]{3,2,1,0:T(8,128)(2,1)S(1)} %pad_maximum_fusion.1.refs_2_), channel_id=1, source_target_pairs={{0,38},{2,0},{4,2},{6,4},{32,6},{34,32},{36,34},{38,36},{1,39},{3,... | collective-permute-start | bytes 1769480 | tf_op jit(solution)/shard_map/ppermute | solution.py:29
  55.1 15.3 %collective-permute-start.9 = (bf16[4,2,48,768]{3,2,1,0:T(8,128)(2,1)S(1)}, bf16[4,2,48,768]{3,2,1,0:T(8,128)(2,1)S(1)}, u32[]{:S(2)}, u32[]{:S(2)}) collective-permute-start(bf16[4,2,48,768]{3,2,1,0:T(8,128)(2,1)S(1)} %pad_maximum_fusion.1.refs_2_), channel_id=1, source_target_pairs={{0,2},{2,4},{4,6},{6,32},{32,34},{34,36},{36,38},{38,0},{1,3},{3,5... | collective-permute-start | bytes 1769480 | tf_op jit(solution)/shard_map/ppermute | solution.py:29
  67.5 3.0 %copy-start.3 = (bf16[4,2,48,768]{3,2,1,0:T(8,128)(2,1)}, bf16[4,2,48,768]{3,2,1,0:T(8,128)(2,1)S(1)}, u32[]{:S(2)}) copy-start(bf16[4,2,48,768]{3,2,1,0:T(8,128)(2,1)S(1)} %collective-permute-done.10.refs_4_) | copy-start | bytes 1769476
  67.5 7.2 %collective-permute-start.12 = (bf16[2,2,48,768]{3,2,1,0:T(8,128)(2,1)S(1)}, bf16[2,2,48,768]{3,2,1,0:T(8,128)(2,1)S(1)}, u32[]{:S(2)}, u32[]{:S(2)}) collective-permute-start(bf16[2,2,48,768]{3,2,1,0:T(8,128)(2,1)S(1)} %slice.109), channel_id=1, source_target_pairs={{0,38},{2,0},{4,2},{6,4},{32,6},{34,32},{36,34},{38,36},{1,39},{3,... | collective-permute-start | bytes 884744 | tf_op jit(solution)/shard_map/ppermute | solution.py:29
  70.4 4.2 %copy-start.4 = (bf16[4,2,48,768]{3,2,1,0:T(8,128)(2,1)}, bf16[4,2,48,768]{3,2,1,0:T(8,128)(2,1)S(1)}, u32[]{:S(2)}) copy-start(bf16[4,2,48,768]{3,2,1,0:T(8,128)(2,1)S(1)} %collective-permute-done.9.refs_3_) | copy-start | bytes 1769476
  70.4 8.3 %collective-permute-start.11 = (bf16[2,2,48,768]{3,2,1,0:T(8,128)(2,1)S(1)}, bf16[2,2,48,768]{3,2,1,0:T(8,128)(2,1)}, u32[]{:S(2)}, u32[]{:S(2)}) collective-permute-start(bf16[2,2,48,768]{3,2,1,0:T(8,128)(2,1)S(1)} %slice.108), channel_id=1, source_target_pairs={{0,2},{2,4},{4,6},{6,32},{32,34},{34,36},{36,38},{38,0},{1,3},{3,5... | collective-permute-start | bytes 884744 | tf_op jit(solution)/shard_map/ppermute | solution.py:29
  74.7 6.9 %copy-start.5 = (bf16[2,2,48,768]{3,2,1,0:T(8,128)(2,1)}, bf16[2,2,48,768]{3,2,1,0:T(8,128)(2,1)S(1)}, u32[]{:S(2)}) copy-start(bf16[2,2,48,768]{3,2,1,0:T(8,128)(2,1)S(1)} %collective-permute-done.12.refs_6_) | copy-start | bytes 884740
  81.5 1.4 copy-start
  106.7 30.8 %all-to-all-start.2 = ((bf16[4,8,48,768]{3,2,1,0:T(8,128)(2,1)}), bf16[4,8,48,768]{3,2,1,0:T(8,128)(2,1)S(1)}, u32[]{:S(2)}, u32[]{:S(2)}) async-start(bf16[4,8,48,768]{3,2,1,0:T(8,128)(2,1)} %shard_map.96.refs_2_), calls=%async_computation.2 | async-start | bytes 4718592 | tf_op jit(solution)/shard_map/all_to_all | solution.py:269
  118.2 2.6 %collective-permute-start.13 = (bf16[256,1536]{1,0:T(8,128)(2,1)}, bf16[256,1536]{1,0:T(8,128)(2,1)S(1)}, u32[]{:S(2)}, u32[]{:S(2)}) collective-permute-start(bf16[256,1536]{1,0:T(8,128)(2,1)} %get-tuple-element.42), channel_id=1, source_target_pairs={{0,1},{1,0},{2,3},{3,2},{4,5},{5,4},{6,7},{7,6},{8,9},{9,8},{10,11... | collective-permute-start | bytes 2359304 | tf_op jit(solution)/shard_map/ppermute | solution.py:29
  118.3 3.6 %collective-permute-start.14 = (bf16[256,1536]{1,0:T(8,128)(2,1)}, bf16[256,1536]{1,0:T(8,128)(2,1)S(1)}, u32[]{:S(2)}, u32[]{:S(2)}) collective-permute-start(bf16[256,1536]{1,0:T(8,128)(2,1)} %get-tuple-element.43), channel_id=1, source_target_pairs={{0,1},{1,0},{2,3},{3,2},{4,5},{5,4},{6,7},{7,6},{8,9},{9,8},{10,11... | collective-permute-start | bytes 2359304 | tf_op jit(solution)/shard_map/ppermute | solution.py:29
  137.5 31.6 %all-to-all-start.1 = ((bf16[4,128,1536]{2,1,0:T(8,128)(2,1)}), bf16[4,128,1536]{2,1,0:T(8,128)(2,1)}, u32[]{:S(2)}, u32[]{:S(2)}) async-start(bf16[4,128,1536]{2,1,0:T(8,128)(2,1)} %bitcast.53), calls=%async_computation.1 | async-start | bytes 3145728 | tf_op jit(solution)/shard_map/all_to_all | solution.py:283
  145.1 9.7 %collective-permute-start.20 = (bf16[2,48,768]{2,1,0:T(8,128)(2,1)S(1)}, bf16[2,48,768]{2,1,0:T(8,128)(2,1)S(1)}, u32[]{:S(2)}, u32[]{:S(2)}) collective-permute-start(bf16[2,48,768]{2,1,0:T(8,128)(2,1)S(1)} %get-tuple-element.51), channel_id=1, source_target_pairs={{0,4},{2,6},{4,32},{6,34},{32,36},{34,38},{36,0},{38,2},{1,5},{3,7... | collective-permute-start | bytes 442376 | tf_op jit(solution)/shard_map/ppermute | solution.py:29
  145.2 9.7 %collective-permute-start.19 = (bf16[2,48,768]{2,1,0:T(8,128)(2,1)S(1)}, bf16[2,48,768]{2,1,0:T(8,128)(2,1)S(1)}, u32[]{:S(2)}, u32[]{:S(2)}) collective-permute-start(bf16[2,48,768]{2,1,0:T(8,128)(2,1)S(1)} %get-tuple-element.52), channel_id=1, source_target_pairs={{0,38},{2,0},{4,2},{6,4},{32,6},{34,32},{36,34},{38,36},{1,39},{3,... | collective-permute-start | bytes 442376 | tf_op jit(solution)/shard_map/ppermute | solution.py:29
  150.5 6.9 %collective-permute-start.18 = (bf16[2,48,768]{2,1,0:T(8,128)(2,1)S(1)}, bf16[2,48,768]{2,1,0:T(8,128)(2,1)S(1)}, u32[]{:S(2)}, u32[]{:S(2)}) collective-permute-start(bf16[2,48,768]{2,1,0:T(8,128)(2,1)S(1)} %get-tuple-element.53), channel_id=1, source_target_pairs={{0,2},{2,4},{4,6},{6,32},{32,34},{34,36},{36,38},{38,0},{1,3},{3,5... | collective-permute-start | bytes 442376 | tf_op jit(solution)/shard_map/ppermute | solution.py:29
  151.5 6.0 %collective-permute-start.17 = (bf16[48,768]{1,0:T(8,128)(2,1)S(1)}, bf16[48,768]{1,0:T(8,128)(2,1)S(1)}, u32[]{:S(2)}, u32[]{:S(2)}) collective-permute-start(bf16[48,768]{1,0:T(8,128)(2,1)S(1)} %get-tuple-element.54), channel_id=1, source_target_pairs={{0,16},{8,24},{16,0},{24,8},{1,17},{9,25},{17,1},{25,9},{2,18},{10... | collective-permute-start | bytes 221192 | tf_op jit(solution)/shard_map/ppermute | solution.py:29
  152.1 5.3 %collective-permute-start.16 = (bf16[48,768]{1,0:T(8,128)(2,1)S(1)}, bf16[48,768]{1,0:T(8,128)(2,1)S(1)}, u32[]{:S(2)}, u32[]{:S(2)}) collective-permute-start(bf16[48,768]{1,0:T(8,128)(2,1)S(1)} %get-tuple-element.55), channel_id=1, source_target_pairs={{0,24},{8,0},{16,8},{24,16},{1,25},{9,1},{17,9},{25,17},{2,26},{10... | collective-permute-start | bytes 221192 | tf_op jit(solution)/shard_map/ppermute | solution.py:29
  154.8 5.6 %collective-permute-start.15 = (bf16[48,768]{1,0:T(8,128)(2,1)S(1)}, bf16[48,768]{1,0:T(8,128)(2,1)S(1)}, u32[]{:S(2)}, u32[]{:S(2)}) collective-permute-start(bf16[48,768]{1,0:T(8,128)(2,1)S(1)} %get-tuple-element.56), channel_id=1, source_target_pairs={{0,8},{8,16},{16,24},{24,0},{1,9},{9,17},{17,25},{25,1},{2,10},{10... | collective-permute-start | bytes 221192 | tf_op jit(solution)/shard_map/ppermute | solution.py:29
  161.4 7.6 %copy-start.1 = (bf16[2,48,768]{2,1,0:T(8,128)(2,1)}, bf16[2,48,768]{2,1,0:T(8,128)(2,1)S(1)}, u32[]{:S(2)}) copy-start(bf16[2,48,768]{2,1,0:T(8,128)(2,1)S(1)} %pad_maximum_fusion.5.after_ref) | copy-start | bytes 442372
  161.4 13.2 %collective-permute-start.21 = (bf16[2,48,768]{2,1,0:T(8,128)(2,1)S(1)}, bf16[2,48,768]{2,1,0:T(8,128)(2,1)S(1)}, u32[]{:S(2)}, u32[]{:S(2)}) collective-permute-start(bf16[2,48,768]{2,1,0:T(8,128)(2,1)S(1)} %pad_maximum_fusion.5.after_ref), channel_id=1, source_target_pairs={{0,0},{2,64},{4,128},{6,192},{32,32},{34,96},{36,160},{38,224},{64... | collective-permute-start | bytes 442376 | tf_op jit(solution)/shard_map/ppermute | solution.py:39
  163.4 11.9 %collective-permute-start.22 = (bf16[48,768]{1,0:T(8,128)(2,1)S(1)}, bf16[48,768]{1,0:T(8,128)(2,1)S(1)}, u32[]{:S(2)}, u32[]{:S(2)}) collective-permute-start(bf16[48,768]{1,0:T(8,128)(2,1)S(1)} %get-tuple-element.57), channel_id=1, source_target_pairs={{0,32},{2,96},{4,160},{6,224},{32,0},{34,64},{36,128},{38,192},{64... | collective-permute-start | bytes 221192 | tf_op jit(solution)/shard_map/ppermute | solution.py:39
Sparse Core Ops, SparseCore 0:
  30.7 41.7 all-gather.2
  99.2 41.4 reduce-scatter.1

commit v6 on v4

--- a/solution.py
+++ b/solution.py
@@ -301,7 +301,7 @@
         out_specs=VM,
         compiler_params=PARAMS,
         cost_estimate=cost(20 * TD * D, 14 * TD * D),
-    )(inputs, norm_gain, grad_out, dx_y, sums)
+    )(inputs, norm_gain, grad_out, dx_y, far)
     return grad_in, grad_w_in, grad_w_out
 
 

time: 179 us -> 184 us (1.028)
  waiting for transfers between devices: 50.3 us -> 53.6 us
    ppermute x5, waiting for transfers between devices: 3.23 us -> 6.55 us  [turn(): return lax.ppermute(value, ('y', 'zh', 'zl'), pairs)]
  transfers between devices with their start and end apart: 32 -> 32, of which waited for: 18 -> 18; matrix products, arithmetic and copies ran while one was open for 5% -> 5% of each run, Pallas kernels for 12% -> 11%
where the time goes in v6:
time: 184 us; the launch traced here: 183 us
  starting transfers between devices  64.4 us (35%)
  waiting for transfers between devices  53.6 us (29%)
  Pallas kernels  37 us (20%)
  between operations  14.3 us (8%)
  other arithmetic  8.24 us (4%)
  local copies, waits for them, and re-layouts  5.29 us (3%)
    ppermute x22, waiting for transfers between devices, shift(): return lax.ppermute(value, axis, [(i, (i + by) % n) for i in range(n)])  38.1 us
    ppermute x22, starting transfers between devices, shift(): return lax.ppermute(value, axis, [(i, (i + by) % n) for i in range(n)])  24.8 us
    ppermute x5, starting transfers between devices, turn(): return lax.ppermute(value, ('y', 'zh', 'zl'), pairs)  24.3 us
    pallas_call x1, Pallas kernels, on_device(): pl.pallas_call(main_kernel, out_shape=(jax.ShapeDtypeStruct((1024, FD), B...  16.2 us
    all_to_all x1, waiting for transfers between devices, on_device(): dws = lax.all_to_all(dws, 'x', 0, 0, tiled=True)  8.89 us
    pallas_call x1, Pallas kernels, on_device(): pl.pallas_call(dx_kernel, out_shape=[jax.ShapeDtypeStruct((512, D), BF)]...  7.78 us
    pallas_call x1, Pallas kernels, on_device(): pl.pallas_call(dwin_kernel, out_shape=jax.ShapeDtypeStruct((4, 8, RB, FD)...  7.55 us
    ppermute x5, waiting for transfers between devices, turn(): return lax.ppermute(value, ('y', 'zh', 'zl'), pairs)  6.55 us
  transfers between devices with their start and end apart: 32, of which 18 were waited for; matrix products, arithmetic and copies ran while one was open for 5% of the time, Pallas kernels for 11%

profile of v6, /device:TPU:16, one launch (start us, length us, event | category | flops | bytes accessed | tf_op | source)
XLA Modules:
  0.0 182.7 jit_solution(9989272321981814391)
XLA Ops:
  7.2 0.9 pad_maximum_fusion.2
  8.1 5.0 %collective-permute-start.1 = (bf16[2,48,768]{2,1,0:T(8,128)(2,1)S(1)}, bf16[2,48,768]{2,1,0:T(8,128)(2,1)S(1)}, u32[]{:S(2)}, u32[]{:S(2)}) collective-permute-start(bf16[2,48,768]{2,1,0:T(8,128)(2,1)S(1)} %pad_maximum_fusion.2), channel_id=1, source_target_pairs={{0,0},{2,64},{4,128},{6,192},{32,32},{34,96},{36,160},{38,224},{64... | collective-permute-start | bytes 442376 | tf_op jit(solution)/shard_map/ppermute | solution.py:39
  13.1 7.2 %collective-permute-start.2 = (bf16[48,768]{1,0:T(8,128)(2,1)}, bf16[48,768]{1,0:T(8,128)(2,1)S(1)}, u32[]{:S(2)}, u32[]{:S(2)}) collective-permute-start(bf16[48,768]{1,0:T(8,128)(2,1)} %param.10), channel_id=1, source_target_pairs={{0,32},{2,96},{4,160},{6,224},{32,0},{34,64},{36,128},{38,192},{64... | collective-permute-start | bytes 221192 | tf_op jit(solution)/shard_map/ppermute | solution.py:39
  20.3 3.1 %collective-permute-start = (f32[768]{0:T(1024)}, f32[768]{0:T(1024)S(1)}, u32[]{:S(2)}, u32[]{:S(2)}) collective-permute-start(f32[768]{0:T(1024)} %param.11), channel_id=1, source_target_pairs={{0,0},{2,64},{4,128},{6,192},{32,32},{34,96},{36,160},{38,224},{64... | collective-permute-start | bytes 9224 | tf_op jit(solution)/shard_map/ppermute | solution.py:39
  24.1 2.3 %shard_map.94 = bf16[2,128,1536]{2,1,0:T(8,128)(2,1)} custom-call(bf16[128,1536]{1,0:T(8,128)(2,1)} %x_ref.3, f32[1536]{0:T(1024)} %gain_ref.3, f32[1536]{0:T(1024)} %bias_ref.1, bf16[128,1536]{1,0:T(8,128)(2,1)} %grad_ref.3), custom_call_target="tpu_custom_call" | custom-call | flops 1966080 | bytes 1572864 | tf_op jit(solution)/shard_map/pallas_call | solution.py:199
  26.5 2.9 %collective-permute-done = f32[768]{0:T(1024)S(1)} collective-permute-done((f32[768]{0:T(1024)}, f32[768]{0:T(1024)S(1)}, u32[]{:S(2)}, u32[]{:S(2)}) %collective-permute-start) | collective-permute-done | bytes 3104 | tf_op jit(solution)/shard_map/ppermute | solution.py:39
  29.4 3.1 %collective-permute-start.5 = (bf16[48,768]{1,0:T(8,128)(2,1)S(1)}, bf16[48,768]{1,0:T(8,128)(2,1)S(1)}, u32[]{:S(2)}, u32[]{:S(2)}) collective-permute-start(bf16[48,768]{1,0:T(8,128)(2,1)S(1)} %get-tuple-element.35), channel_id=1, source_target_pairs={{0,16},{8,24},{16,0},{24,8},{1,17},{9,25},{17,1},{25,9},{2,18},{10... | collective-permute-start | bytes 221192 | tf_op jit(solution)/shard_map/ppermute | solution.py:29
  32.6 2.8 %collective-permute-start.7 = (bf16[2,48,768]{2,1,0:T(8,128)(2,1)S(1)}, bf16[2,48,768]{2,1,0:T(8,128)(2,1)S(1)}, u32[]{:S(2)}, u32[]{:S(2)}) collective-permute-start(bf16[2,48,768]{2,1,0:T(8,128)(2,1)S(1)} %pad_maximum_fusion.3), channel_id=1, source_target_pairs={{0,38},{2,0},{4,2},{6,4},{32,6},{34,32},{36,34},{38,36},{1,39},{3,... | collective-permute-start | bytes 442376 | tf_op jit(solution)/shard_map/ppermute | solution.py:29
  35.4 1.1 collective-permute-start.4
  37.4 2.3 %collective-permute-done.4 = bf16[48,768]{1,0:T(8,128)(2,1)S(1)} collective-permute-done((bf16[48,768]{1,0:T(8,128)(2,1)S(1)}, bf16[48,768]{1,0:T(8,128)(2,1)S(1)}, u32[]{:S(2)}, u32[]{:S(2)}) %collective-permute-start.4) | collective-permute-done | bytes 73760 | tf_op jit(solution)/shard_map/ppermute | solution.py:29
  39.7 2.4 %collective-permute-done.3 = bf16[48,768]{1,0:T(8,128)(2,1)S(1)} collective-permute-done((bf16[48,768]{1,0:T(8,128)(2,1)S(1)}, bf16[48,768]{1,0:T(8,128)(2,1)S(1)}, u32[]{:S(2)}, u32[]{:S(2)}) %collective-permute-start.3) | collective-permute-done | bytes 73760 | tf_op jit(solution)/shard_map/ppermute | solution.py:29
  42.1 1.2 collective-permute-done.8
  43.3 1.0 collective-permute-done.6
  44.3 1.7 broadcast_in_dim.2
  46.0 3.6 %all-to-all-start = ((bf16[4,8,48,768]{3,2,1,0:T(8,128)(2,1)}), bf16[4,8,48,768]{3,2,1,0:T(8,128)(2,1)S(1)}, u32[]{:S(2)}, u32[]{:S(2)}) async-start(bf16[4,8,48,768]{3,2,1,0:T(8,128)(2,1)} %broadcast_in_dim.2), calls=%async_computation | async-start | bytes 4718592 | tf_op jit(solution)/shard_map/all_to_all | solution.py:219
  49.7 1.2 collective-permute-start.10
  50.9 0.9 collective-permute-start.9
  51.9 6.5 %collective-permute-done.10.refs_4_ = bf16[4,48,768]{2,1,0:T(8,128)(2,1)S(1)} collective-permute-done((bf16[4,48,768]{2,1,0:T(8,128)(2,1)S(1)}, bf16[4,48,768]{2,1,0:T(8,128)(2,1)S(1)}, u32[]{:S(2)}, u32[]{:S(2)}) %collective-permute-start.10) | collective-permute-done | bytes 294944 | tf_op jit(solution)/shard_map/ppermute | solution.py:29
  58.3 1.5 collective-permute-start.12
  60.3 5.6 %collective-permute-done.12.refs_6_ = bf16[4,48,768]{2,1,0:T(8,128)(2,1)S(1)} collective-permute-done((bf16[4,48,768]{2,1,0:T(8,128)(2,1)S(1)}, bf16[4,48,768]{2,1,0:T(8,128)(2,1)S(1)}, u32[]{:S(2)}, u32[]{:S(2)}) %collective-permute-start.12) | collective-permute-done | bytes 294944 | tf_op jit(solution)/shard_map/ppermute | solution.py:29
  66.0 1.8 collective-permute-start.14
  68.1 5.0 %collective-permute-done.14.refs_8_ = bf16[4,48,768]{2,1,0:T(8,128)(2,1)S(1)} collective-permute-done((bf16[4,48,768]{2,1,0:T(8,128)(2,1)S(1)}, bf16[4,48,768]{2,1,0:T(8,128)(2,1)S(1)}, u32[]{:S(2)}, u32[]{:S(2)}) %collective-permute-start.14) | collective-permute-done | bytes 294944 | tf_op jit(solution)/shard_map/ppermute | solution.py:29
  73.1 2.7 %collective-permute-start.16 = (bf16[2,48,768]{2,1,0:T(8,128)(2,1)S(1)}, bf16[2,48,768]{2,1,0:T(8,128)(2,1)S(1)}, u32[]{:S(2)}, u32[]{:S(2)}) collective-permute-start(bf16[2,48,768]{2,1,0:T(8,128)(2,1)S(1)} %slice.104), channel_id=1, source_target_pairs={{0,38},{2,0},{4,2},{6,4},{32,6},{34,32},{36,34},{38,36},{1,39},{3,... | collective-permute-start | bytes 442376 | tf_op jit(solution)/shard_map/ppermute | solution.py:29
  76.7 1.8 collective-permute-done.16.refs_10_
  78.5 4.1 %collective-permute-done.15.refs_9_ = bf16[2,48,768]{2,1,0:T(8,128)(2,1)} collective-permute-done((bf16[2,48,768]{2,1,0:T(8,128)(2,1)S(1)}, bf16[2,48,768]{2,1,0:T(8,128)(2,1)}, u32[]{:S(2)}, u32[]{:S(2)}) %collective-permute-start.15) | collective-permute-done | bytes 147488 | tf_op jit(solution)/shard_map/ppermute | solution.py:29
  82.6 1.3 copy-done
  83.9 16.2 %shard_map.95 = (bf16[1024,768]{1,0:T(8,128)(2,1)}, bf16[8,4,48,768]{3,2,1,0:T(8,128)(2,1)}) custom-call(s32[3]{0:T(128)} %pad_add_fusion.me, bf16[8,2,128,1536]{3,2,1,0:T(8,128)(2,1)} %bitcast.54, bf16[4,8,48,768]{3,2,1,0:T(8,128)(2,1)} %copy-done, bf16[4,48,768]{2,1,0:T(8,128)(2,1)} %copy-done.2, bf16[4,48,768]{2,1,0:T(8,128)(2,1)} %copy-done.6, ...), custom_call_target="tpu_custom_call" | custom-call | flops 7247757312 | bytes 20971520 | tf_op jit(solution)/shard_map/pallas_call | solution.py:228
  100.1 7.6 %shard_map.96.refs_2_ = bf16[4,8,48,768]{3,2,1,0:T(8,128)(2,1)} custom-call(s32[3]{0:T(128)} %pad_add_fusion.me, bf16[8,2,128,1536]{3,2,1,0:T(8,128)(2,1)} %bitcast.55, bf16[1024,768]{1,0:T(8,128)(2,1)} %get-tuple-element.40.refs_1_.refs_0_), custom_call_target="tpu_custom_call" | custom-call | flops 2415919104 | bytes 7340032 | tf_op jit(solution)/shard_map/pallas_call | solution.py:254
  107.7 5.1 %all-to-all-start.2 = ((bf16[4,8,48,768]{3,2,1,0:T(8,128)(2,1)}), bf16[4,8,48,768]{3,2,1,0:T(8,128)(2,1)S(1)}, u32[]{:S(2)}, u32[]{:S(2)}) async-start(bf16[4,8,48,768]{3,2,1,0:T(8,128)(2,1)} %shard_map.96.refs_2_), calls=%async_computation.2 | async-start | bytes 4718592 | tf_op jit(solution)/shard_map/all_to_all | solution.py:269
  112.8 7.8 %shard_map.97 = (bf16[512,1536]{1,0:T(8,128)(2,1)}, bf16[256,1536]{1,0:T(8,128)(2,1)}, bf16[256,1536]{1,0:T(8,128)(2,1)}) custom-call(s32[3]{0:T(128)} %pad_add_fusion.me, bf16[1024,768]{1,0:T(8,128)(2,1)} %get-tuple-element.40.refs_1_.refs_0_, bf16[4,8,48,768]{3,2,1,0:T(8,128)(2,1)} %copy-done, bf16[4,8,48,768]{3,2,1,0:T(8,128)(2,1)} %shard_map.96.refs_2_), custom_call_target="tpu_custom_call" | custom-call | flops 2415919104 | bytes 7340032 | tf_op jit(solution)/shard_map/pallas_call | solution.py:271
  121.2 2.0 %collective-permute-done.17 = bf16[256,1536]{1,0:T(8,128)(2,1)S(1)} collective-permute-done((bf16[256,1536]{1,0:T(8,128)(2,1)}, bf16[256,1536]{1,0:T(8,128)(2,1)S(1)}, u32[]{:S(2)}, u32[]{:S(2)}) %collective-permute-start.17) | collective-permute-done | bytes 786464 | tf_op jit(solution)/shard_map/ppermute | solution.py:29
  123.2 1.1 collective-permute-done.18
  124.3 3.0 %add_convert_fusion = bf16[512,1536]{1,0:T(8,128)(2,1)} fusion(bf16[512,1536]{1,0:T(8,128)(2,1)} %get-tuple-element.41, bf16[256,1536]{1,0:T(8,128)(2,1)S(1)} %collective-permute-done.18, bf16[256,1536]{1,0:T(8,128)(2,1)S(1)} %collective-permute-done.17), kind=kLoop, calls=%fused_computation | loop fusion | flops 5505024 | bytes 4718592 | tf_op jit(solution)/shard_map/convert_element_type | solution.py:282
  127.3 8.9 %all-to-all-done.2 = bf16[4,8,48,768]{3,2,1,0:T(8,128)(2,1)S(1)} async-done(((bf16[4,8,48,768]{3,2,1,0:T(8,128)(2,1)}), bf16[4,8,48,768]{3,2,1,0:T(8,128)(2,1)S(1)}, u32[]{:S(2)}, u32[]{:S(2)}) %all-to-all-start.2) | async-done | bytes 2359328 | tf_op jit(solution)/shard_map/all_to_all | solution.py:269
  136.1 6.4 %all-to-all-start.1 = ((bf16[4,128,1536]{2,1,0:T(8,128)(2,1)}), bf16[4,128,1536]{2,1,0:T(8,128)(2,1)}, u32[]{:S(2)}, u32[]{:S(2)}) async-start(bf16[4,128,1536]{2,1,0:T(8,128)(2,1)} %bitcast.56), calls=%async_computation.1 | async-start | bytes 3145728 | tf_op jit(solution)/shard_map/all_to_all | solution.py:283
  143.0 1.8 collective-permute-start.23
  145.1 1.0 slice_bitcast_fusion.8
  146.1 3.0 %collective-permute-start.21 = (bf16[48,768]{1,0:T(8,128)(2,1)S(1)}, bf16[48,768]{1,0:T(8,128)(2,1)S(1)}, u32[]{:S(2)}, u32[]{:S(2)}) collective-permute-start(bf16[48,768]{1,0:T(8,128)(2,1)S(1)} %get-tuple-element.54), channel_id=1, source_target_pairs={{0,16},{8,24},{16,0},{24,8},{1,17},{9,25},{17,1},{25,9},{2,18},{10... | collective-permute-start | bytes 221192 | tf_op jit(solution)/shard_map/ppermute | solution.py:29
  149.1 1.2 collective-permute-start.20
  151.1 0.9 collective-permute-done.22
  152.0 1.4 collective-permute-done.20
  153.5 2.6 %collective-permute-done.19 = bf16[48,768]{1,0:T(8,128)(2,1)S(1)} collective-permute-done((bf16[48,768]{1,0:T(8,128)(2,1)S(1)}, bf16[48,768]{1,0:T(8,128)(2,1)S(1)}, u32[]{:S(2)}, u32[]{:S(2)}) %collective-permute-start.19) | collective-permute-done | bytes 73760 | tf_op jit(solution)/shard_map/ppermute | solution.py:29
  156.2 0.9 fusion.6
  157.2 3.1 %collective-permute-start.26 = (bf16[2,48,768]{2,1,0:T(8,128)(2,1)S(1)}, bf16[2,48,768]{2,1,0:T(8,128)(2,1)S(1)}, u32[]{:S(2)}, u32[]{:S(2)}) collective-permute-start(bf16[2,48,768]{2,1,0:T(8,128)(2,1)S(1)} %pad_maximum_fusion.4), channel_id=1, source_target_pairs={{0,0},{2,64},{4,128},{6,192},{32,32},{34,96},{36,160},{38,224},{64... | collective-permute-start | bytes 442376 | tf_op jit(solution)/shard_map/ppermute | solution.py:39
  160.3 5.9 %collective-permute-start.25 = (bf16[48,768]{1,0:T(8,128)(2,1)S(1)}, bf16[48,768]{1,0:T(8,128)(2,1)S(1)}, u32[]{:S(2)}, u32[]{:S(2)}) collective-permute-start(bf16[48,768]{1,0:T(8,128)(2,1)S(1)} %get-tuple-element.58), channel_id=1, source_target_pairs={{0,32},{2,96},{4,160},{6,224},{32,0},{34,64},{36,128},{38,192},{64... | collective-permute-start | bytes 221192 | tf_op jit(solution)/shard_map/ppermute | solution.py:39
  166.2 3.7 %collective-permute-done.25.after_ref = bf16[48,768]{1,0:T(8,128)(2,1)S(1)} collective-permute-done((bf16[48,768]{1,0:T(8,128)(2,1)S(1)}, bf16[48,768]{1,0:T(8,128)(2,1)S(1)}, u32[]{:S(2)}, u32[]{:S(2)}) %collective-permute-start.25) | collective-permute-done | bytes 73760 | tf_op jit(solution)/shard_map/ppermute | solution.py:39
  170.5 3.1 %shard_map.98 = bf16[128,1536]{1,0:T(8,128)(2,1)} custom-call(bf16[128,1536]{1,0:T(8,128)(2,1)} %x_ref.3, f32[1536]{0:T(1024)} %gain_ref.3, bf16[128,1536]{1,0:T(8,128)(2,1)} %grad_ref.3, bf16[4,128,1536]{2,1,0:T(8,128)(2,1)} %all-to-all-done.1.dx_ref, bf16[48,768]{1,0:T(8,128)(2,1)} %copy-done.1), custom_call_target="tpu_custom_call" | custom-call | flops 3932160 | bytes 2752512 | tf_op jit(solution)/shard_map/pallas_call | solution.py:297
  174.3 1.6 convert_add_fusion.1
  (63 shorter events, 7.2 us)
Async XLA Ops:
  7.2 75.4 %all-gather.3.cloned.1.call-start = ((), (), s32[]{:S(2)}) async-start(), calls=%async_computation.5 | async-start | bytes 7077888 | tf_op jit(solution)/shard_map/all_gather | solution.py:209
  8.1 21.2 %collective-permute-start.1 = (bf16[2,48,768]{2,1,0:T(8,128)(2,1)S(1)}, bf16[2,48,768]{2,1,0:T(8,128)(2,1)S(1)}, u32[]{:S(2)}, u32[]{:S(2)}) collective-permute-start(bf16[2,48,768]{2,1,0:T(8,128)(2,1)S(1)} %pad_maximum_fusion.2), channel_id=1, source_target_pairs={{0,0},{2,64},{4,128},{6,192},{32,32},{34,96},{36,160},{38,224},{64... | collective-permute-start | bytes 442376 | tf_op jit(solution)/shard_map/ppermute | solution.py:39
  13.1 16.2 %collective-permute-start.2 = (bf16[48,768]{1,0:T(8,128)(2,1)}, bf16[48,768]{1,0:T(8,128)(2,1)S(1)}, u32[]{:S(2)}, u32[]{:S(2)}) collective-permute-start(bf16[48,768]{1,0:T(8,128)(2,1)} %param.10), channel_id=1, source_target_pairs={{0,32},{2,96},{4,160},{6,224},{32,0},{34,64},{36,128},{38,192},{64... | collective-permute-start | bytes 221192 | tf_op jit(solution)/shard_map/ppermute | solution.py:39
  20.3 9.0 %collective-permute-start = (f32[768]{0:T(1024)}, f32[768]{0:T(1024)S(1)}, u32[]{:S(2)}, u32[]{:S(2)}) collective-permute-start(f32[768]{0:T(1024)} %param.11), channel_id=1, source_target_pairs={{0,0},{2,64},{4,128},{6,192},{32,32},{34,96},{36,160},{38,224},{64... | collective-permute-start | bytes 9224 | tf_op jit(solution)/shard_map/ppermute | solution.py:39
  29.4 7.2 %collective-permute-start.5 = (bf16[48,768]{1,0:T(8,128)(2,1)S(1)}, bf16[48,768]{1,0:T(8,128)(2,1)S(1)}, u32[]{:S(2)}, u32[]{:S(2)}) collective-permute-start(bf16[48,768]{1,0:T(8,128)(2,1)S(1)} %get-tuple-element.35), channel_id=1, source_target_pairs={{0,16},{8,24},{16,0},{24,8},{1,17},{9,25},{17,1},{25,9},{2,18},{10... | collective-permute-start | bytes 221192 | tf_op jit(solution)/shard_map/ppermute | solution.py:29
  32.5 10.8 %collective-permute-start.8 = (bf16[2,48,768]{2,1,0:T(8,128)(2,1)S(1)}, bf16[2,48,768]{2,1,0:T(8,128)(2,1)S(1)}, u32[]{:S(2)}, u32[]{:S(2)}) collective-permute-start(bf16[2,48,768]{2,1,0:T(8,128)(2,1)S(1)} %pad_maximum_fusion.3), channel_id=1, source_target_pairs={{0,4},{2,6},{4,32},{6,34},{32,36},{34,38},{36,0},{38,2},{1,5},{3,7... | collective-permute-start | bytes 442376 | tf_op jit(solution)/shard_map/ppermute | solution.py:29
  32.6 10.7 %collective-permute-start.7 = (bf16[2,48,768]{2,1,0:T(8,128)(2,1)S(1)}, bf16[2,48,768]{2,1,0:T(8,128)(2,1)S(1)}, u32[]{:S(2)}, u32[]{:S(2)}) collective-permute-start(bf16[2,48,768]{2,1,0:T(8,128)(2,1)S(1)} %pad_maximum_fusion.3), channel_id=1, source_target_pairs={{0,38},{2,0},{4,2},{6,4},{32,6},{34,32},{36,34},{38,36},{1,39},{3,... | collective-permute-start | bytes 442376 | tf_op jit(solution)/shard_map/ppermute | solution.py:29
  35.4 8.9 %collective-permute-start.6 = (bf16[2,48,768]{2,1,0:T(8,128)(2,1)S(1)}, bf16[2,48,768]{2,1,0:T(8,128)(2,1)S(1)}, u32[]{:S(2)}, u32[]{:S(2)}) collective-permute-start(bf16[2,48,768]{2,1,0:T(8,128)(2,1)S(1)} %pad_maximum_fusion.3), channel_id=1, source_target_pairs={{0,2},{2,4},{4,6},{6,32},{32,34},{34,36},{36,38},{38,0},{1,3},{3,5... | collective-permute-start | bytes 442376 | tf_op jit(solution)/shard_map/ppermute | solution.py:29
  35.4 4.4 %collective-permute-start.4 = (bf16[48,768]{1,0:T(8,128)(2,1)S(1)}, bf16[48,768]{1,0:T(8,128)(2,1)S(1)}, u32[]{:S(2)}, u32[]{:S(2)}) collective-permute-start(bf16[48,768]{1,0:T(8,128)(2,1)S(1)} %get-tuple-element.35), channel_id=1, source_target_pairs={{0,24},{8,0},{16,8},{24,16},{1,25},{9,1},{17,9},{25,17},{2,26},{10... | collective-permute-start | bytes 221192 | tf_op jit(solution)/shard_map/ppermute | solution.py:29
  36.5 5.6 %collective-permute-start.3 = (bf16[48,768]{1,0:T(8,128)(2,1)S(1)}, bf16[48,768]{1,0:T(8,128)(2,1)S(1)}, u32[]{:S(2)}, u32[]{:S(2)}) collective-permute-start(bf16[48,768]{1,0:T(8,128)(2,1)S(1)} %get-tuple-element.35), channel_id=1, source_target_pairs={{0,8},{8,16},{16,24},{24,0},{1,9},{9,17},{17,25},{25,1},{2,10},{10... | collective-permute-start | bytes 221192 | tf_op jit(solution)/shard_map/ppermute | solution.py:29
  46.0 36.5 %all-to-all-start = ((bf16[4,8,48,768]{3,2,1,0:T(8,128)(2,1)}), bf16[4,8,48,768]{3,2,1,0:T(8,128)(2,1)S(1)}, u32[]{:S(2)}, u32[]{:S(2)}) async-start(bf16[4,8,48,768]{3,2,1,0:T(8,128)(2,1)} %broadcast_in_dim.2), calls=%async_computation | async-start | bytes 4718592 | tf_op jit(solution)/shard_map/all_to_all | solution.py:219
  49.6 95.5 %reduce-scatter.2.cloned.1.call-start = ((), (), s32[]{:S(2)}) async-start(), calls=%async_computation.4 | async-start | bytes 2654208 | tf_op jit(solution)/shard_map/reduce_scatter | solution.py:252
  49.7 32.8 %copy-start.2 = (bf16[4,48,768]{2,1,0:T(8,128)(2,1)}, bf16[4,48,768]{2,1,0:T(8,128)(2,1)S(1)}, u32[]{:S(2)}) copy-start(bf16[4,48,768]{2,1,0:T(8,128)(2,1)S(1)} %pad_maximum_fusion.1.refs_2_) | copy-start | bytes 884740
  49.7 8.6 %collective-permute-start.10 = (bf16[4,48,768]{2,1,0:T(8,128)(2,1)S(1)}, bf16[4,48,768]{2,1,0:T(8,128)(2,1)S(1)}, u32[]{:S(2)}, u32[]{:S(2)}) collective-permute-start(bf16[4,48,768]{2,1,0:T(8,128)(2,1)S(1)} %pad_maximum_fusion.1.refs_2_), channel_id=1, source_target_pairs={{0,38},{2,0},{4,2},{6,4},{32,6},{34,32},{36,34},{38,36},{1,39},{3,... | collective-permute-start | bytes 884744 | tf_op jit(solution)/shard_map/ppermute | solution.py:29
  50.9 8.9 %collective-permute-start.9 = (bf16[4,48,768]{2,1,0:T(8,128)(2,1)S(1)}, bf16[4,48,768]{2,1,0:T(8,128)(2,1)S(1)}, u32[]{:S(2)}, u32[]{:S(2)}) collective-permute-start(bf16[4,48,768]{2,1,0:T(8,128)(2,1)S(1)} %pad_maximum_fusion.1.refs_2_), channel_id=1, source_target_pairs={{0,2},{2,4},{4,6},{6,32},{32,34},{34,36},{36,38},{38,0},{1,3},{3,5... | collective-permute-start | bytes 884744 | tf_op jit(solution)/shard_map/ppermute | solution.py:29
  58.3 2.0 %copy-start.5 = (bf16[4,48,768]{2,1,0:T(8,128)(2,1)}, bf16[4,48,768]{2,1,0:T(8,128)(2,1)S(1)}, u32[]{:S(2)}) copy-start(bf16[4,48,768]{2,1,0:T(8,128)(2,1)S(1)} %collective-permute-done.10.refs_4_) | copy-start | bytes 884740
  58.3 7.7 %collective-permute-start.12 = (bf16[4,48,768]{2,1,0:T(8,128)(2,1)S(1)}, bf16[4,48,768]{2,1,0:T(8,128)(2,1)S(1)}, u32[]{:S(2)}, u32[]{:S(2)}) collective-permute-start(bf16[4,48,768]{2,1,0:T(8,128)(2,1)S(1)} %collective-permute-done.10.refs_4_), channel_id=1, source_target_pairs={{0,38},{2,0},{4,2},{6,4},{32,6},{34,32},{36,34},{38,36},{1,39},{3,... | collective-permute-start | bytes 884744 | tf_op jit(solution)/shard_map/ppermute | solution.py:29
  59.8 8.0 %copy-start.6 = (bf16[4,48,768]{2,1,0:T(8,128)(2,1)}, bf16[4,48,768]{2,1,0:T(8,128)(2,1)S(1)}, u32[]{:S(2)}) copy-start(bf16[4,48,768]{2,1,0:T(8,128)(2,1)S(1)} %collective-permute-done.9.refs_3_) | copy-start | bytes 884740
  59.8 8.0 %collective-permute-start.11 = (bf16[4,48,768]{2,1,0:T(8,128)(2,1)S(1)}, bf16[4,48,768]{2,1,0:T(8,128)(2,1)S(1)}, u32[]{:S(2)}, u32[]{:S(2)}) collective-permute-start(bf16[4,48,768]{2,1,0:T(8,128)(2,1)S(1)} %collective-permute-done.9.refs_3_), channel_id=1, source_target_pairs={{0,2},{2,4},{4,6},{6,32},{32,34},{34,36},{36,38},{38,0},{1,3},{3,5... | collective-permute-start | bytes 884744 | tf_op jit(solution)/shard_map/ppermute | solution.py:29
  66.0 2.1 %copy-start.7 = (bf16[4,48,768]{2,1,0:T(8,128)(2,1)}, bf16[4,48,768]{2,1,0:T(8,128)(2,1)S(1)}, u32[]{:S(2)}) copy-start(bf16[4,48,768]{2,1,0:T(8,128)(2,1)S(1)} %collective-permute-done.12.refs_6_) | copy-start | bytes 884740
  66.0 7.1 %collective-permute-start.14 = (bf16[4,48,768]{2,1,0:T(8,128)(2,1)S(1)}, bf16[4,48,768]{2,1,0:T(8,128)(2,1)S(1)}, u32[]{:S(2)}, u32[]{:S(2)}) collective-permute-start(bf16[4,48,768]{2,1,0:T(8,128)(2,1)S(1)} %collective-permute-done.12.refs_6_), channel_id=1, source_target_pairs={{0,38},{2,0},{4,2},{6,4},{32,6},{34,32},{36,34},{38,36},{1,39},{3,... | collective-permute-start | bytes 884744 | tf_op jit(solution)/shard_map/ppermute | solution.py:29
  67.8 8.0 %copy-start.8 = (bf16[4,48,768]{2,1,0:T(8,128)(2,1)}, bf16[4,48,768]{2,1,0:T(8,128)(2,1)S(1)}, u32[]{:S(2)}) copy-start(bf16[4,48,768]{2,1,0:T(8,128)(2,1)S(1)} %collective-permute-done.11.refs_5_) | copy-start | bytes 884740
  67.8 8.0 %collective-permute-start.13 = (bf16[4,48,768]{2,1,0:T(8,128)(2,1)S(1)}, bf16[4,48,768]{2,1,0:T(8,128)(2,1)S(1)}, u32[]{:S(2)}, u32[]{:S(2)}) collective-permute-start(bf16[4,48,768]{2,1,0:T(8,128)(2,1)S(1)} %collective-permute-done.11.refs_5_), channel_id=1, source_target_pairs={{0,2},{2,4},{4,6},{6,32},{32,34},{34,36},{36,38},{38,0},{1,3},{3,5... | collective-permute-start | bytes 884744 | tf_op jit(solution)/shard_map/ppermute | solution.py:29
  73.1 9.5 %copy-start.3 = (bf16[4,48,768]{2,1,0:T(8,128)(2,1)}, bf16[4,48,768]{2,1,0:T(8,128)(2,1)S(1)}, u32[]{:S(2)}) copy-start(bf16[4,48,768]{2,1,0:T(8,128)(2,1)S(1)} %collective-permute-done.14.refs_8_) | copy-start | bytes 884740
  73.1 5.4 %collective-permute-start.16 = (bf16[2,48,768]{2,1,0:T(8,128)(2,1)S(1)}, bf16[2,48,768]{2,1,0:T(8,128)(2,1)S(1)}, u32[]{:S(2)}, u32[]{:S(2)}) collective-permute-start(bf16[2,48,768]{2,1,0:T(8,128)(2,1)S(1)} %slice.104), channel_id=1, source_target_pairs={{0,38},{2,0},{4,2},{6,4},{32,6},{34,32},{36,34},{38,36},{1,39},{3,... | collective-permute-start | bytes 442376 | tf_op jit(solution)/shard_map/ppermute | solution.py:29
  75.8 6.8 %copy-start.4 = (bf16[4,48,768]{2,1,0:T(8,128)(2,1)}, bf16[4,48,768]{2,1,0:T(8,128)(2,1)S(1)}, u32[]{:S(2)}) copy-start(bf16[4,48,768]{2,1,0:T(8,128)(2,1)S(1)} %collective-permute-done.13.refs_7_) | copy-start | bytes 884740
  75.8 6.7 %collective-permute-start.15 = (bf16[2,48,768]{2,1,0:T(8,128)(2,1)S(1)}, bf16[2,48,768]{2,1,0:T(8,128)(2,1)}, u32[]{:S(2)}, u32[]{:S(2)}) collective-permute-start(bf16[2,48,768]{2,1,0:T(8,128)(2,1)S(1)} %slice.103), channel_id=1, source_target_pairs={{0,2},{2,4},{4,6},{6,32},{32,34},{34,36},{36,38},{38,0},{1,3},{3,5... | collective-permute-start | bytes 442376 | tf_op jit(solution)/shard_map/ppermute | solution.py:29
  78.5 4.1 %copy-start.9 = (bf16[2,48,768]{2,1,0:T(8,128)(2,1)}, bf16[2,48,768]{2,1,0:T(8,128)(2,1)S(1)}, u32[]{:S(2)}) copy-start(bf16[2,48,768]{2,1,0:T(8,128)(2,1)S(1)} %collective-permute-done.16.refs_10_) | copy-start | bytes 442372
  82.5 1.4 copy-start
  107.7 28.5 %all-to-all-start.2 = ((bf16[4,8,48,768]{3,2,1,0:T(8,128)(2,1)}), bf16[4,8,48,768]{3,2,1,0:T(8,128)(2,1)S(1)}, u32[]{:S(2)}, u32[]{:S(2)}) async-start(bf16[4,8,48,768]{3,2,1,0:T(8,128)(2,1)} %shard_map.96.refs_2_), calls=%async_computation.2 | async-start | bytes 4718592 | tf_op jit(solution)/shard_map/all_to_all | solution.py:269
  120.6 2.6 %collective-permute-start.17 = (bf16[256,1536]{1,0:T(8,128)(2,1)}, bf16[256,1536]{1,0:T(8,128)(2,1)S(1)}, u32[]{:S(2)}, u32[]{:S(2)}) collective-permute-start(bf16[256,1536]{1,0:T(8,128)(2,1)} %get-tuple-element.42), channel_id=1, source_target_pairs={{0,1},{1,0},{2,3},{3,2},{4,5},{5,4},{6,7},{7,6},{8,9},{9,8},{10,11... | collective-permute-start | bytes 2359304 | tf_op jit(solution)/shard_map/ppermute | solution.py:29
  120.7 3.6 %collective-permute-start.18 = (bf16[256,1536]{1,0:T(8,128)(2,1)}, bf16[256,1536]{1,0:T(8,128)(2,1)S(1)}, u32[]{:S(2)}, u32[]{:S(2)}) collective-permute-start(bf16[256,1536]{1,0:T(8,128)(2,1)} %get-tuple-element.43), channel_id=1, source_target_pairs={{0,1},{1,0},{2,3},{3,2},{4,5},{5,4},{6,7},{7,6},{8,9},{9,8},{10,11... | collective-permute-start | bytes 2359304 | tf_op jit(solution)/shard_map/ppermute | solution.py:29
  136.1 30.0 %all-to-all-start.1 = ((bf16[4,128,1536]{2,1,0:T(8,128)(2,1)}), bf16[4,128,1536]{2,1,0:T(8,128)(2,1)}, u32[]{:S(2)}, u32[]{:S(2)}) async-start(bf16[4,128,1536]{2,1,0:T(8,128)(2,1)} %bitcast.56), calls=%async_computation.1 | async-start | bytes 3145728 | tf_op jit(solution)/shard_map/all_to_all | solution.py:283
  142.9 7.6 %collective-permute-start.24 = (bf16[2,48,768]{2,1,0:T(8,128)(2,1)S(1)}, bf16[2,48,768]{2,1,0:T(8,128)(2,1)S(1)}, u32[]{:S(2)}, u32[]{:S(2)}) collective-permute-start(bf16[2,48,768]{2,1,0:T(8,128)(2,1)S(1)} %get-tuple-element.51), channel_id=1, source_target_pairs={{0,4},{2,6},{4,32},{6,34},{32,36},{34,38},{36,0},{38,2},{1,5},{3,7... | collective-permute-start | bytes 442376 | tf_op jit(solution)/shard_map/ppermute | solution.py:29
  143.0 8.1 %collective-permute-start.23 = (bf16[2,48,768]{2,1,0:T(8,128)(2,1)S(1)}, bf16[2,48,768]{2,1,0:T(8,128)(2,1)S(1)}, u32[]{:S(2)}, u32[]{:S(2)}) collective-permute-start(bf16[2,48,768]{2,1,0:T(8,128)(2,1)S(1)} %get-tuple-element.52), channel_id=1, source_target_pairs={{0,38},{2,0},{4,2},{6,4},{32,6},{34,32},{36,34},{38,36},{1,39},{3,... | collective-permute-start | bytes 442376 | tf_op jit(solution)/shard_map/ppermute | solution.py:29
  144.8 7.3 %collective-permute-start.22 = (bf16[2,48,768]{2,1,0:T(8,128)(2,1)S(1)}, bf16[2,48,768]{2,1,0:T(8,128)(2,1)S(1)}, u32[]{:S(2)}, u32[]{:S(2)}) collective-permute-start(bf16[2,48,768]{2,1,0:T(8,128)(2,1)S(1)} %get-tuple-element.53), channel_id=1, source_target_pairs={{0,2},{2,4},{4,6},{6,32},{32,34},{34,36},{36,38},{38,0},{1,3},{3,5... | collective-permute-start | bytes 442376 | tf_op jit(solution)/shard_map/ppermute | solution.py:29
  146.1 6.0 %collective-permute-start.21 = (bf16[48,768]{1,0:T(8,128)(2,1)S(1)}, bf16[48,768]{1,0:T(8,128)(2,1)S(1)}, u32[]{:S(2)}, u32[]{:S(2)}) collective-permute-start(bf16[48,768]{1,0:T(8,128)(2,1)S(1)} %get-tuple-element.54), channel_id=1, source_target_pairs={{0,16},{8,24},{16,0},{24,8},{1,17},{9,25},{17,1},{25,9},{2,18},{10... | collective-permute-start | bytes 221192 | tf_op jit(solution)/shard_map/ppermute | solution.py:29
  149.1 4.4 %collective-permute-start.20 = (bf16[48,768]{1,0:T(8,128)(2,1)S(1)}, bf16[48,768]{1,0:T(8,128)(2,1)S(1)}, u32[]{:S(2)}, u32[]{:S(2)}) collective-permute-start(bf16[48,768]{1,0:T(8,128)(2,1)S(1)} %get-tuple-element.55), channel_id=1, source_target_pairs={{0,24},{8,0},{16,8},{24,16},{1,25},{9,1},{17,9},{25,17},{2,26},{10... | collective-permute-start | bytes 221192 | tf_op jit(solution)/shard_map/ppermute | solution.py:29
  150.5 5.6 %collective-permute-start.19 = (bf16[48,768]{1,0:T(8,128)(2,1)S(1)}, bf16[48,768]{1,0:T(8,128)(2,1)S(1)}, u32[]{:S(2)}, u32[]{:S(2)}) collective-permute-start(bf16[48,768]{1,0:T(8,128)(2,1)S(1)} %get-tuple-element.56), channel_id=1, source_target_pairs={{0,8},{8,16},{16,24},{24,0},{1,9},{9,17},{17,25},{25,1},{2,10},{10... | collective-permute-start | bytes 221192 | tf_op jit(solution)/shard_map/ppermute | solution.py:29
  157.2 16.5 %collective-permute-start.26 = (bf16[2,48,768]{2,1,0:T(8,128)(2,1)S(1)}, bf16[2,48,768]{2,1,0:T(8,128)(2,1)S(1)}, u32[]{:S(2)}, u32[]{:S(2)}) collective-permute-start(bf16[2,48,768]{2,1,0:T(8,128)(2,1)S(1)} %pad_maximum_fusion.4), channel_id=1, source_target_pairs={{0,0},{2,64},{4,128},{6,192},{32,32},{34,96},{36,160},{38,224},{64... | collective-permute-start | bytes 442376 | tf_op jit(solution)/shard_map/ppermute | solution.py:39
  160.3 9.6 %collective-permute-start.25 = (bf16[48,768]{1,0:T(8,128)(2,1)S(1)}, bf16[48,768]{1,0:T(8,128)(2,1)S(1)}, u32[]{:S(2)}, u32[]{:S(2)}) collective-permute-start(bf16[48,768]{1,0:T(8,128)(2,1)S(1)} %get-tuple-element.58), channel_id=1, source_target_pairs={{0,32},{2,96},{4,160},{6,224},{32,0},{34,64},{36,128},{38,192},{64... | collective-permute-start | bytes 221192 | tf_op jit(solution)/shard_map/ppermute | solution.py:39
  169.9 0.6 copy-start.1
Sparse Core Ops, SparseCore 0:
  29.5 40.5 all-gather.2
  100.2 44.4 reduce-scatter.1
